TPU v7x, 256 devices: a whole 4x4x8 slice. The times are simulated.
256 devices in a mesh: resp: 64 (over z_hi, x, y, core), tp: 4 (over z_lo).
Axes of the slice: x: 4, y: 4, z: 8 (z_hi: 2, z_lo: 4; z = z_hi * 4 + z_lo), core: 2. Of those that a mesh axis runs over, the one named last changes fastest.
Arguments:
- queries: bfloat16 [40960, 8192], P('resp', 'tp'), may hold values from -8 to 8
- resp_keys: bfloat16 [40960, 1024], P('resp', 'tp'), may hold values from -4 to 4
- resp_values: bfloat16 [40960, 1024], P('resp', 'tp'), may hold values from -4 to 4
- out_grad: bfloat16 [40960, 8192], P('resp', 'tp'), may hold values from -24 to 24
- prompt_keys: bfloat16 [4096, 1024], P(('resp', 'tp')), may hold values from -4 to 4
- prompt_values: bfloat16 [4096, 1024], P(('resp', 'tp')), may hold values from -4 to 4
- lengths: int32 [256], P('resp'), may hold values from 1 to 160, 25600 in all
- prompt_of: int32 [256], P('resp'), may hold values from 0 to 15, as said below
Outputs:
- attn_out: bfloat16 [40960, 8192], P('resp', 'tp')
- query_grad: bfloat16 [40960, 8192], P('resp', 'tp')
- resp_key_grad: bfloat16 [40960, 1024], P('resp', 'tp')
- resp_value_grad: bfloat16 [40960, 1024], P('resp', 'tp')
- prompt_key_grad: bfloat16 [4096, 1024], P(('resp', 'tp'))
- prompt_value_grad: bfloat16 [4096, 1024], P(('resp', 'tp'))
Inputs may be any that keep to these rules, and one draw needn't show every extreme that they name: `prompt_of`: each prompt is named by exactly 16 responses.
All inputs are finite; a program needn't handle non-finite values. No bound on the sum of `lengths` on one device may be relied on, other than what follows from the above.
Results may differ from a plain program's by a relative error of at most 0.03.
Values may be sent and summed in bfloat16 or wider, within the bound.
No kernel may reach another device: no remote copies, remote signals or barrier semaphores. Data moves between devices by JAX's collectives and lax.ppermute only.
A program may use at most 128 MiB of HBM per device.

v0:
```python
import jax
import jax.numpy as jnp
from jax import lax
from jax.sharding import PartitionSpec as P

HD = 128
LP = 256


def attend_head(query_part, key_part, value_part, grad_part, allowed, valid_rows, score_scale):
    query_count = query_part.shape[0]
    head_dim = key_part.shape[1]
    per_group = query_part.shape[1] // head_dim
    query_three = query_part.reshape(query_count, per_group, head_dim)
    grad_three = grad_part.reshape(query_count, per_group, head_dim)
    scores = (
        jnp.einsum("qgd,kd->gqk", query_three, key_part, preferred_element_type=jnp.float32)
        * score_scale
    )
    scores = jnp.where(allowed, scores, -1e30)
    largest = jnp.max(scores, axis=-1, keepdims=True)
    weights = jnp.where(allowed, jnp.exp(scores - largest), 0.0)
    probability = weights / jnp.sum(weights, axis=-1, keepdims=True) * valid_rows
    probability_low = probability.astype(jnp.bfloat16)
    output = jnp.einsum(
        "gqk,kd->qgd", probability_low, value_part, preferred_element_type=jnp.float32
    ).astype(jnp.bfloat16)
    delta_rows = jnp.sum(grad_three.astype(jnp.float32) * output.astype(jnp.float32), axis=-1)
    prob_grad = jnp.einsum(
        "qgd,kd->gqk", grad_three, value_part, preferred_element_type=jnp.float32
    )
    score_grad = (probability * (prob_grad - jnp.transpose(delta_rows)[:, :, None])).astype(
        jnp.bfloat16
    )
    query_grad = (
        jnp.einsum("gqk,kd->qgd", score_grad, key_part, preferred_element_type=jnp.float32)
        * score_scale
    ).astype(jnp.bfloat16)
    key_terms = (
        jnp.einsum("gqk,qgd->kd", score_grad, query_three, preferred_element_type=jnp.float32)
        * score_scale
    )
    value_terms = jnp.einsum(
        "gqk,qgd->kd", probability_low, grad_three, preferred_element_type=jnp.float32
    )
    return (
        output.reshape(query_count, -1),
        query_grad.reshape(query_count, -1),
        key_terms,
        value_terms,
    )


def respond(
    query_rows, key_rows, value_rows, grad_rows, prompt_key_rows, prompt_value_rows, length
):
    query_count = query_rows.shape[0]
    prompt_count = prompt_key_rows.shape[0]
    kv_heads = key_rows.shape[1] // HD
    query_width = query_rows.shape[1] // kv_heads
    score_scale = HD ** (-0.5)
    positions = jnp.arange(query_count)
    offsets = jnp.arange(prompt_count + query_count) - prompt_count
    valid_mask = positions < length
    allowed = (offsets[None, :] < 0) | (offsets[None, :] <= positions[:, None]) & (
        offsets[None, :] < length
    )
    valid_rows = valid_mask.astype(jnp.float32)[None, :, None]
    masked_grad = jnp.where(valid_mask[:, None], grad_rows, jnp.zeros_like(grad_rows))
    all_keys = jnp.concatenate([prompt_key_rows, key_rows], 0)
    all_values = jnp.concatenate([prompt_value_rows, value_rows], 0)
    collected = []
    for head_index in range(kv_heads):
        collected.append(
            attend_head(
                query_rows[:, head_index * query_width : (head_index + 1) * query_width],
                all_keys[:, head_index * HD : (head_index + 1) * HD],
                all_values[:, head_index * HD : (head_index + 1) * HD],
                masked_grad[:, head_index * query_width : (head_index + 1) * query_width],
                allowed,
                valid_rows,
                score_scale,
            )
        )
    output = jnp.concatenate([member[0] for member in collected], 1)
    query_grad = jnp.concatenate([member[1] for member in collected], 1)
    key_terms = jnp.concatenate([member[2] for member in collected], 1)
    value_terms = jnp.concatenate([member[3] for member in collected], 1)
    return (
        output,
        query_grad,
        key_terms[:prompt_count],
        value_terms[:prompt_count],
        key_terms[prompt_count:].astype(jnp.bfloat16),
        value_terms[prompt_count:].astype(jnp.bfloat16),
    )


def shards(
    queries, resp_keys, resp_values, out_grad, prompt_keys, prompt_values, lengths, prompt_of
):
    lane_count = lax.axis_size("tp")
    resp_count = lax.axis_size("resp")
    shard_rows = prompt_keys.shape[0]
    lane_width = resp_keys.shape[1]
    wide_keys, wide_values = (
        lax.all_gather(prompt_keys, "resp", axis=0, tiled=True),
        lax.all_gather(prompt_values, "resp", axis=0, tiled=True),
    )
    split_keys, split_values = (
        lax.all_to_all(wide_keys, "tp", split_axis=1, concat_axis=0, tiled=True),
        lax.all_to_all(wide_values, "tp", split_axis=1, concat_axis=0, tiled=True),
    )
    cache_keys = (
        split_keys.reshape(lane_count, resp_count, shard_rows, lane_width)
        .transpose(1, 0, 2, 3)
        .reshape(-1, lane_width)
    )
    cache_values = (
        split_values.reshape(lane_count, resp_count, shard_rows, lane_width)
        .transpose(1, 0, 2, 3)
        .reshape(-1, lane_width)
    )
    local_count = lengths.shape[0]
    span_rows = queries.shape[0] // local_count
    blank_sums = jnp.zeros((cache_keys.shape[0], lane_width), jnp.float32)

    def visit(totals, number):
        key_sums, value_sums = totals
        first_row = number * span_rows
        owner_row = prompt_of[number] * LP
        results = respond(
            lax.dynamic_slice_in_dim(queries, first_row, span_rows, 0),
            lax.dynamic_slice_in_dim(resp_keys, first_row, span_rows, 0),
            lax.dynamic_slice_in_dim(resp_values, first_row, span_rows, 0),
            lax.dynamic_slice_in_dim(out_grad, first_row, span_rows, 0),
            lax.dynamic_slice_in_dim(cache_keys, owner_row, LP, 0),
            lax.dynamic_slice_in_dim(cache_values, owner_row, LP, 0),
            lengths[number],
        )
        key_sums = lax.dynamic_update_slice_in_dim(
            key_sums,
            lax.dynamic_slice_in_dim(key_sums, owner_row, LP, 0) + results[2],
            owner_row,
            0,
        )
        value_sums = lax.dynamic_update_slice_in_dim(
            value_sums,
            lax.dynamic_slice_in_dim(value_sums, owner_row, LP, 0) + results[3],
            owner_row,
            0,
        )
        return ((key_sums, value_sums), (results[0], results[1], results[4], results[5]))

    (key_sums, value_sums), pieces = lax.scan(
        visit, (blank_sums, blank_sums), jnp.arange(local_count, dtype=jnp.int32)
    )
    attn_out = pieces[0].reshape(-1, queries.shape[1])
    query_grad = pieces[1].reshape(-1, queries.shape[1])
    resp_key_grad = pieces[2].reshape(-1, lane_width)
    resp_value_grad = pieces[3].reshape(-1, lane_width)
    order_keys = (
        key_sums.reshape(resp_count, lane_count, shard_rows, lane_width)
        .transpose(1, 0, 2, 3)
        .reshape(-1, lane_width)
    )
    order_values = (
        value_sums.reshape(resp_count, lane_count, shard_rows, lane_width)
        .transpose(1, 0, 2, 3)
        .reshape(-1, lane_width)
    )
    mixed_keys, mixed_values = (
        lax.all_to_all(order_keys, "tp", split_axis=0, concat_axis=1, tiled=True),
        lax.all_to_all(order_values, "tp", split_axis=0, concat_axis=1, tiled=True),
    )
    summed_keys, summed_values = (
        lax.psum_scatter(mixed_keys, "resp", scatter_dimension=0, tiled=True),
        lax.psum_scatter(mixed_values, "resp", scatter_dimension=0, tiled=True),
    )
    prompt_key_grad = summed_keys.astype(jnp.bfloat16)
    prompt_value_grad = summed_values.astype(jnp.bfloat16)
    return (
        attn_out,
        query_grad,
        resp_key_grad,
        resp_value_grad,
        prompt_key_grad,
        prompt_value_grad,
    )


def solution(mesh):
    return jax.shard_map(
        shards,
        mesh=mesh,
        in_specs=(
            P("resp", "tp"),
            P("resp", "tp"),
            P("resp", "tp"),
            P("resp", "tp"),
            P(("resp", "tp"), None),
            P(("resp", "tp"), None),
            P("resp"),
            P("resp"),
        ),
        out_specs=(
            P("resp", "tp"),
            P("resp", "tp"),
            P("resp", "tp"),
            P("resp", "tp"),
            P(("resp", "tp"), None),
            P(("resp", "tp"), None),
        ),
        check_vma=False,
    )
```

profile of v0, /device:TPU:1, one launch (start us, length us, event | category | flops | bytes accessed | tf_op | source)
XLA Modules:
  0.0 1335.6 jit_solution(992465903243036048)
XLA Ops:
  8.6 90.0 %all-gather.5.cloned.1.call-done = bf16[1024,1024]{1,0:T(8,128)(2,1)} async-done(((bf16[16,1024]{1,0:T(8,128)(2,1)}), bf16[1024,1024]{1,0:T(8,128)(2,1)}) %all-gather.5.cloned.1.call-update) | async-done | bytes 2097168 | tf_op jit(solution)/shard_map/all_gather | solution.py:108
  98.6 3.9 copy.119
  102.6 3.6 all-to-all-start.1
  106.2 86.8 %all-gather.3.cloned.1.call-done = bf16[1024,1024]{1,0:T(8,128)(2,1)} async-done(((bf16[16,1024]{1,0:T(8,128)(2,1)}), bf16[1024,1024]{1,0:T(8,128)(2,1)}) %all-gather.3.cloned.1.call-update) | async-done | bytes 2097168 | tf_op jit(solution)/shard_map/all_gather | solution.py:107
  193.0 3.9 copy.116
  196.9 4.5 all-to-all-start
  204.1 3.3 copy.121
  207.3 42.3 %all-to-all-done = bf16[1024,4,256]{0,2,1:T(8,128)(2,1)} async-done(((bf16[1024,4,256]{0,2,1:T(8,128)(2,1)}), bf16[1024,4,256]{0,2,1:T(8,128)(2,1)}, u32[]{:S(2)}, u32[]{:S(2)}) %all-to-all-start) | async-done | bytes 2097184 | tf_op jit(solution)/shard_map/all_to_all | solution.py:111
  249.6 2.8 copy.117
  258.5 132.8 %while.22 = (s32[]{:T(128)}, f32[4096,256]{1,0:T(8,128)}, f32[4096,256]{1,0:T(8,128)}, bf16[4,160,2048]{2,1,0:T(8,128)(2,1)}, bf16[4,160,2048]{2,1,0:T(8,128)(2,...) while((s32[]{:T(128)}, f32[4096,256]{1,0:T(8,128)}, ...), condition=%wide.region_7.8_spmd, body=%wide.region_0.7_spmd.sunk | while | flops 1660661632 | bytes 60923956 | solution.py:155
  271.7 2.9 fusion.177
  274.6 2.7 convolution_bitcast_fusion.6
  279.8 2.9 fusion.179
  282.7 2.7 convolution_bitcast_fusion.7
  304.9 2.9 fusion.177
  307.7 2.7 convolution_bitcast_fusion.6
  313.0 2.9 fusion.179
  338.1 2.9 fusion.177
  346.2 2.9 fusion.179
  371.3 2.9 fusion.177
  374.1 2.7 convolution_bitcast_fusion.6
  379.4 2.9 fusion.179
  391.3 2.8 copy.122
  394.1 95.6 %all_to_all.70 = f32[4,1024,256]{2,1,0:T(8,128)} all-to-all(f32[4,1024,256]{2,1,0:T(8,128)S(1)} %bitcast.297), channel_id=1, replica_groups=mesh['resp'=64,'tp'=4] {'tp'}, dimensions={0} | all-to-all | bytes 8388608 | tf_op jit(solution)/shard_map/all_to_all | solution.py:173
  489.7 5.4 copy.123
  495.1 5.4 copy.128
  500.5 2.8 copy.124
  503.3 106.1 %all_to_all.71 = f32[4,1024,256]{2,1,0:T(8,128)} all-to-all(f32[4,1024,256]{2,1,0:T(8,128)S(1)} %bitcast.299), channel_id=1, replica_groups=mesh['resp'=64,'tp'=4] {'tp'}, dimensions={0} | all-to-all | bytes 8388608 | tf_op jit(solution)/shard_map/all_to_all | solution.py:174
  609.5 5.4 copy.125
  614.9 5.4 copy.130
  620.3 289.3 %reduce-scatter.7.cloned.1.call-done = f32[16,1024]{1,0:T(8,128)} async-done(((f32[1024,1024]{1,0:T(8,128)}), f32[16,1024]{1,0:T(8,128)}) %reduce-scatter.7.cloned.1.call-update) | async-done | bytes 65552
  911.3 416.0 %reduce-scatter.9.cloned.1.call-done = f32[16,1024]{1,0:T(8,128)} async-done(((f32[1024,1024]{1,0:T(8,128)}), f32[16,1024]{1,0:T(8,128)}) %reduce-scatter.9.cloned.1.call-update) | async-done | bytes 65552
  (170 shorter events, 99.1 us)
Async XLA Ops:
  7.2 91.5 %all-gather.5.cloned.1.call-start = ((), (), s32[]{:S(2)}) async-start(), calls=%async_computation.7 | async-start | bytes 2129920 | tf_op jit(solution)/shard_map/all_gather | solution.py:108
  7.9 185.1 %all-gather.3.cloned.1.call-start = ((), (), s32[]{:S(2)}) async-start(), calls=%async_computation.6 | async-start | bytes 2129920 | tf_op jit(solution)/shard_map/all_gather | solution.py:107
  102.6 94.4 %all-to-all-start.1 = ((bf16[1024,4,256]{0,2,1:T(8,128)(2,1)}), bf16[1024,4,256]{0,2,1:T(8,128)(2,1)S(1)}, u32[]{:S(2)}, u32[]{:S(2)}) async-start(bf16[1024,4,256]{0,2,1:T(8,128)(2,1)} %bitcast.303), calls=%async_computation.1 | async-start | bytes 4194304 | tf_op jit(solution)/shard_map/all_to_all | solution.py:112
  196.9 52.6 %all-to-all-start = ((bf16[1024,4,256]{0,2,1:T(8,128)(2,1)}), bf16[1024,4,256]{0,2,1:T(8,128)(2,1)}, u32[]{:S(2)}, u32[]{:S(2)}) async-start(bf16[1024,4,256]{0,2,1:T(8,128)(2,1)} %bitcast.302), calls=%async_computation | async-start | bytes 4194304 | tf_op jit(solution)/shard_map/all_to_all | solution.py:111
  201.4 708.2 %reduce-scatter.7.cloned.1.call-start = ((), (), s32[]{:S(2)}) async-start(), calls=%async_computation.8 | async-start | bytes 4259840
  256.3 2.2 copy-start
  256.3 2.2 copy-start.1
  274.6 2.7 copy-start.3
  282.7 2.7 copy-start.2
  307.7 2.7 copy-start.3
  315.9 2.7 copy-start.2
  340.9 2.7 copy-start.3
  349.1 2.7 copy-start.2
  374.1 2.7 copy-start.3
  382.3 2.7 copy-start.2
  500.5 826.8 %reduce-scatter.9.cloned.1.call-start = ((), (), s32[]{:S(2)}) async-start(), calls=%async_computation.9 | async-start | bytes 4259840
Sparse Core Ops, SparseCore 0:
  11.6 87.0 all-gather.4
  102.2 90.7 all-gather.2
  500.6 408.9 reduce-scatter.6
  912.1 415.1 reduce-scatter.8
where the time goes:
time: 1350 us; the launch traced here: 1340 us
  waiting for transfers between devices  926 us (69%)
  blocking collectives  202 us (15%)
  local copies, waits for them, and re-layouts  80.3 us (6%)
  matrix products  63.9 us (5%)
  other arithmetic  28.1 us (2%)
  between operations  13.9 us (1%)
  loops' own time  13.7 us (1%)
    unnamed x6, waiting for transfers between devices  707 us
    all_to_all x1, blocking collectives, shards(): lax.all_to_all(order_values, 'tp', split_axis=0, concat_axis=1, tiled=True)  106 us
    all_to_all x1, blocking collectives, shards(): lax.all_to_all(order_keys, 'tp', split_axis=0, concat_axis=1, tiled=True)  95.6 us
    all_gather x1, waiting for transfers between devices, shards(): lax.all_gather(prompt_values, 'resp', axis=0, tiled=True)  90 us
    all_gather x1, waiting for transfers between devices, shards(): lax.all_gather(prompt_keys, 'resp', axis=0, tiled=True)  86.8 us
    all_to_all x1, waiting for transfers between devices, shards(): lax.all_to_all(wide_keys, 'tp', split_axis=1, concat_axis=0, tiled=True)  42.3 us
  transfers between devices with their start and end apart: 6, of which 5 were waited for; matrix products, arithmetic and copies ran while one was open for 2% of the time, Pallas kernels for 0%

commit v1 on v0

v1 whole, which is shorter than its diff:
```python
import functools

import jax
import jax.numpy as jnp
from jax import lax
from jax.experimental import pallas as pl
from jax.experimental.pallas import tpu as pltpu
from jax.sharding import PartitionSpec as P

HD = 128
LP = 256
ROWS = 32
PER_GROUP = 8
KV_LANE = 2
LANES = 4
GROUPS = 4
TILE = 16
MEMBERS = 16
PROMPTS = 16
LOCAL = 4
SLICE = LP // GROUPS
HALF = LOCAL // 2
SENT = TILE + 8
LOG2E = 1.4426950408889634
SMALL = pltpu.CompilerParams(vmem_limit_bytes=16 * 1024 * 1024)

STORE_GROUPS = [
    [(p * 4 + (turn + t) % 4) * 4 + t for p in range(PROMPTS) for t in range(LANES)]
    for turn in range(4)
]
PICK_GROUPS = [
    [z * 32 + x * 8 + high * 4 + block for x in range(4) for block in range(4)]
    for z in range(2)
    for high in range(2)
]


def over_store(array):
    return lax.all_to_all(
        array,
        ("resp", "tp"),
        split_axis=0,
        concat_axis=0,
        tiled=True,
        axis_index_groups=STORE_GROUPS,
    )


def over_pick(array):
    return lax.all_to_all(
        array, "resp", split_axis=0, concat_axis=0, tiled=True, axis_index_groups=PICK_GROUPS
    )


def column_of(x):
    return (x // KV_LANE, x % KV_LANE)


def stored_kernel(owner_ref, key_ref, value_ref, out_ref):
    at = lax.broadcasted_iota(jnp.int32, (SENT - TILE, HD), 1)
    asked = jnp.zeros((SENT - TILE, HD), jnp.int32)
    for one in range(LOCAL):
        asked = jnp.where(at == one, owner_ref[one], asked)
    asked = asked.astype(jnp.float32).astype(jnp.bfloat16)
    for prompt in range(PROMPTS):
        which, head = column_of(prompt // 2 % 4)
        source = value_ref if which else key_ref
        for lane in range(LANES):
            first = (lane * KV_LANE + head) * HD
            out_ref[prompt * LANES + lane, :TILE] = source[:, first : first + HD]
            out_ref[prompt * LANES + lane, TILE:] = asked


def pick_kernel(pieces_ref, first_ref, second_ref, owner_ref, owners, sem):
    resp = lax.axis_index("resp")
    prompt = resp // 4
    turn = (resp % 4 + LANES - lax.axis_index("tp")) % 4
    for x in range(4):
        for block in range(4):
            source = (prompt // 8 * 8 + x * 2 + prompt % 2) * LANES + (block + 4 - turn) % 4
            tile = pieces_ref[source, TILE:].astype(jnp.float32)
            owner_ref[x * 4 + block : x * 4 + block + 1] = tile[:1].astype(jnp.int32)
    copy = pltpu.make_async_copy(owner_ref, owners, sem)
    copy.start()
    copy.wait()
    for member in range(MEMBERS):
        for one in range(LOCAL):
            owner = owners[member, one]
            out_ref = first_ref if one < HALF else second_ref
            for lane in range(LANES):
                out_ref[member, one % HALF, lane * TILE : (lane + 1) * TILE] = pieces_ref[
                    owner * LANES + lane, :TILE
                ]


def fold_kernel(owner_ref, first_ref, second_ref, out_ref, total):
    total[...] = jnp.zeros_like(total)
    for one in range(LOCAL):
        terms_ref = first_ref if one < HALF else second_ref
        for member in range(MEMBERS):
            owner = owner_ref[member, one]
            total[owner] += terms_ref[member, one % HALF].astype(jnp.float32)
    for prompt in range(PROMPTS):
        for lane in range(LANES):
            out_ref[prompt * LANES + lane] = total[
                prompt, lane * TILE : (lane + 1) * TILE
            ].astype(out_ref.dtype)


def summed_kernel(sums_ref, key_ref, value_ref):
    for x in range(4):
        which, head = column_of(x)
        target = value_ref if which else key_ref
        for lane in range(LANES):
            tile = jnp.zeros((TILE, HD), jnp.float32)
            for z in range(2):
                for high in range(2):
                    source = (z * 8 + x * 2 + high) * LANES + lane
                    tile = tile + sums_ref[source].astype(jnp.float32)
            first = (lane * KV_LANE + head) * HD
            target[:, first : first + HD] = tile.astype(target.dtype)


def attend_kernel(
    first_response, length_ref, query_ref, grad_ref, key_ref, value_ref, prompt_ref, *rest
):
    rest = rest[-17:]
    out_ref, query_grad_ref, key_grad_ref, value_grad_ref, prompt_grad_ref = rest[:5]
    keys, values, keys_t, values_t, stacked_query, stacked_grad = rest[5:11]
    scores, prob_grads, probability_low, score_grad, key_total, value_total = rest[11:]
    length = length_ref[first_response + pl.program_id(0)]
    span = query_ref.shape[0]
    scale = HD**-0.5
    wide = PER_GROUP * ROWS
    key_total[...] = jnp.zeros_like(key_total)
    value_total[...] = jnp.zeros_like(value_total)
    for head in range(KV_LANE):
        for whole, whole_t, own_ref, which in (
            (keys, keys_t, key_ref, 0),
            (values, values_t, value_ref, 1),
        ):
            whole[head, :LP] = prompt_ref[which, head, :, 0].reshape(LP, HD)
            whole[head, LP:] = own_ref[:, head * HD : (head + 1) * HD]
            whole_t[head] = whole[head].T

    def heads(slot, head):
        for at in range(PER_GROUP):
            column = (head * PER_GROUP + at) * HD
            yield slice(at * ROWS, (at + 1) * ROWS), slice(column, column + HD)

    def score(slot, head, first):
        count = LP + first + ROWS
        lane = lax.broadcasted_iota(jnp.int32, (1, wide), 1) % ROWS
        causal = lax.broadcasted_iota(jnp.int32, (ROWS, 1), 0) <= lane
        for part, column in heads(slot, head):
            stacked_query[slot, part] = query_ref[first : first + ROWS, column]
            stacked_grad[slot, part] = grad_ref[first : first + ROWS, column]
        raw = lax.dot_general(
            keys[head, :count],
            stacked_query[slot],
            (((1,), (1,)), ((), ())),
            preferred_element_type=jnp.float32,
        )
        tail = jnp.where(causal, raw[count - ROWS :], -1e30)
        scores[slot, : count - ROWS] = raw[: count - ROWS]
        scores[slot, count - ROWS : count] = tail
        top = jnp.max(raw[: count - ROWS].reshape(-1, 8, wide), axis=0)
        top = jnp.maximum(top, jnp.max(tail.reshape(-1, 8, wide), axis=0))
        prob_grads[slot, :count] = lax.dot_general(
            values[head, :count],
            stacked_grad[slot],
            (((1,), (1,)), ((), ())),
            preferred_element_type=jnp.float32,
        )
        return jnp.max(top, axis=0, keepdims=True) * (scale * LOG2E)

    def soften(slot, head, first, largest):
        count = LP + first + ROWS
        lane = lax.broadcasted_iota(jnp.int32, (1, wide), 1) % ROWS
        live = first + lane < length
        blocks = [slice(at, at + ROWS) for at in range(0, count, ROWS)]
        total = jnp.zeros((8, wide), jnp.float32)
        for block in blocks:
            weights = jnp.exp2(scores[slot, block] * (scale * LOG2E) - largest)
            scores[slot, block] = weights
            total = total + jnp.sum(weights.reshape(-1, 8, wide), axis=0)
        inverse = jnp.where(live, 1.0 / jnp.sum(total, axis=0, keepdims=True), 0.0)
        total = jnp.zeros((8, wide), jnp.float32)
        for block in blocks:
            probability = scores[slot, block] * inverse
            probability_low[slot, block] = probability.astype(jnp.bfloat16)
            terms = probability * prob_grads[slot, block]
            total = total + jnp.sum(terms.reshape(-1, 8, wide), axis=0)
        delta = jnp.sum(total, axis=0, keepdims=True)
        for block in blocks:
            probability = scores[slot, block] * inverse
            score_grad[slot, block] = (probability * (prob_grads[slot, block] - delta)).astype(
                jnp.bfloat16
            )

    def spread(slot, head, first):
        count = LP + first + ROWS
        rows = slice(first, first + ROWS)
        output = (
            jnp.dot(
                values_t[head, :, :count],
                probability_low[slot, :count],
                preferred_element_type=jnp.float32,
            )
            .astype(jnp.bfloat16)
            .T
        )
        query_grad = (
            (
                jnp.dot(
                    keys_t[head, :, :count],
                    score_grad[slot, :count],
                    preferred_element_type=jnp.float32,
                )
                * scale
            )
            .astype(jnp.bfloat16)
            .T
        )
        for part, column in heads(slot, head):
            out_ref[rows, column] = output[part]
            query_grad_ref[rows, column] = query_grad[part]
        value_total[head, :count] += jnp.dot(
            probability_low[slot, :count], stacked_grad[slot], preferred_element_type=jnp.float32
        )
        key_total[head, :count] += jnp.dot(
            score_grad[slot, :count], stacked_query[slot], preferred_element_type=jnp.float32
        )

    def work(firsts):
        streams = [(head, first) for first in firsts for head in range(KV_LANE)]
        largest = {0: score(0, *streams[0])}
        for slot, stream in enumerate(streams):
            if slot + 1 < len(streams):
                largest[slot + 1] = score(slot + 1, *streams[slot + 1])
            soften(slot, *stream, largest[slot])
            spread(slot, *stream)

    def blank(first, last):
        zeros = jnp.zeros((last - first, query_ref.shape[1]), jnp.bfloat16)
        out_ref[first:last, :] = zeros
        query_grad_ref[first:last, :] = zeros

    for first in range(0, span, 2 * ROWS):
        second = first + ROWS
        last = min(second + ROWS, span)
        if second < span:

            @pl.when(length > second)
            def _():
                work((first, second))

        @pl.when((length > first) & ((length <= second) | (second >= span)))
        def _():
            work((first,))
            if second < span:
                blank(second, last)

        @pl.when(length <= first)
        def _():
            blank(first, last)

    for head in range(KV_LANE):
        lanes = slice(head * HD, (head + 1) * HD)
        key_terms = (key_total[head] * scale).astype(jnp.bfloat16)
        value_terms = value_total[head].astype(jnp.bfloat16)
        prompt_grad_ref[0, head, :, 0] = key_terms[:LP].reshape(GROUPS, SLICE, HD)
        prompt_grad_ref[1, head, :, 0] = value_terms[:LP].reshape(GROUPS, SLICE, HD)
        key_grad_ref[:, lanes] = key_terms[LP:]
        value_grad_ref[:, lanes] = value_terms[LP:]


def attend(
    lengths, queries, out_grad, resp_keys, resp_values, prompt_rows, first=0, earlier=()
):
    count = prompt_rows.shape[3]
    span = queries.shape[0] // lengths.shape[0]
    wide = pl.BlockSpec((span, queries.shape[1]), lambda i, length: (first + i, 0))
    narrow = pl.BlockSpec((span, resp_keys.shape[1]), lambda i, length: (first + i, 0))
    prompt = pl.BlockSpec(
        (2, KV_LANE, GROUPS, 1, SLICE, HD), lambda i, length: (0, 0, 0, i, 0, 0)
    )
    both = LP + span
    streams = 2 * KV_LANE
    stacked = PER_GROUP * ROWS
    return pl.pallas_call(
        functools.partial(attend_kernel, first),
        out_shape=(
            jax.ShapeDtypeStruct(queries.shape, jnp.bfloat16),
            jax.ShapeDtypeStruct(queries.shape, jnp.bfloat16),
            jax.ShapeDtypeStruct(resp_keys.shape, jnp.bfloat16),
            jax.ShapeDtypeStruct(resp_keys.shape, jnp.bfloat16),
            jax.ShapeDtypeStruct(prompt_rows.shape, jnp.bfloat16),
        ),
        grid_spec=pltpu.PrefetchScalarGridSpec(
            num_scalar_prefetch=1,
            grid=(count,),
            in_specs=[wide, wide, narrow, narrow, prompt]
            + [pl.BlockSpec(memory_space=pl.ANY)] * len(earlier),
            out_specs=[wide, wide, narrow, narrow, prompt],
            scratch_shapes=[
                pltpu.VMEM((KV_LANE, both, HD), jnp.bfloat16),
                pltpu.VMEM((KV_LANE, both, HD), jnp.bfloat16),
                pltpu.VMEM((KV_LANE, HD, both), jnp.bfloat16),
                pltpu.VMEM((KV_LANE, HD, both), jnp.bfloat16),
                pltpu.VMEM((streams, stacked, HD), jnp.bfloat16),
                pltpu.VMEM((streams, stacked, HD), jnp.bfloat16),
                pltpu.VMEM((streams, both, stacked), jnp.float32),
                pltpu.VMEM((streams, both, stacked), jnp.float32),
                pltpu.VMEM((streams, both, stacked), jnp.bfloat16),
                pltpu.VMEM((streams, both, stacked), jnp.bfloat16),
                pltpu.VMEM((KV_LANE, both, HD), jnp.float32),
                pltpu.VMEM((KV_LANE, both, HD), jnp.float32),
            ],
        ),
        input_output_aliases={6 + at: at for at in range(len(earlier))},
        compiler_params=pltpu.CompilerParams(vmem_limit_bytes=32 * 1024 * 1024),
        cost_estimate=pl.CostEstimate(
            flops=24 * count * span * queries.shape[1] * both,
            bytes_accessed=8 * count * span * queries.shape[1],
            transcendentals=count * span * queries.shape[1] * both // HD,
        ),
    )(lengths, queries, out_grad, resp_keys, resp_values, prompt_rows, *earlier)


def in_vmem(kernel, out_shape, *operands, scalars=0, **more):
    spaces = [pltpu.SMEM] * scalars + [pltpu.VMEM] * (len(operands) - scalars)
    return pl.pallas_call(
        kernel,
        out_shape=out_shape,
        in_specs=[pl.BlockSpec(memory_space=space) for space in spaces],
        compiler_params=SMALL,
        **more,
    )(*operands)


def low(*shape):
    return jax.ShapeDtypeStruct(shape, jnp.bfloat16)


def shards(
    queries, resp_keys, resp_values, out_grad, prompt_keys, prompt_values, lengths, prompt_of
):
    pieces = over_store(
        in_vmem(
            stored_kernel,
            low(PROMPTS * LANES, SENT, HD),
            prompt_of,
            prompt_keys,
            prompt_values,
            scalars=1,
        )
    )
    *picked, owners = in_vmem(
        pick_kernel,
        (low(MEMBERS, HALF, SLICE, HD),) * 2
        + (jax.ShapeDtypeStruct((MEMBERS, HD), jnp.int32),),
        pieces,
        scratch_shapes=[pltpu.SMEM((MEMBERS, HD), jnp.int32), pltpu.SemaphoreType.DMA],
    )
    picked = [over_pick(part) for part in picked]
    results, terms = (), []
    for half in range(2):
        *results, part = attend(
            lengths,
            queries,
            out_grad,
            resp_keys,
            resp_values,
            picked[half].reshape(2, KV_LANE, GROUPS, HALF, SLICE, HD),
            half * HALF,
            results,
        )
        terms.append(over_pick(part.reshape(MEMBERS, HALF, SLICE, HD)))
    sums = in_vmem(
        fold_kernel,
        low(PROMPTS * LANES, TILE, HD),
        owners,
        *terms,
        scalars=1,
        scratch_shapes=[pltpu.VMEM((PROMPTS, SLICE, HD), jnp.float32)],
    )
    prompt_key_grad, prompt_value_grad = in_vmem(
        summed_kernel,
        (low(*prompt_keys.shape), low(*prompt_values.shape)),
        over_store(sums),
    )
    return (*results, prompt_key_grad, prompt_value_grad)


def solution(mesh):
    wide = P("resp", "tp")
    stored = P(("resp", "tp"), None)
    return jax.shard_map(
        shards,
        mesh=mesh,
        in_specs=(wide, wide, wide, wide, stored, stored, P("resp"), P("resp")),
        out_specs=(wide, wide, wide, wide, stored, stored),
        check_vma=False,
    )
```

time: 1350 us -> 137 us (0.10)
  waiting for transfers between devices: 926 us -> 0.01 us
  blocking collectives: 202 us -> 102 us
  local copies, waits for them, and re-layouts: 80.3 us -> 9.13 us
  matrix products: 63.9 us -> 0 us
  other arithmetic: 28.1 us -> 0 us
  Pallas kernels: 0 us -> 19.4 us
  loops' own time: 13.7 us -> 0 us
    unnamed x6 -> x0, waiting for transfers between devices: 707 us -> none
    all_gather x2 -> x0, waiting for transfers between devices: 177 us -> none  [the longest x1 90 us: shards(): lax.all_gather(prompt_values, 'resp', axis=0, tiled=True)]
    all_to_all x2 -> x5, blocking collectives: 202 us -> 102 us  [the longest x2 51.8 us: over_store(): lax.all_to_all(array, ('resp', 'tp'), split_axis=0, concat_axis=0, tiled=...]
    all_to_all x2 -> x1, waiting for transfers between devices: 42.3 us -> 0.01 us  [over_pick(): lax.all_to_all(array, 'resp', split_axis=0, concat_axis=0, tiled=True, ax...]
    dot_general x40 -> x0, matrix products: 41 us -> none  [the longest x8 21.6 us: attend_head(): jnp.einsum('gqk,qgd->kd', probability_low, grad_three, preferred_element_...]
    sub x8 -> x0, matrix products: 22.9 us -> none  [attend_head(): weights = jnp.where(allowed, jnp.exp(scores - largest), 0.0)]
    dynamic_slice x28 -> x0, local copies, waits for them, and re-layouts: 21.5 us -> none  [the longest x4 3.68 us: visit(): lax.dynamic_slice_in_dim(cache_keys, owner_row, LP, 0)]
    pallas_call x0 -> x6, Pallas kernels: none -> 19.4 us  [the longest x2 15.5 us: attend(): pl.pallas_call(functools.partial(attend_kernel, first), out_shape=(jax.Sh...]
  transfers between devices with their start and end apart: 6 -> 1, of which waited for: 5 -> 0; matrix products, arithmetic and copies ran while one was open for 2% -> 0% of each run, Pallas kernels for 0% -> 6%
where the time goes in v1:
time: 137 us; the launch traced here: 136 us
  blocking collectives  102 us (74%)
  Pallas kernels  19.4 us (14%)
  local copies, waits for them, and re-layouts  9.13 us (7%)
  starting transfers between devices  4.69 us (3%)
    all_to_all x2, blocking collectives, over_store(): lax.all_to_all(array, ('resp', 'tp'), split_axis=0, concat_axis=0, tiled=...  51.8 us
    all_to_all x3, blocking collectives, over_pick(): lax.all_to_all(array, 'resp', split_axis=0, concat_axis=0, tiled=True, ax...  49.9 us
    pallas_call x2, Pallas kernels, attend(): pl.pallas_call(functools.partial(attend_kernel, first), out_shape=(jax.Sh...  15.5 us
    unnamed x20, local copies, waits for them, and re-layouts  9.13 us
    all_to_all x1, starting transfers between devices, over_pick(): lax.all_to_all(array, 'resp', split_axis=0, concat_axis=0, tiled=True, ax...  4.69 us
    pallas_call x4, Pallas kernels, in_vmem(): pl.pallas_call(kernel, out_shape=out_shape, in_specs=[pl.BlockSpec(memory...  3.86 us
  transfers between devices with their start and end apart: 1, of which 0 were waited for; matrix products, arithmetic and copies ran while one was open for 0% of the time, Pallas kernels for 6%

profile of v1, /device:TPU:1, one launch (start us, length us, event | category | flops | bytes accessed | tf_op | source)
XLA Modules:
  0.0 135.7 jit_solution(9485033340597171280)
XLA Ops:
  0.6 0.0 copy-start
  0.6 0.7 copy-done
  1.4 0.0 copy-start.1
  1.4 0.8 copy-done.1
  2.2 0.0 copy-start.2
  2.2 0.7 copy-done.2
  2.8 0.0 copy-start.7
  2.8 0.0 copy-start.8
  2.8 0.0 copy-start.9
  2.8 0.6 shard_map.127
  3.4 30.6 %all_to_all.30.pieces_ref = bf16[64,24,128]{2,1,0:T(8,128)(2,1)S(1)} all-to-all(bf16[64,24,128]{2,1,0:T(8,128)(2,1)S(1)} %shard_map.127), channel_id=1, replica_groups={{0,5,10,15,16,21,26,31,32,37,42,47,48,53,58,63,64,69,74,79,80,85,90,95,..., dimensions={0} | all-to-all | bytes 786432 | tf_op jit(solution)/shard_map/all_to_all | solution.py:39
  34.0 1.6 %shard_map.128 = (bf16[16,2,64,128]{3,2,1,0:T(8,128)(2,1)S(1)}, bf16[16,2,64,128]{3,2,1,0:T(8,128)(2,1)}, s32[16,128]{1,0:T(8,128)S(1)}) custom-call(bf16[64,24,128]{2,1,0:T(8,128)(2,1)S(1)} %all_to_all.30.pieces_ref), custom_call_target="tpu_custom_call" | custom-call | tf_op jit(solution)/shard_map/pallas_call | solution.py:333
  35.5 15.5 %all_to_all.31 = bf16[16,2,64,128]{3,2,1,0:T(8,128)(2,1)S(1)} all-to-all(bf16[16,2,64,128]{3,2,1,0:T(8,128)(2,1)S(1)} %get-tuple-element.22), channel_id=1, replica_groups={{0,4,8,12,32,36,40,44,64,68,72,76,96,100,104,108},{16,20,24,28,48,52,56..., dimensions={0} | all-to-all | bytes 1048576 | tf_op jit(solution)/shard_map/all_to_all | solution.py:50
  51.0 4.7 %all-to-all-start.1 = ((bf16[16,2,64,128]{3,2,1,0:T(8,128)(2,1)}), bf16[16,2,64,128]{3,2,1,0:T(8,128)(2,1)S(1)}, u32[]{:S(2)}, u32[]{:S(2)}) async-start(bf16[16,2,64,128]{3,2,1,0:T(8,128)(2,1)} %get-tuple-element.21), calls=%async_computation.1 | async-start | bytes 1048576 | tf_op jit(solution)/shard_map/all_to_all | solution.py:50
  55.7 0.0 copy-done.7
  55.7 0.0 copy-done.8
  55.7 0.0 copy-done.9
  55.8 0.0 copy-start.3
  55.8 1.7 %copy-done.3 = bf16[640,2048]{1,0:T(8,128)(2,1)S(1)} copy-done((bf16[640,2048]{1,0:T(8,128)(2,1)S(1)}, bf16[640,2048]{1,0:T(8,128)(2,1)}, u32[]{:S(2)}) %copy-start.3) | copy-done | bytes 2621464
  57.5 0.0 copy-start.5
  57.5 1.7 %copy-done.5 = bf16[640,2048]{1,0:T(8,128)(2,1)S(1)} copy-done((bf16[640,2048]{1,0:T(8,128)(2,1)S(1)}, bf16[640,2048]{1,0:T(8,128)(2,1)}, u32[]{:S(2)}) %copy-start.5) | copy-done | bytes 2621464
  59.2 8.6 %shard_map.129 = (bf16[640,2048]{1,0:T(8,128)(2,1)}, bf16[640,2048]{1,0:T(8,128)(2,1)}, bf16[640,256]{1,0:T(8,128)(2,1)}, bf16[640,256]{1,0:T(8,128)(2,1)}, bf16[2,2,4,2,64,128]{5,4,3,2,1,0:T(8,128)(2,1)S(1)}) custom-call(s32[4]{0:T(128)S(1)} %copy-done.9, bf16[640,2048]{1,0:T(8,128)(2,1)S(1)} %copy-done.3, bf16[640,2048]{1,0:T(8,128)(2,1)S(1)} %copy-done.5, ...), custom_call_target="tpu_custom_call" | custom-call | flops 6543114240 | bytes 5242880 | tf_op jit(solution)/shard_map/pallas_call | solution.py:291
  67.9 0.0 all-to-all-done.1
  67.9 0.0 copy-start.4
  67.9 1.7 %copy-done.4 = bf16[640,2048]{1,0:T(8,128)(2,1)S(1)} copy-done((bf16[640,2048]{1,0:T(8,128)(2,1)S(1)}, bf16[640,2048]{1,0:T(8,128)(2,1)}, u32[]{:S(2)}) %copy-start.4) | copy-done | bytes 2621464
  69.6 1.7 %copy-done.6 = bf16[640,2048]{1,0:T(8,128)(2,1)S(1)} copy-done((bf16[640,2048]{1,0:T(8,128)(2,1)S(1)}, bf16[640,2048]{1,0:T(8,128)(2,1)}, u32[]{:S(2)}) %copy-start.6) | copy-done | bytes 2621464
  71.3 6.9 %shard_map.130 = (bf16[640,2048]{1,0:T(8,128)(2,1)}, bf16[640,2048]{1,0:T(8,128)(2,1)}, bf16[640,256]{1,0:T(8,128)(2,1)}, bf16[640,256]{1,0:T(8,128)(2,1)}, bf16[2,2,4,2,64,128]{5,4,3,2,1,0:T(8,128)(2,1)S(1)}) custom-call(s32[4]{0:T(128)S(1)} %copy-done.9, ...), custom_call_target="tpu_custom_call", output_to_operand_aliasing={{0}: (6, {}), {1}: (7, {}), {2}: (8, {}), {3}: (9, {})} | custom-call | flops 6543114240 | bytes 5242880 | tf_op jit(solution)/shard_map/pallas_call | solution.py:291
  78.3 21.0 %all_to_all.32.second_ref = bf16[16,2,64,128]{3,2,1,0:T(8,128)(2,1)S(1)} all-to-all(bf16[16,2,64,128]{3,2,1,0:T(8,128)(2,1)S(1)} %bitcast.7), channel_id=1, replica_groups={{0,4,8,12,32,36,40,44,64,68,72,76,96,100,104,108},{16,20,24,28,48,52,56..., dimensions={0} | all-to-all | bytes 1048576 | tf_op jit(solution)/shard_map/all_to_all | solution.py:50
  99.2 13.4 %all_to_all.33.first_ref = bf16[16,2,64,128]{3,2,1,0:T(8,128)(2,1)S(1)} all-to-all(bf16[16,2,64,128]{3,2,1,0:T(8,128)(2,1)S(1)} %bitcast.5), channel_id=1, replica_groups={{0,4,8,12,32,36,40,44,64,68,72,76,96,100,104,108},{16,20,24,28,48,52,56..., dimensions={0} | all-to-all | bytes 1048576 | tf_op jit(solution)/shard_map/all_to_all | solution.py:50
  112.7 1.1 shard_map.131
  113.8 21.2 %all_to_all.34.sums_ref = bf16[64,16,128]{2,1,0:T(8,128)(2,1)S(1)} all-to-all(bf16[64,16,128]{2,1,0:T(8,128)(2,1)S(1)} %shard_map.131), channel_id=1, replica_groups={{0,5,10,15,16,21,26,31,32,37,42,47,48,53,58,63,64,69,74,79,80,85,90,95,..., dimensions={0} | all-to-all | bytes 524288 | tf_op jit(solution)/shard_map/all_to_all | solution.py:39
  135.0 0.7 shard_map.132
  (1 shorter events, 0.0 us)
Async XLA Ops:
  0.6 0.8 copy-start
  1.4 0.8 copy-start.1
  2.2 0.7 copy-start.2
  2.8 52.9 %copy-start.7 = (bf16[640,256]{1,0:T(8,128)(2,1)S(1)}, bf16[640,256]{1,0:T(8,128)(2,1)}, u32[]{:S(2)}) copy-start(bf16[640,256]{1,0:T(8,128)(2,1)} %key_ref.5) | copy-start | bytes 983044
  2.8 52.9 %copy-start.8 = (bf16[640,256]{1,0:T(8,128)(2,1)S(1)}, bf16[640,256]{1,0:T(8,128)(2,1)}, u32[]{:S(2)}) copy-start(bf16[640,256]{1,0:T(8,128)(2,1)} %value_ref.5) | copy-start | bytes 983044
  2.8 52.9 %copy-start.9 = (s32[4]{0:T(128)S(1)}, s32[4]{0:T(128)}, u32[]{:S(2)}) copy-start(s32[4]{0:T(128)} %length_ref.3) | copy-start | bytes 52
  51.0 16.8 %all-to-all-start.1 = ((bf16[16,2,64,128]{3,2,1,0:T(8,128)(2,1)}), bf16[16,2,64,128]{3,2,1,0:T(8,128)(2,1)S(1)}, u32[]{:S(2)}, u32[]{:S(2)}) async-start(bf16[16,2,64,128]{3,2,1,0:T(8,128)(2,1)} %get-tuple-element.21), calls=%async_computation.1 | async-start | bytes 1048576 | tf_op jit(solution)/shard_map/all_to_all | solution.py:50
  55.8 1.7 %copy-start.3 = (bf16[640,2048]{1,0:T(8,128)(2,1)S(1)}, bf16[640,2048]{1,0:T(8,128)(2,1)}, u32[]{:S(2)}) copy-start(bf16[640,2048]{1,0:T(8,128)(2,1)} %query_ref.3) | copy-start | bytes 7864324
  57.5 1.7 %copy-start.5 = (bf16[640,2048]{1,0:T(8,128)(2,1)S(1)}, bf16[640,2048]{1,0:T(8,128)(2,1)}, u32[]{:S(2)}) copy-start(bf16[640,2048]{1,0:T(8,128)(2,1)} %grad_ref.3) | copy-start | bytes 7864324
  67.9 1.7 %copy-start.4 = (bf16[640,2048]{1,0:T(8,128)(2,1)S(1)}, bf16[640,2048]{1,0:T(8,128)(2,1)}, u32[]{:S(2)}) copy-start(bf16[640,2048]{1,0:T(8,128)(2,1)} %query_ref.3) | copy-start | bytes 7864324
  69.6 1.7 %copy-start.6 = (bf16[640,2048]{1,0:T(8,128)(2,1)S(1)}, bf16[640,2048]{1,0:T(8,128)(2,1)}, u32[]{:S(2)}) copy-start(bf16[640,2048]{1,0:T(8,128)(2,1)} %grad_ref.3) | copy-start | bytes 7864324

commit v2 on v1

v2 whole, which is shorter than its diff:
```python
import jax
import jax.numpy as jnp
from jax import lax
from jax.experimental import pallas as pl
from jax.experimental.pallas import tpu as pltpu
from jax.sharding import PartitionSpec as P

HD = 128
LP = 256
ROWS = 32
PER_GROUP = 8
KV_LANE = 2
LANES = 4
GROUPS = 4
TILE = 16
MEMBERS = 16
PROMPTS = 16
LOCAL = 4
SLICE = LP // GROUPS
CHUNKS = 5
SENT = TILE + 8
LOG2E = 1.4426950408889634
LARGE = pltpu.CompilerParams(vmem_limit_bytes=48 * 1024 * 1024)
SMALL = pltpu.CompilerParams(vmem_limit_bytes=16 * 1024 * 1024)

STORE_GROUPS = [
    [(p * 4 + (turn + t) % 4) * 4 + t for p in range(PROMPTS) for t in range(LANES)]
    for turn in range(4)
]
PICK_GROUPS = [
    [z * 32 + x * 8 + high * 4 + block for x in range(4) for block in range(4)]
    for z in range(2)
    for high in range(2)
]


def over_store(array):
    return lax.all_to_all(
        array,
        ("resp", "tp"),
        split_axis=0,
        concat_axis=0,
        tiled=True,
        axis_index_groups=STORE_GROUPS,
    )


def over_pick(array):
    return lax.all_to_all(
        array, "resp", split_axis=0, concat_axis=0, tiled=True, axis_index_groups=PICK_GROUPS
    )


def column_of(x):
    return (x // KV_LANE, x % KV_LANE)


def stored_kernel(
    owner_hbm, key_hbm, value_hbm, out_ref, owner_ref, key_ref, value_ref, sems
):
    copies = [
        pltpu.make_async_copy(source, target, sems.at[at])
        for at, (source, target) in enumerate(
            ((owner_hbm, owner_ref), (key_hbm, key_ref), (value_hbm, value_ref))
        )
    ]
    for copy in copies:
        copy.start()
    for copy in copies:
        copy.wait()
    at = lax.broadcasted_iota(jnp.int32, (SENT - TILE, HD), 1)
    asked = jnp.zeros((SENT - TILE, HD), jnp.int32)
    for one in range(LOCAL):
        asked = jnp.where(at == one, owner_ref[one], asked)
    asked = asked.astype(jnp.float32).astype(jnp.bfloat16)
    for prompt in range(PROMPTS):
        which, head = column_of(prompt // 2 % 4)
        source = value_ref if which else key_ref
        for lane in range(LANES):
            first = (lane * KV_LANE + head) * HD
            out_ref[prompt * LANES + lane] = jnp.concatenate(
                [source[:, first : first + HD], asked], 0
            )


def pick_kernel(pieces_ref, out_ref, owner_ref, owners, sem):
    resp = lax.axis_index("resp")
    prompt = resp // 4
    turn = (resp % 4 + LANES - lax.axis_index("tp")) % 4
    for x in range(4):
        for block in range(4):
            source = (prompt // 8 * 8 + x * 2 + prompt % 2) * LANES + (block + 4 - turn) % 4
            tile = pieces_ref[source].astype(jnp.float32)
            owner_ref[x * 4 + block : x * 4 + block + 1] = tile[TILE : TILE + 1].astype(jnp.int32)
    copy = pltpu.make_async_copy(owner_ref, owners, sem)
    copy.start()
    copy.wait()
    for member in range(MEMBERS):
        for one in range(LOCAL):
            owner = owners[member, one]
            for lane in range(LANES):
                out_ref[member, one, lane * TILE : (lane + 1) * TILE] = pieces_ref[
                    owner * LANES + lane, :TILE
                ]


def fold_kernel(owner_ref, terms_ref, token_ref, out_ref, total):
    total[...] = jnp.zeros_like(total)
    for one in range(LOCAL):
        for member in range(MEMBERS):
            owner = owner_ref[member, one]
            total[owner] += terms_ref[member, one].astype(jnp.float32)
    for prompt in range(PROMPTS):
        for lane in range(LANES):
            out_ref[prompt * LANES + lane] = total[
                prompt, lane * TILE : (lane + 1) * TILE
            ].astype(out_ref.dtype)


def summed_kernel(sums_ref, key_ref, value_ref):
    for x in range(4):
        which, head = column_of(x)
        target = value_ref if which else key_ref
        for lane in range(LANES):
            tile = jnp.zeros((TILE, HD), jnp.float32)
            for z in range(2):
                for high in range(2):
                    source = (z * 8 + x * 2 + high) * LANES + lane
                    tile = tile + sums_ref[source].astype(jnp.float32)
            first = (lane * KV_LANE + head) * HD
            target[:, first : first + HD] = tile.astype(target.dtype)


def heads(head):
    for at in range(PER_GROUP):
        column = (head * PER_GROUP + at) * HD
        yield slice(at * ROWS, (at + 1) * ROWS), slice(column, column + HD)


def by_length(length, span, work, blank):
    for first in range(0, span, 2 * ROWS):
        second = first + ROWS
        last = min(second + ROWS, span)
        if second < span:

            @pl.when(length > second)
            def _():
                work((first, second))

        @pl.when((length > first) & ((length <= second) | (second >= span)))
        def _():
            work((first,))
            if second < span:
                blank(second, last)

        @pl.when(length <= first)
        def _():
            blank(first, last)


def attend_kernel(
    length_ref,
    query_ref,
    grad_ref,
    key_ref,
    value_ref,
    prompt_ref,
    key_grad_ref,
    value_grad_ref,
    prompt_grad_ref,
    probability_ref,
    score_grad_ref,
    keys,
    values,
    stacked_query,
    stacked_grad,
    scores,
    prob_grads,
    key_total,
    value_total,
):
    length = length_ref[pl.program_id(0)]
    span = query_ref.shape[0]
    scale = HD**-0.5
    wide = PER_GROUP * ROWS
    for head in range(KV_LANE):
        for whole, own_ref, which in ((keys, key_ref, 0), (values, value_ref, 1)):
            whole[head, :LP] = prompt_ref[which, head, :, 0].reshape(LP, HD)
            whole[head, LP:] = own_ref[:, head * HD : (head + 1) * HD]

    def score(slot, head, first):
        count = LP + first + ROWS
        lane = lax.broadcasted_iota(jnp.int32, (1, wide), 1) % ROWS
        causal = lax.broadcasted_iota(jnp.int32, (ROWS, 1), 0) <= lane
        for part, column in heads(head):
            stacked_query[slot, part] = query_ref[first : first + ROWS, column]
            stacked_grad[slot, part] = grad_ref[first : first + ROWS, column]
        raw = lax.dot_general(
            keys[head, :count],
            stacked_query[slot],
            (((1,), (1,)), ((), ())),
            preferred_element_type=jnp.float32,
        )
        tail = jnp.where(causal, raw[count - ROWS :], -1e30)
        scores[slot, : count - ROWS] = raw[: count - ROWS]
        scores[slot, count - ROWS : count] = tail
        top = jnp.max(raw[: count - ROWS].reshape(-1, 8, wide), axis=0)
        top = jnp.maximum(top, jnp.max(tail.reshape(-1, 8, wide), axis=0))
        prob_grads[slot, :count] = lax.dot_general(
            values[head, :count],
            stacked_grad[slot],
            (((1,), (1,)), ((), ())),
            preferred_element_type=jnp.float32,
        )
        return jnp.max(top, axis=0, keepdims=True) * (scale * LOG2E)

    def soften(slot, head, first, largest):
        count = LP + first + ROWS
        chunk = first // ROWS
        lane = lax.broadcasted_iota(jnp.int32, (1, wide), 1) % ROWS
        live = first + lane < length
        blocks = [slice(at, at + ROWS) for at in range(0, count, ROWS)]
        total = jnp.zeros((8, wide), jnp.float32)
        for block in blocks:
            weights = jnp.exp2(scores[slot, block] * (scale * LOG2E) - largest)
            scores[slot, block] = weights
            total = total + jnp.sum(weights.reshape(-1, 8, wide), axis=0)
        inverse = jnp.where(live, 1.0 / jnp.sum(total, axis=0, keepdims=True), 0.0)
        total = jnp.zeros((8, wide), jnp.float32)
        for block in blocks:
            probability = scores[slot, block] * inverse
            probability_ref[0, head, chunk, block] = probability.astype(jnp.bfloat16)
            terms = probability * prob_grads[slot, block]
            total = total + jnp.sum(terms.reshape(-1, 8, wide), axis=0)
        delta = jnp.sum(total, axis=0, keepdims=True)
        for block in blocks:
            probability = scores[slot, block] * inverse
            score_grad_ref[0, head, chunk, block] = (
                probability * (prob_grads[slot, block] - delta)
            ).astype(jnp.bfloat16)

    def gather(slot, head, first):
        count = LP + first + ROWS
        chunk = first // ROWS
        for total, left_ref, stacked in (
            (value_total, probability_ref, stacked_grad),
            (key_total, score_grad_ref, stacked_query),
        ):
            terms = jnp.dot(
                left_ref[0, head, chunk, :count],
                stacked[slot],
                preferred_element_type=jnp.float32,
            )
            if first == 0:
                total[head, :count] = terms
            else:
                total[head, : count - ROWS] += terms[: count - ROWS]
                total[head, count - ROWS : count] = terms[count - ROWS :]

    def work(firsts):
        streams = [(head, first) for first in firsts for head in range(KV_LANE)]
        largest = {0: score(0, *streams[0])}
        for slot, stream in enumerate(streams):
            if slot + 1 < len(streams):
                largest[slot + 1] = score(slot + 1, *streams[slot + 1])
            soften(slot, *stream, largest[slot])
            gather(slot, *stream)

    def blank(first, last):
        zeros = jnp.zeros((KV_LANE, last - first, HD), jnp.float32)
        key_total[:, LP + first : LP + last] = zeros
        value_total[:, LP + first : LP + last] = zeros

    by_length(length, span, work, blank)

    for head in range(KV_LANE):
        lanes = slice(head * HD, (head + 1) * HD)
        key_terms = (key_total[head] * scale).astype(jnp.bfloat16)
        value_terms = value_total[head].astype(jnp.bfloat16)
        prompt_grad_ref[0, head, :, 0] = key_terms[:LP].reshape(GROUPS, SLICE, HD)
        prompt_grad_ref[1, head, :, 0] = value_terms[:LP].reshape(GROUPS, SLICE, HD)
        key_grad_ref[:, lanes] = key_terms[LP:]
        value_grad_ref[:, lanes] = value_terms[LP:]


def outputs_kernel(
    length_ref,
    key_ref,
    value_ref,
    prompt_ref,
    probability_ref,
    score_grad_ref,
    out_ref,
    query_grad_ref,
    token_ref,
    keys_t,
    values_t,
):
    length = length_ref[pl.program_id(0)]
    span = out_ref.shape[0]
    scale = HD**-0.5
    for head in range(KV_LANE):
        lanes = slice(head * HD, (head + 1) * HD)
        for whole_t, own_ref, which in ((keys_t, key_ref, 0), (values_t, value_ref, 1)):
            whole_t[head] = jnp.concatenate(
                [prompt_ref[which, head, :, 0].reshape(LP, HD), own_ref[:, lanes]], 0
            ).T

    def work(firsts):
        for first in firsts:
            count = LP + first + ROWS
            chunk = first // ROWS
            rows = slice(first, first + ROWS)
            for head in range(KV_LANE):
                output = jnp.dot(
                    values_t[head, :, :count],
                    probability_ref[0, head, chunk, :count],
                    preferred_element_type=jnp.float32,
                )
                query_grad = jnp.dot(
                    keys_t[head, :, :count],
                    score_grad_ref[0, head, chunk, :count],
                    preferred_element_type=jnp.float32,
                )
                output = output.astype(jnp.bfloat16).T
                query_grad = (query_grad * scale).astype(jnp.bfloat16).T
                for part, column in heads(head):
                    out_ref[rows, column] = output[part]
                    query_grad_ref[rows, column] = query_grad[part]

    def blank(first, last):
        zeros = jnp.zeros((last - first, out_ref.shape[1]), jnp.bfloat16)
        out_ref[first:last, :] = zeros
        query_grad_ref[first:last, :] = zeros

    by_length(length, span, work, blank)
    token_ref[...] = jnp.zeros_like(token_ref)


def specs(span, wide, narrow):
    both = LP + span
    stacked = PER_GROUP * ROWS
    return dict(
        wide=pl.BlockSpec((span, wide), lambda i, length: (i, 0)),
        narrow=pl.BlockSpec((span, narrow), lambda i, length: (i, 0)),
        prompt=pl.BlockSpec(
            (2, KV_LANE, GROUPS, 1, SLICE, HD), lambda i, length: (0, 0, 0, i, 0, 0)
        ),
        kept=pl.BlockSpec(
            (1, KV_LANE, CHUNKS, both, stacked), lambda i, length: (i, 0, 0, 0, 0)
        ),
    )


def attend(lengths, queries, out_grad, resp_keys, resp_values, prompt_rows):
    count = lengths.shape[0]
    span = queries.shape[0] // count
    both = LP + span
    streams = 2 * KV_LANE
    stacked = PER_GROUP * ROWS
    spec = specs(span, queries.shape[1], resp_keys.shape[1])
    kept = jax.ShapeDtypeStruct((count, KV_LANE, CHUNKS, both, stacked), jnp.bfloat16)
    return pl.pallas_call(
        attend_kernel,
        out_shape=(
            jax.ShapeDtypeStruct(resp_keys.shape, jnp.bfloat16),
            jax.ShapeDtypeStruct(resp_keys.shape, jnp.bfloat16),
            jax.ShapeDtypeStruct(prompt_rows.shape, jnp.bfloat16),
            kept,
            kept,
        ),
        grid_spec=pltpu.PrefetchScalarGridSpec(
            num_scalar_prefetch=1,
            grid=(count,),
            in_specs=[spec[name] for name in ("wide", "wide", "narrow", "narrow", "prompt")],
            out_specs=[spec[name] for name in ("narrow", "narrow", "prompt", "kept", "kept")],
            scratch_shapes=[
                pltpu.VMEM((KV_LANE, both, HD), jnp.bfloat16),
                pltpu.VMEM((KV_LANE, both, HD), jnp.bfloat16),
                pltpu.VMEM((streams, stacked, HD), jnp.bfloat16),
                pltpu.VMEM((streams, stacked, HD), jnp.bfloat16),
                pltpu.VMEM((streams, both, stacked), jnp.float32),
                pltpu.VMEM((streams, both, stacked), jnp.float32),
                pltpu.VMEM((KV_LANE, both, HD), jnp.float32),
                pltpu.VMEM((KV_LANE, both, HD), jnp.float32),
            ],
        ),
        compiler_params=LARGE,
        cost_estimate=pl.CostEstimate(
            flops=16 * queries.size * both,
            bytes_accessed=4 * queries.size,
            transcendentals=queries.size * both // HD,
        ),
    )(lengths, queries, out_grad, resp_keys, resp_values, prompt_rows)


def outputs(lengths, resp_keys, resp_values, prompt_rows, probability, score_grad, wide):
    count = lengths.shape[0]
    rows = resp_keys.shape[0]
    span = rows // count
    both = LP + span
    spec = specs(span, wide, resp_keys.shape[1])
    shape = jax.ShapeDtypeStruct((rows, wide), jnp.bfloat16)
    return pl.pallas_call(
        outputs_kernel,
        out_shape=(shape, shape, jax.ShapeDtypeStruct((8, HD), jnp.int32)),
        grid_spec=pltpu.PrefetchScalarGridSpec(
            num_scalar_prefetch=1,
            grid=(count,),
            in_specs=[spec[name] for name in ("narrow", "narrow", "prompt", "kept", "kept")],
            out_specs=[
                spec["wide"],
                spec["wide"],
                pl.BlockSpec((8, HD), lambda i, length: (0, 0)),
            ],
            scratch_shapes=[
                pltpu.VMEM((KV_LANE, HD, both), jnp.bfloat16),
                pltpu.VMEM((KV_LANE, HD, both), jnp.bfloat16),
            ],
        ),
        compiler_params=LARGE,
        cost_estimate=pl.CostEstimate(
            flops=8 * rows * wide * both,
            bytes_accessed=4 * rows * wide + 4 * probability.size,
            transcendentals=0,
        ),
    )(lengths, resp_keys, resp_values, prompt_rows, probability, score_grad)


def whole(kernel, out_shape, spaces, *operands, **more):
    return pl.pallas_call(
        kernel,
        out_shape=out_shape,
        in_specs=[pl.BlockSpec(memory_space=space) for space in spaces],
        compiler_params=SMALL,
        **more,
    )(*operands)


def low(*shape):
    return jax.ShapeDtypeStruct(shape, jnp.bfloat16)


def shards(
    queries, resp_keys, resp_values, out_grad, prompt_keys, prompt_values, lengths, prompt_of
):
    pieces = over_store(
        whole(
            stored_kernel,
            low(PROMPTS * LANES, SENT, HD),
            [pltpu.HBM] * 3,
            prompt_of,
            prompt_keys,
            prompt_values,
            scratch_shapes=[
                pltpu.SMEM(prompt_of.shape, jnp.int32),
                pltpu.VMEM(prompt_keys.shape, jnp.bfloat16),
                pltpu.VMEM(prompt_values.shape, jnp.bfloat16),
                pltpu.SemaphoreType.DMA((3,)),
            ],
        )
    )
    picked, owners = whole(
        pick_kernel,
        (low(MEMBERS, LOCAL, SLICE, HD), jax.ShapeDtypeStruct((MEMBERS, HD), jnp.int32)),
        [pltpu.VMEM],
        pieces,
        scratch_shapes=[pltpu.SMEM((MEMBERS, HD), jnp.int32), pltpu.SemaphoreType.DMA],
    )
    prompt_rows = over_pick(picked).reshape(2, KV_LANE, GROUPS, LOCAL, SLICE, HD)
    resp_key_grad, resp_value_grad, terms, probability, score_grad = attend(
        lengths, queries, out_grad, resp_keys, resp_values, prompt_rows
    )
    terms = over_pick(terms.reshape(MEMBERS, LOCAL, SLICE, HD))
    attn_out, query_grad, token = outputs(
        lengths, resp_keys, resp_values, prompt_rows, probability, score_grad, queries.shape[1]
    )
    sums = whole(
        fold_kernel,
        low(PROMPTS * LANES, TILE, HD),
        [pltpu.SMEM, pltpu.VMEM, pl.ANY],
        owners,
        terms,
        token,
        scratch_shapes=[pltpu.VMEM((PROMPTS, SLICE, HD), jnp.float32)],
    )
    prompt_key_grad, prompt_value_grad = whole(
        summed_kernel,
        (low(*prompt_keys.shape), low(*prompt_values.shape)),
        [pltpu.VMEM],
        over_store(sums),
    )
    return (
        attn_out,
        query_grad,
        resp_key_grad,
        resp_value_grad,
        prompt_key_grad,
        prompt_value_grad,
    )


def solution(mesh):
    wide = P("resp", "tp")
    stored = P(("resp", "tp"), None)
    return jax.shard_map(
        shards,
        mesh=mesh,
        in_specs=(wide, wide, wide, wide, stored, stored, P("resp"), P("resp")),
        out_specs=(wide, wide, wide, wide, stored, stored),
        check_vma=False,
    )
```

time: 137 us -> 116 us (0.85)
  blocking collectives: 102 us -> 71.1 us
  Pallas kernels: 19.4 us -> 31.1 us
  local copies, waits for them, and re-layouts: 9.13 us -> 2.24 us
  waiting for transfers between devices: 0.01 us -> 4.38 us
    all_to_all x3 -> x1, blocking collectives: 49.9 us -> 21.1 us  [over_pick(): lax.all_to_all(array, 'resp', split_axis=0, concat_axis=0, tiled=True, ax...]
    pallas_call x6, Pallas kernels: 19.4 us -> 31.1 us  [the longest x1 16.6 us: attend(): pl.pallas_call(attend_kernel, out_shape=(jax.ShapeDtypeStruct(resp_keys.s...]
    unnamed x20 -> x14, local copies, waits for them, and re-layouts: 9.13 us -> 2.24 us
    all_to_all x1, waiting for transfers between devices: 0.01 us -> 4.38 us  [over_pick(): lax.all_to_all(array, 'resp', split_axis=0, concat_axis=0, tiled=True, ax...]
    all_to_all x2, blocking collectives: 51.8 us -> 50 us  [over_store(): lax.all_to_all(array, ('resp', 'tp'), split_axis=0, concat_axis=0, tiled=...]
  transfers between devices with their start and end apart: 1 -> 1, of which waited for: 0 -> 1; matrix products, arithmetic and copies ran while one was open for 0% -> 0% of each run, Pallas kernels for 6% -> 10%
where the time goes in v2:
time: 116 us; the launch traced here: 114 us
  blocking collectives  71.1 us (61%)
  Pallas kernels  31.1 us (27%)
  starting transfers between devices  4.6 us (4%)
  waiting for transfers between devices  4.38 us (4%)
  local copies, waits for them, and re-layouts  2.24 us (2%)
    all_to_all x2, blocking collectives, over_store(): lax.all_to_all(array, ('resp', 'tp'), split_axis=0, concat_axis=0, tiled=...  50 us
    all_to_all x1, blocking collectives, over_pick(): lax.all_to_all(array, 'resp', split_axis=0, concat_axis=0, tiled=True, ax...  21.1 us
    pallas_call x1, Pallas kernels, attend(): pl.pallas_call(attend_kernel, out_shape=(jax.ShapeDtypeStruct(resp_keys.s...  16.6 us
    pallas_call x1, Pallas kernels, outputs(): pl.pallas_call(outputs_kernel, out_shape=(shape, shape, jax.ShapeDtypeStr...  11.3 us
    all_to_all x1, starting transfers between devices, over_pick(): lax.all_to_all(array, 'resp', split_axis=0, concat_axis=0, tiled=True, ax...  4.6 us
    all_to_all x1, waiting for transfers between devices, over_pick(): lax.all_to_all(array, 'resp', split_axis=0, concat_axis=0, tiled=True, ax...  4.38 us
    pallas_call x4, Pallas kernels, whole(): pl.pallas_call(kernel, out_shape=out_shape, in_specs=[pl.BlockSpec(memory...  3.18 us
  transfers between devices with their start and end apart: 1, of which 1 were waited for; matrix products, arithmetic and copies ran while one was open for 0% of the time, Pallas kernels for 10%

profile of v2, /device:TPU:1, one launch (start us, length us, event | category | flops | bytes accessed | tf_op | source)
XLA Modules:
  0.0 114.1 jit_solution(13390910460734214749)
XLA Ops:
  0.6 0.0 copy-start.1
  0.6 0.0 copy-start
  0.7 0.0 copy-start.2
  0.7 0.8 copy-done.2
  1.5 0.0 copy-start.3
  1.5 0.8 copy-done.3
  2.2 0.0 copy-start.5
  2.2 0.7 copy-done.5
  2.9 0.0 copy-start.4
  2.9 0.0 copy-start.6
  2.9 0.6 shard_map.127
  3.5 30.7 %all_to_all.20.pieces_ref = bf16[64,24,128]{2,1,0:T(8,128)(2,1)S(1)} all-to-all(bf16[64,24,128]{2,1,0:T(8,128)(2,1)S(1)} %shard_map.127), channel_id=1, replica_groups={{0,5,10,15,16,21,26,31,32,37,42,47,48,53,58,63,64,69,74,79,80,85,90,95,..., dimensions={0} | all-to-all | bytes 786432 | tf_op jit(solution)/shard_map/all_to_all | solution.py:38
  34.2 0.8 shard_map.128
  35.0 21.1 %all_to_all.21 = bf16[16,4,64,128]{3,2,1,0:T(8,128)(2,1)S(1)} all-to-all(bf16[16,4,64,128]{3,2,1,0:T(8,128)(2,1)S(1)} %get-tuple-element.18), channel_id=1, replica_groups={{0,4,8,12,32,36,40,44,64,68,72,76,96,100,104,108},{16,20,24,28,48,52,56..., dimensions={0} | all-to-all | bytes 2097152 | tf_op jit(solution)/shard_map/all_to_all | solution.py:49
  56.1 0.0 copy-done.1
  56.1 0.0 copy-done
  56.1 0.0 copy-done.4
  56.1 0.0 copy-done.6
  56.1 16.6 %shard_map.129 = (bf16[640,256]{1,0:T(8,128)(2,1)}, bf16[640,256]{1,0:T(8,128)(2,1)}, bf16[2,2,4,4,64,128]{5,4,3,2,1,0:T(8,128)(2,1)}, bf16[4,2,5,416,256]{4,3,2,1,0:T(8,128)(2,1)}, bf16[4,2,5,416,256]{4,3,2,1,0:T(8,128)(2,1)}) custom-call(s32[4]{0:T(128)S(1)} %copy-done.4, bf16[640,2048]{1,0:T(8,128)(2,1)S(1)} %copy-done.6, bf16[640,2048]{1,0:T(8,128)(2,1)} %grad_ref.1, ...), custom_call_target="tpu_custom_call" | custom-call | flops 8724152320 | bytes 5242880 | tf_op jit(solution)/shard_map/pallas_call | solution.py:363
  72.8 4.6 %all-to-all-start.2 = ((bf16[16,4,64,128]{3,2,1,0:T(8,128)(2,1)}), bf16[16,4,64,128]{3,2,1,0:T(8,128)(2,1)S(1)}, u32[]{:S(2)}, u32[]{:S(2)}) async-start(bf16[16,4,64,128]{3,2,1,0:T(8,128)(2,1)} %bitcast.1), calls=%async_computation.2 | async-start | bytes 2097152 | tf_op jit(solution)/shard_map/all_to_all | solution.py:49
  77.4 11.3 %shard_map.130 = (bf16[640,2048]{1,0:T(8,128)(2,1)}, bf16[640,2048]{1,0:T(8,128)(2,1)}, s32[8,128]{1,0:T(8,128)S(1)}) custom-call(s32[4]{0:T(128)S(1)} %copy-done.4, bf16[640,256]{1,0:T(8,128)(2,1)S(1)} %copy-done, bf16[640,256]{1,0:T(8,128)(2,1)S(1)} %copy-done.1, bf16[2,2,4,4,64,128]{5,4,3,2,1,0:T(8,128)(2,1)S(1)} %bitcast.3, ...), custom_call_target="tpu_custom_call" | custom-call | flops 4362076160 | bytes 22282240 | tf_op jit(solution)/shard_map/pallas_call | solution.py:404
  88.7 4.4 %all-to-all-done.2.terms_ref = bf16[16,4,64,128]{3,2,1,0:T(8,128)(2,1)S(1)} async-done(((bf16[16,4,64,128]{3,2,1,0:T(8,128)(2,1)}), bf16[16,4,64,128]{3,2,1,0:T(8,128)(2,1)S(1)}, u32[]{:S(2)}, u32[]{:S(2)}) %all-to-all-start.2) | async-done | bytes 1048608 | tf_op jit(solution)/shard_map/all_to_all | solution.py:49
  93.1 1.1 shard_map.131
  94.2 19.3 %all_to_all.22.sums_ref = bf16[64,16,128]{2,1,0:T(8,128)(2,1)S(1)} all-to-all(bf16[64,16,128]{2,1,0:T(8,128)(2,1)S(1)} %shard_map.131), channel_id=1, replica_groups={{0,5,10,15,16,21,26,31,32,37,42,47,48,53,58,63,64,69,74,79,80,85,90,95,..., dimensions={0} | all-to-all | bytes 524288 | tf_op jit(solution)/shard_map/all_to_all | solution.py:38
  113.5 0.7 shard_map.132
Async XLA Ops:
  0.6 55.5 %copy-start.1 = (bf16[640,256]{1,0:T(8,128)(2,1)S(1)}, bf16[640,256]{1,0:T(8,128)(2,1)}, u32[]{:S(2)}) copy-start(bf16[640,256]{1,0:T(8,128)(2,1)} %value_ref.3) | copy-start | bytes 983044
  0.6 55.5 %copy-start = (bf16[640,256]{1,0:T(8,128)(2,1)S(1)}, bf16[640,256]{1,0:T(8,128)(2,1)}, u32[]{:S(2)}) copy-start(bf16[640,256]{1,0:T(8,128)(2,1)} %key_ref.3) | copy-start | bytes 983044
  0.7 0.8 copy-start.2
  1.5 0.8 copy-start.3
  2.2 0.7 copy-start.5
  2.9 53.2 %copy-start.4 = (s32[4]{0:T(128)S(1)}, s32[4]{0:T(128)}, u32[]{:S(2)}) copy-start(s32[4]{0:T(128)} %length_ref.3) | copy-start | bytes 52
  2.9 53.2 %copy-start.6 = (bf16[640,2048]{1,0:T(8,128)(2,1)S(1)}, bf16[640,2048]{1,0:T(8,128)(2,1)}, u32[]{:S(2)}) copy-start(bf16[640,2048]{1,0:T(8,128)(2,1)} %query_ref.1) | copy-start | bytes 7864324
  72.8 20.3 %all-to-all-start.2 = ((bf16[16,4,64,128]{3,2,1,0:T(8,128)(2,1)}), bf16[16,4,64,128]{3,2,1,0:T(8,128)(2,1)S(1)}, u32[]{:S(2)}, u32[]{:S(2)}) async-start(bf16[16,4,64,128]{3,2,1,0:T(8,128)(2,1)} %bitcast.1), calls=%async_computation.2 | async-start | bytes 2097152 | tf_op jit(solution)/shard_map/all_to_all | solution.py:49

commit v3 on v2

--- a/solution.py
+++ b/solution.py
@@ -21,10 +21,17 @@
 SENT = TILE + 8
 LOG2E = 1.4426950408889634
 LARGE = pltpu.CompilerParams(vmem_limit_bytes=48 * 1024 * 1024)
+FIRST = pltpu.CompilerParams(vmem_limit_bytes=(64 * 1024 - 64) * 1024)
 SMALL = pltpu.CompilerParams(vmem_limit_bytes=16 * 1024 * 1024)
 
 STORE_GROUPS = [
-    [(p * 4 + (turn + t) % 4) * 4 + t for p in range(PROMPTS) for t in range(LANES)]
+    [
+        (z * 32 + x * 8 + high * 4 + (turn + t) % 4) * 4 + t
+        for x in range(4)
+        for t in range(LANES)
+    ]
+    for z in range(2)
+    for high in range(2)
     for turn in range(4)
 ]
 PICK_GROUPS = [
@@ -49,6 +56,18 @@
     return lax.all_to_all(
         array, "resp", split_axis=0, concat_axis=0, tiled=True, axis_index_groups=PICK_GROUPS
     )
+
+
+FLIPS = (4, 32, 36)
+
+
+def across(array, flip):
+    return lax.ppermute(array, "resp", [(at, at ^ flip) for at in range(64)])
+
+
+def corner():
+    prompt = lax.axis_index("resp") // 4
+    return prompt // 8, prompt % 2
 
 
 def column_of(x):
@@ -73,62 +92,73 @@
     for one in range(LOCAL):
         asked = jnp.where(at == one, owner_ref[one], asked)
     asked = asked.astype(jnp.float32).astype(jnp.bfloat16)
-    for prompt in range(PROMPTS):
-        which, head = column_of(prompt // 2 % 4)
+    for x in range(4):
+        which, head = column_of(x)
         source = value_ref if which else key_ref
         for lane in range(LANES):
             first = (lane * KV_LANE + head) * HD
-            out_ref[prompt * LANES + lane] = jnp.concatenate(
+            out_ref[x * LANES + lane] = jnp.concatenate(
                 [source[:, first : first + HD], asked], 0
             )
 
 
-def pick_kernel(pieces_ref, out_ref, owner_ref, owners, sem):
-    resp = lax.axis_index("resp")
-    prompt = resp // 4
-    turn = (resp % 4 + LANES - lax.axis_index("tp")) % 4
+def asked_kernel(pieces_ref, out_ref, owner_ref):
+    turn = (lax.axis_index("resp") % 4 + LANES - lax.axis_index("tp")) % 4
     for x in range(4):
         for block in range(4):
-            source = (prompt // 8 * 8 + x * 2 + prompt % 2) * LANES + (block + 4 - turn) % 4
-            tile = pieces_ref[source].astype(jnp.float32)
+            tile = pieces_ref[x * LANES + (block + 4 - turn) % 4].astype(jnp.float32)
             owner_ref[x * 4 + block : x * 4 + block + 1] = tile[TILE : TILE + 1].astype(jnp.int32)
-    copy = pltpu.make_async_copy(owner_ref, owners, sem)
-    copy.start()
-    copy.wait()
+    for member in range(MEMBERS):
+        out_ref[member] = pieces_ref[member, :TILE]
+
+
+def pick_kernel(owner_ref, own_ref, first_ref, second_ref, third_ref, out_ref, table):
+    z, high = corner()
+    for flip, part_ref in enumerate((own_ref, first_ref, second_ref, third_ref)):
+        for member in range(MEMBERS):
+            table[flip * MEMBERS + member] = part_ref[member]
     for member in range(MEMBERS):
         for one in range(LOCAL):
-            owner = owners[member, one]
+            owner = owner_ref[member, one]
+            flip = (owner // 8 + z) % 2 * 2 + (owner + high) % 2
+            source = flip * MEMBERS + owner // 2 % 4 * LANES
             for lane in range(LANES):
-                out_ref[member, one, lane * TILE : (lane + 1) * TILE] = pieces_ref[
-                    owner * LANES + lane, :TILE
-                ]
-
-
-def fold_kernel(owner_ref, terms_ref, token_ref, out_ref, total):
+                out_ref[member, one, lane * TILE : (lane + 1) * TILE] = table[source + lane]
+
+
+def fold_kernel(
+    owner_ref, terms_ref, token_ref, own_ref, first_ref, second_ref, third_ref, total
+):
+    z, high = corner()
     total[...] = jnp.zeros_like(total)
     for one in range(LOCAL):
         for member in range(MEMBERS):
             owner = owner_ref[member, one]
             total[owner] += terms_ref[member, one].astype(jnp.float32)
-    for prompt in range(PROMPTS):
-        for lane in range(LANES):
-            out_ref[prompt * LANES + lane] = total[
-                prompt, lane * TILE : (lane + 1) * TILE
-            ].astype(out_ref.dtype)
-
-
-def summed_kernel(sums_ref, key_ref, value_ref):
+    for flip, out_ref in enumerate((own_ref, first_ref, second_ref, third_ref)):
+        for x in range(4):
+            prompt = (z + flip // 2) % 2 * 8 + x * 2 + (high + flip) % 2
+            for lane in range(LANES):
+                out_ref[x * LANES + lane] = total[
+                    prompt, lane * TILE : (lane + 1) * TILE
+                ].astype(out_ref.dtype)
+
+
+def sum_kernel(own_ref, first_ref, second_ref, third_ref, out_ref):
+    for member in range(MEMBERS):
+        tile = own_ref[member]
+        for part_ref in (first_ref, second_ref, third_ref):
+            tile = tile + part_ref[member].astype(jnp.float32)
+        out_ref[member] = tile.astype(out_ref.dtype)
+
+
+def place_kernel(sums_ref, key_ref, value_ref):
     for x in range(4):
         which, head = column_of(x)
         target = value_ref if which else key_ref
         for lane in range(LANES):
-            tile = jnp.zeros((TILE, HD), jnp.float32)
-            for z in range(2):
-                for high in range(2):
-                    source = (z * 8 + x * 2 + high) * LANES + lane
-                    tile = tile + sums_ref[source].astype(jnp.float32)
             first = (lane * KV_LANE + head) * HD
-            target[:, first : first + HD] = tile.astype(target.dtype)
+            target[:, first : first + HD] = sums_ref[x * LANES + lane]
 
 
 def heads(head):
@@ -221,20 +251,18 @@
         live = first + lane < length
         blocks = [slice(at, at + ROWS) for at in range(0, count, ROWS)]
         total = jnp.zeros((8, wide), jnp.float32)
+        moved = jnp.zeros((8, wide), jnp.float32)
         for block in blocks:
             weights = jnp.exp2(scores[slot, block] * (scale * LOG2E) - largest)
             scores[slot, block] = weights
             total = total + jnp.sum(weights.reshape(-1, 8, wide), axis=0)
+            terms = weights * prob_grads[slot, block]
+            moved = moved + jnp.sum(terms.reshape(-1, 8, wide), axis=0)
         inverse = jnp.where(live, 1.0 / jnp.sum(total, axis=0, keepdims=True), 0.0)
-        total = jnp.zeros((8, wide), jnp.float32)
+        delta = jnp.sum(moved, axis=0, keepdims=True) * inverse
         for block in blocks:
             probability = scores[slot, block] * inverse
             probability_ref[0, head, chunk, block] = probability.astype(jnp.bfloat16)
-            terms = probability * prob_grads[slot, block]
-            total = total + jnp.sum(terms.reshape(-1, 8, wide), axis=0)
-        delta = jnp.sum(total, axis=0, keepdims=True)
-        for block in blocks:
-            probability = scores[slot, block] * inverse
             score_grad_ref[0, head, chunk, block] = (
                 probability * (prob_grads[slot, block] - delta)
             ).astype(jnp.bfloat16)
@@ -427,12 +455,12 @@
     )(lengths, resp_keys, resp_values, prompt_rows, probability, score_grad)
 
 
-def whole(kernel, out_shape, spaces, *operands, **more):
+def whole(kernel, out_shape, spaces, *operands, params=SMALL, **more):
     return pl.pallas_call(
         kernel,
         out_shape=out_shape,
         in_specs=[pl.BlockSpec(memory_space=space) for space in spaces],
-        compiler_params=SMALL,
+        compiler_params=params,
         **more,
     )(*operands)
 
@@ -447,11 +475,12 @@
     pieces = over_store(
         whole(
             stored_kernel,
-            low(PROMPTS * LANES, SENT, HD),
+            low(MEMBERS, SENT, HD),
             [pltpu.HBM] * 3,
             prompt_of,
             prompt_keys,
             prompt_values,
+            params=FIRST,
             scratch_shapes=[
                 pltpu.SMEM(prompt_of.shape, jnp.int32),
                 pltpu.VMEM(prompt_keys.shape, jnp.bfloat16),
@@ -460,12 +489,21 @@
             ],
         )
     )
-    picked, owners = whole(
-        pick_kernel,
-        (low(MEMBERS, LOCAL, SLICE, HD), jax.ShapeDtypeStruct((MEMBERS, HD), jnp.int32)),
+    part = (MEMBERS, TILE, HD)
+    own, owners = whole(
+        asked_kernel,
+        (low(*part), jax.ShapeDtypeStruct((MEMBERS, HD), jnp.int32)),
         [pltpu.VMEM],
         pieces,
-        scratch_shapes=[pltpu.SMEM((MEMBERS, HD), jnp.int32), pltpu.SemaphoreType.DMA],
+    )
+    picked = whole(
+        pick_kernel,
+        low(MEMBERS, LOCAL, SLICE, HD),
+        [pltpu.SMEM] + [pltpu.VMEM] * 4,
+        owners,
+        own,
+        *(across(own, flip) for flip in FLIPS),
+        scratch_shapes=[pltpu.VMEM((PROMPTS * LANES, TILE, HD), jnp.bfloat16)],
     )
     prompt_rows = over_pick(picked).reshape(2, KV_LANE, GROUPS, LOCAL, SLICE, HD)
     resp_key_grad, resp_value_grad, terms, probability, score_grad = attend(
@@ -475,17 +513,19 @@
     attn_out, query_grad, token = outputs(
         lengths, resp_keys, resp_values, prompt_rows, probability, score_grad, queries.shape[1]
     )
-    sums = whole(
+    own, *others = whole(
         fold_kernel,
-        low(PROMPTS * LANES, TILE, HD),
+        (jax.ShapeDtypeStruct(part, jnp.float32),) + (low(*part),) * 3,
         [pltpu.SMEM, pltpu.VMEM, pl.ANY],
         owners,
         terms,
         token,
         scratch_shapes=[pltpu.VMEM((PROMPTS, SLICE, HD), jnp.float32)],
     )
+    others = [across(other, flip) for other, flip in zip(others, FLIPS)]
+    sums = whole(sum_kernel, low(*part), [pltpu.VMEM] * 4, own, *others)
     prompt_key_grad, prompt_value_grad = whole(
-        summed_kernel,
+        place_kernel,
         (low(*prompt_keys.shape), low(*prompt_values.shape)),
         [pltpu.VMEM],
         over_store(sums),

time: 116 us -> 126 us (1.086); the launches traced: 114 us -> 126 us
  blocking collectives: 71.1 us -> 52 us
  starting transfers between devices: 4.6 us -> 21.7 us
  waiting for transfers between devices: 4.38 us -> 20.3 us
  local copies, waits for them, and re-layouts: 2.24 us -> 0.03 us
    all_to_all x2, blocking collectives: 50 us -> 32.1 us  [over_store(): lax.all_to_all(array, ('resp', 'tp'), split_axis=0, concat_axis=0, tiled=...]
    ppermute x0 -> x6, starting transfers between devices: none -> 16.3 us  [across(): return lax.ppermute(array, 'resp', [(at, at ^ flip) for at in range(64)])]
    ppermute x0 -> x6, waiting for transfers between devices: none -> 14.8 us  [across(): return lax.ppermute(array, 'resp', [(at, at ^ flip) for at in range(64)])]
    unnamed x14 -> x8, local copies, waits for them, and re-layouts: 2.24 us -> 0.03 us
    pallas_call x4 -> x6, Pallas kernels: 3.18 us -> 4.91 us  [whole(): pl.pallas_call(kernel, out_shape=out_shape, in_specs=[pl.BlockSpec(memory...]
  transfers between devices with their start and end apart: 1 -> 7, of which waited for: 1 -> 5; matrix products, arithmetic and copies ran while one was open for 0% -> 0% of each run, Pallas kernels for 10% -> 8%
where the time goes in v3:
time: 126 us
  blocking collectives  52 us (41%)
  Pallas kernels  31 us (25%)
  starting transfers between devices  21.7 us (17%)
  waiting for transfers between devices  20.3 us (16%)
    all_to_all x2, blocking collectives, over_store(): lax.all_to_all(array, ('resp', 'tp'), split_axis=0, concat_axis=0, tiled=...  32.1 us
    all_to_all x1, blocking collectives, over_pick(): lax.all_to_all(array, 'resp', split_axis=0, concat_axis=0, tiled=True, ax...  19.9 us
    ppermute x6, starting transfers between devices, across(): return lax.ppermute(array, 'resp', [(at, at ^ flip) for at in range(64)])  16.3 us
    pallas_call x1, Pallas kernels, attend(): pl.pallas_call(attend_kernel, out_shape=(jax.ShapeDtypeStruct(resp_keys.s...  15.8 us
    ppermute x6, waiting for transfers between devices, across(): return lax.ppermute(array, 'resp', [(at, at ^ flip) for at in range(64)])  14.8 us
    pallas_call x1, Pallas kernels, outputs(): pl.pallas_call(outputs_kernel, out_shape=(shape, shape, jax.ShapeDtypeStr...  10.3 us
    all_to_all x1, waiting for transfers between devices, over_pick(): lax.all_to_all(array, 'resp', split_axis=0, concat_axis=0, tiled=True, ax...  5.46 us
    all_to_all x1, starting transfers between devices, over_pick(): lax.all_to_all(array, 'resp', split_axis=0, concat_axis=0, tiled=True, ax...  5.42 us
  transfers between devices with their start and end apart: 7, of which 5 were waited for; matrix products, arithmetic and copies ran while one was open for 0% of the time, Pallas kernels for 8%

profile of v3, /device:TPU:1, one launch (start us, length us, event | category | flops | bytes accessed | tf_op | source)
XLA Modules:
  0.0 125.8 jit_solution(8650244599416602092)
XLA Ops:
  0.6 1.5 %shard_map.127 = bf16[16,24,128]{2,1,0:T(8,128)(2,1)} custom-call(s32[4]{0:T(128)} %owner_hbm.1, bf16[16,1024]{1,0:T(8,128)(2,1)} %key_hbm.1, bf16[16,1024]{1,0:T(8,128)(2,1)} %value_hbm.1), custom_call_target="tpu_custom_call" | custom-call | tf_op jit(solution)/shard_map/pallas_call | solution.py:459
  2.1 0.0 copy-start
  2.1 0.0 copy-start.1
  2.1 0.0 copy-start.2
  2.1 0.0 copy-start.3
  2.1 18.2 %all_to_all.20.pieces_ref = bf16[16,24,128]{2,1,0:T(8,128)(2,1)S(1)} all-to-all(bf16[16,24,128]{2,1,0:T(8,128)(2,1)} %shard_map.127), channel_id=1, replica_groups={{0,5,10,15,32,37,42,47,64,69,74,79,96,101,106,111},{4,9,14,3,36,41,46,3..., dimensions={0} | all-to-all | bytes 196608 | tf_op jit(solution)/shard_map/all_to_all | solution.py:45
  20.4 6.8 %collective-permute-start.2 = (bf16[16,16,128]{2,1,0:T(8,128)(2,1)S(1)}, bf16[16,16,128]{2,1,0:T(8,128)(2,1)S(1)}, u32[]{:S(2)}, u32[]{:S(2)}) collective-permute-start(bf16[16,16,128]{2,1,0:T(8,128)(2,1)S(1)} %get-tuple-element.23.own_ref), channel_id=1, source_target_pairs={{0,144},{4,148},{8,152},{12,156},{16,128},{20,132},{24,136},{28,14... | collective-permute-start | bytes 196616 | tf_op jit(solution)/shard_map/ppermute | solution.py:65
  27.1 1.1 collective-permute-start.1
  28.2 0.3 collective-permute-start
  28.5 1.5 %collective-permute-done.2.third_ref = bf16[16,16,128]{2,1,0:T(8,128)(2,1)S(1)} collective-permute-done((bf16[16,16,128]{2,1,0:T(8,128)(2,1)S(1)}, bf16[16,16,128]{2,1,0:T(8,128)(2,1)S(1)}, u32[]{:S(2)}, u32[]{:S(2)}) %collective-permute-start.2) | collective-permute-done | bytes 65568 | tf_op jit(solution)/shard_map/ppermute | solution.py:65
  30.0 4.9 %collective-permute-done.1.second_ref = bf16[16,16,128]{2,1,0:T(8,128)(2,1)S(1)} collective-permute-done((bf16[16,16,128]{2,1,0:T(8,128)(2,1)S(1)}, bf16[16,16,128]{2,1,0:T(8,128)(2,1)S(1)}, u32[]{:S(2)}, u32[]{:S(2)}) %collective-permute-start.1) | collective-permute-done | bytes 65568 | tf_op jit(solution)/shard_map/ppermute | solution.py:65
  34.9 0.0 collective-permute-done.first_ref
  34.9 1.8 %shard_map.129 = bf16[16,4,64,128]{3,2,1,0:T(8,128)(2,1)S(1)} custom-call(s32[16,128]{1,0:T(8,128)S(1)} %get-tuple-element.22.owner_ref, bf16[16,16,128]{2,1,0:T(8,128)(2,1)S(1)} %get-tuple-element.23.own_ref, bf16[16,16,128]{2,1,0:T(8,128)(2,1)S(1)} %collective-permute-done.first_ref, bf16[16,16,128]{2,1,0:T(8,128)(2,1)S(1)} %collective-permute-done.1.second_ref, ...), custom_call_target="tpu_custom_call" | custom-call | tf_op jit(solution)/shard_map/pallas_call | solution.py:459
  36.7 19.9 %all_to_all.21 = bf16[16,4,64,128]{3,2,1,0:T(8,128)(2,1)S(1)} all-to-all(bf16[16,4,64,128]{3,2,1,0:T(8,128)(2,1)S(1)} %shard_map.129), channel_id=1, replica_groups={{0,4,8,12,32,36,40,44,64,68,72,76,96,100,104,108},{16,20,24,28,48,52,56..., dimensions={0} | all-to-all | bytes 2097152 | tf_op jit(solution)/shard_map/all_to_all | solution.py:56
  56.6 0.0 copy-done
  56.6 0.0 copy-done.1
  56.6 0.0 copy-done.2
  56.6 0.0 copy-done.3
  56.6 15.8 %shard_map.130 = (bf16[640,256]{1,0:T(8,128)(2,1)}, bf16[640,256]{1,0:T(8,128)(2,1)}, bf16[2,2,4,4,64,128]{5,4,3,2,1,0:T(8,128)(2,1)}, bf16[4,2,5,416,256]{4,3,2,1,0:T(8,128)(2,1)}, bf16[4,2,5,416,256]{4,3,2,1,0:T(8,128)(2,1)}) custom-call(s32[4]{0:T(128)S(1)} %copy-done.2, bf16[640,2048]{1,0:T(8,128)(2,1)S(1)} %copy-done.3, bf16[640,2048]{1,0:T(8,128)(2,1)} %grad_ref.1, ...), custom_call_target="tpu_custom_call" | custom-call | flops 8724152320 | bytes 5242880 | tf_op jit(solution)/shard_map/pallas_call | solution.py:391
  72.4 5.4 %all-to-all-start.2 = ((bf16[16,4,64,128]{3,2,1,0:T(8,128)(2,1)}), bf16[16,4,64,128]{3,2,1,0:T(8,128)(2,1)S(1)}, u32[]{:S(2)}, u32[]{:S(2)}) async-start(bf16[16,4,64,128]{3,2,1,0:T(8,128)(2,1)} %bitcast.1), calls=%async_computation.2 | async-start | bytes 2097152 | tf_op jit(solution)/shard_map/all_to_all | solution.py:56
  77.8 10.3 %shard_map.131 = (bf16[640,2048]{1,0:T(8,128)(2,1)}, bf16[640,2048]{1,0:T(8,128)(2,1)}, s32[8,128]{1,0:T(8,128)S(1)}) custom-call(s32[4]{0:T(128)S(1)} %copy-done.2, bf16[640,256]{1,0:T(8,128)(2,1)S(1)} %copy-done, bf16[640,256]{1,0:T(8,128)(2,1)S(1)} %copy-done.1, bf16[2,2,4,4,64,128]{5,4,3,2,1,0:T(8,128)(2,1)S(1)} %bitcast.3, ...), custom_call_target="tpu_custom_call" | custom-call | flops 4362076160 | bytes 22282240 | tf_op jit(solution)/shard_map/pallas_call | solution.py:432
  88.1 5.5 %all-to-all-done.2.terms_ref = bf16[16,4,64,128]{3,2,1,0:T(8,128)(2,1)S(1)} async-done(((bf16[16,4,64,128]{3,2,1,0:T(8,128)(2,1)}), bf16[16,4,64,128]{3,2,1,0:T(8,128)(2,1)S(1)}, u32[]{:S(2)}, u32[]{:S(2)}) %all-to-all-start.2) | async-done | bytes 1048608 | tf_op jit(solution)/shard_map/all_to_all | solution.py:56
  93.6 1.0 shard_map.132
  94.6 2.0 %collective-permute-start.3 = (bf16[16,16,128]{2,1,0:T(8,128)(2,1)S(1)}, bf16[16,16,128]{2,1,0:T(8,128)(2,1)S(1)}, u32[]{:S(2)}, u32[]{:S(2)}) collective-permute-start(bf16[16,16,128]{2,1,0:T(8,128)(2,1)S(1)} %get-tuple-element.33), channel_id=1, source_target_pairs={{0,16},{4,20},{8,24},{12,28},{16,0},{20,4},{24,8},{28,12},{32,48},... | collective-permute-start | bytes 196616 | tf_op jit(solution)/shard_map/ppermute | solution.py:65
  96.6 5.0 %collective-permute-start.4 = (bf16[16,16,128]{2,1,0:T(8,128)(2,1)S(1)}, bf16[16,16,128]{2,1,0:T(8,128)(2,1)S(1)}, u32[]{:S(2)}, u32[]{:S(2)}) collective-permute-start(bf16[16,16,128]{2,1,0:T(8,128)(2,1)S(1)} %get-tuple-element.34), channel_id=1, source_target_pairs={{0,128},{4,132},{8,136},{12,140},{16,144},{20,148},{24,152},{28,15... | collective-permute-start | bytes 196616 | tf_op jit(solution)/shard_map/ppermute | solution.py:65
  101.6 1.1 collective-permute-start.5
  102.7 0.0 collective-permute-done.3.first_ref
  102.7 1.0 collective-permute-done.4.second_ref
  103.7 7.5 %collective-permute-done.5.third_ref = bf16[16,16,128]{2,1,0:T(8,128)(2,1)S(1)} collective-permute-done((bf16[16,16,128]{2,1,0:T(8,128)(2,1)S(1)}, bf16[16,16,128]{2,1,0:T(8,128)(2,1)S(1)}, u32[]{:S(2)}, u32[]{:S(2)}) %collective-permute-start.5) | collective-permute-done | bytes 65568 | tf_op jit(solution)/shard_map/ppermute | solution.py:65
  111.2 13.9 %all_to_all.22.sums_ref = bf16[16,16,128]{2,1,0:T(8,128)(2,1)S(1)} all-to-all(bf16[16,16,128]{2,1,0:T(8,128)(2,1)S(1)} %shard_map.133), channel_id=1, replica_groups={{0,5,10,15,32,37,42,47,64,69,74,79,96,101,106,111},{4,9,14,3,36,41,46,3..., dimensions={0} | all-to-all | bytes 131072 | tf_op jit(solution)/shard_map/all_to_all | solution.py:45
  125.1 0.6 shard_map.134
  (2 shorter events, 0.0 us)
Async XLA Ops:
  2.1 54.5 %copy-start = (bf16[640,256]{1,0:T(8,128)(2,1)S(1)}, bf16[640,256]{1,0:T(8,128)(2,1)}, u32[]{:S(2)}) copy-start(bf16[640,256]{1,0:T(8,128)(2,1)} %key_ref.3) | copy-start | bytes 983044
  2.1 54.5 %copy-start.1 = (bf16[640,256]{1,0:T(8,128)(2,1)S(1)}, bf16[640,256]{1,0:T(8,128)(2,1)}, u32[]{:S(2)}) copy-start(bf16[640,256]{1,0:T(8,128)(2,1)} %value_ref.3) | copy-start | bytes 983044
  2.1 54.5 %copy-start.2 = (s32[4]{0:T(128)S(1)}, s32[4]{0:T(128)}, u32[]{:S(2)}) copy-start(s32[4]{0:T(128)} %length_ref.3) | copy-start | bytes 52
  2.1 54.5 %copy-start.3 = (bf16[640,2048]{1,0:T(8,128)(2,1)S(1)}, bf16[640,2048]{1,0:T(8,128)(2,1)}, u32[]{:S(2)}) copy-start(bf16[640,2048]{1,0:T(8,128)(2,1)} %query_ref.1) | copy-start | bytes 7864324
  20.4 9.6 %collective-permute-start.2 = (bf16[16,16,128]{2,1,0:T(8,128)(2,1)S(1)}, bf16[16,16,128]{2,1,0:T(8,128)(2,1)S(1)}, u32[]{:S(2)}, u32[]{:S(2)}) collective-permute-start(bf16[16,16,128]{2,1,0:T(8,128)(2,1)S(1)} %get-tuple-element.23.own_ref), channel_id=1, source_target_pairs={{0,144},{4,148},{8,152},{12,156},{16,128},{20,132},{24,136},{28,14... | collective-permute-start | bytes 196616 | tf_op jit(solution)/shard_map/ppermute | solution.py:65
  27.1 7.7 %collective-permute-start.1 = (bf16[16,16,128]{2,1,0:T(8,128)(2,1)S(1)}, bf16[16,16,128]{2,1,0:T(8,128)(2,1)S(1)}, u32[]{:S(2)}, u32[]{:S(2)}) collective-permute-start(bf16[16,16,128]{2,1,0:T(8,128)(2,1)S(1)} %get-tuple-element.23.own_ref), channel_id=1, source_target_pairs={{0,128},{4,132},{8,136},{12,140},{16,144},{20,148},{24,152},{28,15... | collective-permute-start | bytes 196616 | tf_op jit(solution)/shard_map/ppermute | solution.py:65
  28.2 6.7 %collective-permute-start = (bf16[16,16,128]{2,1,0:T(8,128)(2,1)S(1)}, bf16[16,16,128]{2,1,0:T(8,128)(2,1)S(1)}, u32[]{:S(2)}, u32[]{:S(2)}) collective-permute-start(bf16[16,16,128]{2,1,0:T(8,128)(2,1)S(1)} %get-tuple-element.23.own_ref), channel_id=1, source_target_pairs={{0,16},{4,20},{8,24},{12,28},{16,0},{20,4},{24,8},{28,12},{32,48},... | collective-permute-start | bytes 196616 | tf_op jit(solution)/shard_map/ppermute | solution.py:65
  72.4 21.2 %all-to-all-start.2 = ((bf16[16,4,64,128]{3,2,1,0:T(8,128)(2,1)}), bf16[16,4,64,128]{3,2,1,0:T(8,128)(2,1)S(1)}, u32[]{:S(2)}, u32[]{:S(2)}) async-start(bf16[16,4,64,128]{3,2,1,0:T(8,128)(2,1)} %bitcast.1), calls=%async_computation.2 | async-start | bytes 2097152 | tf_op jit(solution)/shard_map/all_to_all | solution.py:56
  94.6 8.2 %collective-permute-start.3 = (bf16[16,16,128]{2,1,0:T(8,128)(2,1)S(1)}, bf16[16,16,128]{2,1,0:T(8,128)(2,1)S(1)}, u32[]{:S(2)}, u32[]{:S(2)}) collective-permute-start(bf16[16,16,128]{2,1,0:T(8,128)(2,1)S(1)} %get-tuple-element.33), channel_id=1, source_target_pairs={{0,16},{4,20},{8,24},{12,28},{16,0},{20,4},{24,8},{28,12},{32,48},... | collective-permute-start | bytes 196616 | tf_op jit(solution)/shard_map/ppermute | solution.py:65
  96.6 7.1 %collective-permute-start.4 = (bf16[16,16,128]{2,1,0:T(8,128)(2,1)S(1)}, bf16[16,16,128]{2,1,0:T(8,128)(2,1)S(1)}, u32[]{:S(2)}, u32[]{:S(2)}) collective-permute-start(bf16[16,16,128]{2,1,0:T(8,128)(2,1)S(1)} %get-tuple-element.34), channel_id=1, source_target_pairs={{0,128},{4,132},{8,136},{12,140},{16,144},{20,148},{24,152},{28,15... | collective-permute-start | bytes 196616 | tf_op jit(solution)/shard_map/ppermute | solution.py:65
  101.6 9.6 %collective-permute-start.5 = (bf16[16,16,128]{2,1,0:T(8,128)(2,1)S(1)}, bf16[16,16,128]{2,1,0:T(8,128)(2,1)S(1)}, u32[]{:S(2)}, u32[]{:S(2)}) collective-permute-start(bf16[16,16,128]{2,1,0:T(8,128)(2,1)S(1)} %get-tuple-element.35), channel_id=1, source_target_pairs={{0,144},{4,148},{8,152},{12,156},{16,128},{20,132},{24,136},{28,14... | collective-permute-start | bytes 196616 | tf_op jit(solution)/shard_map/ppermute | solution.py:65

commit v4 on v2

--- a/solution.py
+++ b/solution.py
@@ -20,7 +20,9 @@
 CHUNKS = 5
 SENT = TILE + 8
 LOG2E = 1.4426950408889634
-LARGE = pltpu.CompilerParams(vmem_limit_bytes=48 * 1024 * 1024)
+LARGE = pltpu.CompilerParams(vmem_limit_bytes=24 * 1024 * 1024)
+FIRST = pltpu.CompilerParams(vmem_limit_bytes=(64 * 1024 - 64) * 1024)
+STACK = pltpu.CompilerParams(vmem_limit_bytes=55 * 1024 * 1024)
 SMALL = pltpu.CompilerParams(vmem_limit_bytes=16 * 1024 * 1024)
 
 STORE_GROUPS = [
@@ -158,10 +160,20 @@
             blank(first, last)
 
 
+def stack_kernel(query_ref, grad_ref, stacked_query, stacked_grad):
+    response = pl.program_id(0)
+    for chunk in range(CHUNKS):
+        rows = slice(chunk * ROWS, (chunk + 1) * ROWS)
+        for head in range(KV_LANE):
+            for part, column in heads(head):
+                stacked_query[response, head, chunk, part] = query_ref[rows, column]
+                stacked_grad[response, head, chunk, part] = grad_ref[rows, column]
+
+
 def attend_kernel(
     length_ref,
-    query_ref,
-    grad_ref,
+    stacked_query,
+    stacked_grad,
     key_ref,
     value_ref,
     prompt_ref,
@@ -172,15 +184,14 @@
     score_grad_ref,
     keys,
     values,
-    stacked_query,
-    stacked_grad,
     scores,
     prob_grads,
     key_total,
     value_total,
 ):
-    length = length_ref[pl.program_id(0)]
-    span = query_ref.shape[0]
+    response = pl.program_id(0)
+    length = length_ref[response]
+    span = key_ref.shape[0]
     scale = HD**-0.5
     wide = PER_GROUP * ROWS
     for head in range(KV_LANE):
@@ -192,12 +203,9 @@
         count = LP + first + ROWS
         lane = lax.broadcasted_iota(jnp.int32, (1, wide), 1) % ROWS
         causal = lax.broadcasted_iota(jnp.int32, (ROWS, 1), 0) <= lane
-        for part, column in heads(head):
-            stacked_query[slot, part] = query_ref[first : first + ROWS, column]
-            stacked_grad[slot, part] = grad_ref[first : first + ROWS, column]
         raw = lax.dot_general(
             keys[head, :count],
-            stacked_query[slot],
+            stacked_query[response, head, first // ROWS],
             (((1,), (1,)), ((), ())),
             preferred_element_type=jnp.float32,
         )
@@ -208,7 +216,7 @@
         top = jnp.maximum(top, jnp.max(tail.reshape(-1, 8, wide), axis=0))
         prob_grads[slot, :count] = lax.dot_general(
             values[head, :count],
-            stacked_grad[slot],
+            stacked_grad[response, head, first // ROWS],
             (((1,), (1,)), ((), ())),
             preferred_element_type=jnp.float32,
         )
@@ -221,21 +229,19 @@
         live = first + lane < length
         blocks = [slice(at, at + ROWS) for at in range(0, count, ROWS)]
         total = jnp.zeros((8, wide), jnp.float32)
+        moved = jnp.zeros((8, wide), jnp.float32)
         for block in blocks:
             weights = jnp.exp2(scores[slot, block] * (scale * LOG2E) - largest)
             scores[slot, block] = weights
             total = total + jnp.sum(weights.reshape(-1, 8, wide), axis=0)
+            terms = weights * prob_grads[slot, block]
+            moved = moved + jnp.sum(terms.reshape(-1, 8, wide), axis=0)
         inverse = jnp.where(live, 1.0 / jnp.sum(total, axis=0, keepdims=True), 0.0)
-        total = jnp.zeros((8, wide), jnp.float32)
+        delta = jnp.sum(moved, axis=0, keepdims=True) * inverse
         for block in blocks:
             probability = scores[slot, block] * inverse
-            probability_ref[0, head, chunk, block] = probability.astype(jnp.bfloat16)
-            terms = probability * prob_grads[slot, block]
-            total = total + jnp.sum(terms.reshape(-1, 8, wide), axis=0)
-        delta = jnp.sum(total, axis=0, keepdims=True)
-        for block in blocks:
-            probability = scores[slot, block] * inverse
-            score_grad_ref[0, head, chunk, block] = (
+            probability_ref[response, head, chunk, block] = probability.astype(jnp.bfloat16)
+            score_grad_ref[response, head, chunk, block] = (
                 probability * (prob_grads[slot, block] - delta)
             ).astype(jnp.bfloat16)
 
@@ -247,8 +253,8 @@
             (key_total, score_grad_ref, stacked_query),
         ):
             terms = jnp.dot(
-                left_ref[0, head, chunk, :count],
-                stacked[slot],
+                left_ref[response, head, chunk, :count],
+                stacked[response, head, chunk],
                 preferred_element_type=jnp.float32,
             )
             if first == 0:
@@ -296,7 +302,8 @@
     keys_t,
     values_t,
 ):
-    length = length_ref[pl.program_id(0)]
+    response = pl.program_id(0)
+    length = length_ref[response]
     span = out_ref.shape[0]
     scale = HD**-0.5
     for head in range(KV_LANE):
@@ -314,12 +321,12 @@
             for head in range(KV_LANE):
                 output = jnp.dot(
                     values_t[head, :, :count],
-                    probability_ref[0, head, chunk, :count],
+                    probability_ref[response, head, chunk, :count],
                     preferred_element_type=jnp.float32,
                 )
                 query_grad = jnp.dot(
                     keys_t[head, :, :count],
-                    score_grad_ref[0, head, chunk, :count],
+                    score_grad_ref[response, head, chunk, :count],
                     preferred_element_type=jnp.float32,
                 )
                 output = output.astype(jnp.bfloat16).T
@@ -338,27 +345,43 @@
 
 
 def specs(span, wide, narrow):
-    both = LP + span
-    stacked = PER_GROUP * ROWS
     return dict(
         wide=pl.BlockSpec((span, wide), lambda i, length: (i, 0)),
         narrow=pl.BlockSpec((span, narrow), lambda i, length: (i, 0)),
         prompt=pl.BlockSpec(
             (2, KV_LANE, GROUPS, 1, SLICE, HD), lambda i, length: (0, 0, 0, i, 0, 0)
         ),
-        kept=pl.BlockSpec(
-            (1, KV_LANE, CHUNKS, both, stacked), lambda i, length: (i, 0, 0, 0, 0)
-        ),
-    )
-
-
-def attend(lengths, queries, out_grad, resp_keys, resp_values, prompt_rows):
+        kept=pl.BlockSpec(memory_space=pltpu.VMEM),
+    )
+
+
+def stack(queries, out_grad, count):
+    span = queries.shape[0] // count
+    shape = jax.ShapeDtypeStruct(
+        (count, KV_LANE, CHUNKS, PER_GROUP * ROWS, HD), jnp.bfloat16
+    )
+    wide = pl.BlockSpec((span, queries.shape[1]), lambda i: (i, 0))
+    return pl.pallas_call(
+        stack_kernel,
+        out_shape=(shape, shape),
+        grid=(count,),
+        in_specs=[wide, wide],
+        out_specs=[pl.BlockSpec(memory_space=pltpu.VMEM)] * 2,
+        compiler_params=STACK,
+        cost_estimate=pl.CostEstimate(
+            flops=0, bytes_accessed=8 * queries.size, transcendentals=0
+        ),
+    )(queries, out_grad)
+
+
+def attend(lengths, stacked_query, stacked_grad, resp_keys, resp_values, prompt_rows):
     count = lengths.shape[0]
-    span = queries.shape[0] // count
+    span = resp_keys.shape[0] // count
     both = LP + span
     streams = 2 * KV_LANE
     stacked = PER_GROUP * ROWS
-    spec = specs(span, queries.shape[1], resp_keys.shape[1])
+    elements = stacked_query.size
+    spec = specs(span, stacked_query.size // resp_keys.shape[0], resp_keys.shape[1])
     kept = jax.ShapeDtypeStruct((count, KV_LANE, CHUNKS, both, stacked), jnp.bfloat16)
     return pl.pallas_call(
         attend_kernel,
@@ -372,13 +395,11 @@
         grid_spec=pltpu.PrefetchScalarGridSpec(
             num_scalar_prefetch=1,
             grid=(count,),
-            in_specs=[spec[name] for name in ("wide", "wide", "narrow", "narrow", "prompt")],
+            in_specs=[spec[name] for name in ("kept", "kept", "narrow", "narrow", "prompt")],
             out_specs=[spec[name] for name in ("narrow", "narrow", "prompt", "kept", "kept")],
             scratch_shapes=[
                 pltpu.VMEM((KV_LANE, both, HD), jnp.bfloat16),
                 pltpu.VMEM((KV_LANE, both, HD), jnp.bfloat16),
-                pltpu.VMEM((streams, stacked, HD), jnp.bfloat16),
-                pltpu.VMEM((streams, stacked, HD), jnp.bfloat16),
                 pltpu.VMEM((streams, both, stacked), jnp.float32),
                 pltpu.VMEM((streams, both, stacked), jnp.float32),
                 pltpu.VMEM((KV_LANE, both, HD), jnp.float32),
@@ -387,11 +408,11 @@
         ),
         compiler_params=LARGE,
         cost_estimate=pl.CostEstimate(
-            flops=16 * queries.size * both,
-            bytes_accessed=4 * queries.size,
-            transcendentals=queries.size * both // HD,
-        ),
-    )(lengths, queries, out_grad, resp_keys, resp_values, prompt_rows)
+            flops=16 * elements * both,
+            bytes_accessed=4 * elements,
+            transcendentals=elements * both // HD,
+        ),
+    )(lengths, stacked_query, stacked_grad, resp_keys, resp_values, prompt_rows)
 
 
 def outputs(lengths, resp_keys, resp_values, prompt_rows, probability, score_grad, wide):
@@ -427,12 +448,12 @@
     )(lengths, resp_keys, resp_values, prompt_rows, probability, score_grad)
 
 
-def whole(kernel, out_shape, spaces, *operands, **more):
+def whole(kernel, out_shape, spaces, *operands, params=SMALL, **more):
     return pl.pallas_call(
         kernel,
         out_shape=out_shape,
         in_specs=[pl.BlockSpec(memory_space=space) for space in spaces],
-        compiler_params=SMALL,
+        compiler_params=params,
         **more,
     )(*operands)
 
@@ -452,6 +473,7 @@
             prompt_of,
             prompt_keys,
             prompt_values,
+            params=FIRST,
             scratch_shapes=[
                 pltpu.SMEM(prompt_of.shape, jnp.int32),
                 pltpu.VMEM(prompt_keys.shape, jnp.bfloat16),
@@ -468,8 +490,9 @@
         scratch_shapes=[pltpu.SMEM((MEMBERS, HD), jnp.int32), pltpu.SemaphoreType.DMA],
     )
     prompt_rows = over_pick(picked).reshape(2, KV_LANE, GROUPS, LOCAL, SLICE, HD)
+    stacked = stack(queries, out_grad, lengths.shape[0])
     resp_key_grad, resp_value_grad, terms, probability, score_grad = attend(
-        lengths, queries, out_grad, resp_keys, resp_values, prompt_rows
+        lengths, *stacked, resp_keys, resp_values, prompt_rows
     )
     terms = over_pick(terms.reshape(MEMBERS, LOCAL, SLICE, HD))
     attn_out, query_grad, token = outputs(

time: 116 us -> 125 us (1.078); the launches traced: 114 us -> 125 us
  blocking collectives: 71.1 us -> 52 us
  local copies, waits for them, and re-layouts: 2.24 us -> 16.9 us
  starting transfers between devices: 4.6 us -> 18.2 us
  waiting for transfers between devices: 4.38 us -> 13.5 us
  Pallas kernels: 31.1 us -> 23.4 us
    all_to_all x1 -> x0, blocking collectives: 21.1 us -> none  [over_pick(): lax.all_to_all(array, 'resp', split_axis=0, concat_axis=0, tiled=True, ax...]
    unnamed x14 -> x18, local copies, waits for them, and re-layouts: 2.24 us -> 16.9 us
    all_to_all x1 -> x2, starting transfers between devices: 4.6 us -> 18.2 us  [over_pick(): lax.all_to_all(array, 'resp', split_axis=0, concat_axis=0, tiled=True, ax...]
    pallas_call x1, Pallas kernels: 16.6 us -> 7.11 us  [attend(): pl.pallas_call(attend_kernel, out_shape=(jax.ShapeDtypeStruct(resp_keys.s...]
    all_to_all x1 -> x2, waiting for transfers between devices: 4.38 us -> 13.5 us  [over_pick(): lax.all_to_all(array, 'resp', split_axis=0, concat_axis=0, tiled=True, ax...]
    pallas_call x1, Pallas kernels: 11.3 us -> 5.23 us  [outputs(): pl.pallas_call(outputs_kernel, out_shape=(shape, shape, jax.ShapeDtypeStr...]
    pallas_call x0 -> x1, Pallas kernels: none -> 5.94 us  [stack(): pl.pallas_call(stack_kernel, out_shape=(shape, shape), grid=(count,), in_...]
    all_to_all x2, blocking collectives: 50 us -> 52 us  [over_store(): lax.all_to_all(array, ('resp', 'tp'), split_axis=0, concat_axis=0, tiled=...]
  transfers between devices with their start and end apart: 1 -> 2, of which waited for: 1 -> 2; matrix products, arithmetic and copies ran while one was open for 0% -> 0% of each run, Pallas kernels for 10% -> 9%
where the time goes in v4:
time: 125 us
  blocking collectives  52 us (42%)
  Pallas kernels  23.4 us (19%)
  starting transfers between devices  18.2 us (15%)
  local copies, waits for them, and re-layouts  16.9 us (14%)
  waiting for transfers between devices  13.5 us (11%)
    all_to_all x2, blocking collectives, over_store(): lax.all_to_all(array, ('resp', 'tp'), split_axis=0, concat_axis=0, tiled=...  52 us
    all_to_all x2, starting transfers between devices, over_pick(): lax.all_to_all(array, 'resp', split_axis=0, concat_axis=0, tiled=True, ax...  18.2 us
    unnamed x18, local copies, waits for them, and re-layouts  16.9 us
    all_to_all x2, waiting for transfers between devices, over_pick(): lax.all_to_all(array, 'resp', split_axis=0, concat_axis=0, tiled=True, ax...  13.5 us
    pallas_call x1, Pallas kernels, attend(): pl.pallas_call(attend_kernel, out_shape=(jax.ShapeDtypeStruct(resp_keys.s...  7.11 us
    pallas_call x1, Pallas kernels, stack(): pl.pallas_call(stack_kernel, out_shape=(shape, shape), grid=(count,), in_...  5.94 us
    pallas_call x1, Pallas kernels, outputs(): pl.pallas_call(outputs_kernel, out_shape=(shape, shape, jax.ShapeDtypeStr...  5.23 us
    pallas_call x4, Pallas kernels, whole(): pl.pallas_call(kernel, out_shape=out_shape, in_specs=[pl.BlockSpec(memory...  5.14 us
  transfers between devices with their start and end apart: 2, of which 2 were waited for; matrix products, arithmetic and copies ran while one was open for 0% of the time, Pallas kernels for 9%

profile of v4, /device:TPU:1, one launch (start us, length us, event | category | flops | bytes accessed | tf_op | source)
XLA Modules:
  0.0 124.6 jit_solution(9452646251896387904)
XLA Ops:
  0.6 1.6 %shard_map.127 = bf16[64,24,128]{2,1,0:T(8,128)(2,1)} custom-call(s32[4]{0:T(128)} %owner_hbm.1, bf16[16,1024]{1,0:T(8,128)(2,1)} %key_hbm.1, bf16[16,1024]{1,0:T(8,128)(2,1)} %value_hbm.1), custom_call_target="tpu_custom_call" | custom-call | tf_op jit(solution)/shard_map/pallas_call | solution.py:452
  2.2 30.8 %all_to_all.20.pieces_ref = bf16[64,24,128]{2,1,0:T(8,128)(2,1)S(1)} all-to-all(bf16[64,24,128]{2,1,0:T(8,128)(2,1)} %shard_map.127), channel_id=1, replica_groups={{0,5,10,15,16,21,26,31,32,37,42,47,48,53,58,63,64,69,74,79,80,85,90,95,..., dimensions={0} | all-to-all | bytes 786432 | tf_op jit(solution)/shard_map/all_to_all | solution.py:40
  33.0 1.7 %shard_map.128 = (bf16[16,4,64,128]{3,2,1,0:T(8,128)(2,1)}, s32[16,128]{1,0:T(8,128)S(1)}) custom-call(bf16[64,24,128]{2,1,0:T(8,128)(2,1)S(1)} %all_to_all.20.pieces_ref), custom_call_target="tpu_custom_call" | custom-call | tf_op jit(solution)/shard_map/pallas_call | solution.py:452
  34.8 6.2 %all-to-all-start.1 = ((bf16[16,4,64,128]{3,2,1,0:T(8,128)(2,1)}), bf16[16,4,64,128]{3,2,1,0:T(8,128)(2,1)S(1)}, u32[]{:S(2)}, u32[]{:S(2)}) async-start(bf16[16,4,64,128]{3,2,1,0:T(8,128)(2,1)} %get-tuple-element.20), calls=%async_computation.1 | async-start | bytes 2097152 | tf_op jit(solution)/shard_map/all_to_all | solution.py:51
  41.0 0.0 copy-start.4
  41.0 0.0 copy-start.5
  41.0 0.0 copy-start.6
  41.0 5.9 %shard_map.129 = (bf16[4,2,5,256,128]{4,3,2,1,0:T(8,128)(2,1)}, bf16[4,2,5,256,128]{4,3,2,1,0:T(8,128)(2,1)}) custom-call(bf16[640,2048]{1,0:T(8,128)(2,1)} %query_ref.1, bf16[640,2048]{1,0:T(8,128)(2,1)} %grad_ref.1), custom_call_target="tpu_custom_call" | custom-call | bytes 10485760 | tf_op jit(solution)/shard_map/pallas_call | solution.py:364
  47.0 9.8 %all-to-all-done.1 = bf16[16,4,64,128]{3,2,1,0:T(8,128)(2,1)S(1)} async-done(((bf16[16,4,64,128]{3,2,1,0:T(8,128)(2,1)}), bf16[16,4,64,128]{3,2,1,0:T(8,128)(2,1)S(1)}, u32[]{:S(2)}, u32[]{:S(2)}) %all-to-all-start.1) | async-done | bytes 1048608 | tf_op jit(solution)/shard_map/all_to_all | solution.py:51
  56.8 0.0 copy-done.4
  56.8 0.0 copy-done.5
  56.8 0.0 copy-done.6
  56.8 0.0 copy-start.7
  56.8 1.7 %copy-done.7 = bf16[4,2,5,256,128]{4,3,2,1,0:T(8,128)(2,1)S(1)} copy-done((bf16[4,2,5,256,128]{4,3,2,1,0:T(8,128)(2,1)S(1)}, bf16[4,2,5,256,128]{4,3,2,1,0:T(8,128)(2,1)}, u32[]{:S(2)}) %copy-start.7) | copy-done | bytes 2621464
  58.5 0.0 copy-start.8
  58.5 1.7 %copy-done.8 = bf16[4,2,5,256,128]{4,3,2,1,0:T(8,128)(2,1)S(1)} copy-done((bf16[4,2,5,256,128]{4,3,2,1,0:T(8,128)(2,1)S(1)}, bf16[4,2,5,256,128]{4,3,2,1,0:T(8,128)(2,1)}, u32[]{:S(2)}) %copy-start.8) | copy-done | bytes 2621464
  60.3 7.1 %shard_map.130 = (bf16[640,256]{1,0:T(8,128)(2,1)}, bf16[640,256]{1,0:T(8,128)(2,1)}, bf16[2,2,4,4,64,128]{5,4,3,2,1,0:T(8,128)(2,1)}, bf16[4,2,5,416,256]{4,3,2...) custom-call(s32[4]{0:T(128)S(1)} %copy-done.6, bf16[4,2,5,256,128]{4,3,2,1,0:T(8,128)(2,1)S(1)} %copy-done.7, ...), custom_call_target="tpu_custom_call" | custom-call | flops 8724152320 | bytes 5242880 | tf_op jit(solution)/shard_map/pallas_call | solution.py:386
  67.4 0.0 copy-start
  67.4 3.3 %copy-done = bf16[4,2,5,416,256]{4,3,2,1,0:T(8,128)(2,1)} copy-done((bf16[4,2,5,416,256]{4,3,2,1,0:T(8,128)(2,1)}, bf16[4,2,5,416,256]{4,3,2,1,0:T(8,128)(2,1)S(1)}, u32[]{:S(2)}) %copy-start) | copy-done | bytes 8519704
  70.7 0.0 copy-start.2
  70.7 3.3 %copy-done.2 = bf16[4,2,5,416,256]{4,3,2,1,0:T(8,128)(2,1)} copy-done((bf16[4,2,5,416,256]{4,3,2,1,0:T(8,128)(2,1)}, bf16[4,2,5,416,256]{4,3,2,1,0:T(8,128)(2,1)S(1)}, u32[]{:S(2)}) %copy-start.2) | copy-done | bytes 8519704
  74.0 12.0 %all-to-all-start.2 = ((bf16[16,4,64,128]{3,2,1,0:T(8,128)(2,1)}), bf16[16,4,64,128]{3,2,1,0:T(8,128)(2,1)S(1)}, u32[]{:S(2)}, u32[]{:S(2)}) async-start(bf16[16,4,64,128]{3,2,1,0:T(8,128)(2,1)} %bitcast.1), calls=%async_computation.2 | async-start | bytes 2097152 | tf_op jit(solution)/shard_map/all_to_all | solution.py:51
  86.0 0.0 copy-start.1
  86.0 3.4 %copy-done.1 = bf16[4,2,5,416,256]{4,3,2,1,0:T(8,128)(2,1)S(1)} copy-done((bf16[4,2,5,416,256]{4,3,2,1,0:T(8,128)(2,1)S(1)}, bf16[4,2,5,416,256]{4,3,2,1,0:T(8,128)(2,1)}, u32[]{:S(2)}) %copy-start.1) | copy-done | bytes 8519704
  89.4 0.0 copy-start.3
  89.4 3.4 %copy-done.3 = bf16[4,2,5,416,256]{4,3,2,1,0:T(8,128)(2,1)S(1)} copy-done((bf16[4,2,5,416,256]{4,3,2,1,0:T(8,128)(2,1)S(1)}, bf16[4,2,5,416,256]{4,3,2,1,0:T(8,128)(2,1)}, u32[]{:S(2)}) %copy-start.3) | copy-done | bytes 8519704
  92.8 5.2 %shard_map.131 = (bf16[640,2048]{1,0:T(8,128)(2,1)}, bf16[640,2048]{1,0:T(8,128)(2,1)}, s32[8,128]{1,0:T(8,128)S(1)}) custom-call(s32[4]{0:T(128)S(1)} %copy-done.6, bf16[640,256]{1,0:T(8,128)(2,1)S(1)} %copy-done.4, bf16[640,256]{1,0:T(8,128)(2,1)S(1)} %copy-done.5, bf16[2,2,4,4,64,128]{5,4,3,2,1,0:T(8,128)(2,1)S(1)} %bitcast.3, ...), custom_call_target="tpu_custom_call" | custom-call | flops 4362076160 | bytes 22282240 | tf_op jit(solution)/shard_map/pallas_call | solution.py:425
  98.0 3.6 %all-to-all-done.2.terms_ref = bf16[16,4,64,128]{3,2,1,0:T(8,128)(2,1)S(1)} async-done(((bf16[16,4,64,128]{3,2,1,0:T(8,128)(2,1)}), bf16[16,4,64,128]{3,2,1,0:T(8,128)(2,1)S(1)}, u32[]{:S(2)}, u32[]{:S(2)}) %all-to-all-start.2) | async-done | bytes 1048608 | tf_op jit(solution)/shard_map/all_to_all | solution.py:51
  101.7 1.1 shard_map.132
  102.8 21.2 %all_to_all.21.sums_ref = bf16[64,16,128]{2,1,0:T(8,128)(2,1)S(1)} all-to-all(bf16[64,16,128]{2,1,0:T(8,128)(2,1)S(1)} %shard_map.132), channel_id=1, replica_groups={{0,5,10,15,16,21,26,31,32,37,42,47,48,53,58,63,64,69,74,79,80,85,90,95,..., dimensions={0} | all-to-all | bytes 524288 | tf_op jit(solution)/shard_map/all_to_all | solution.py:40
  124.0 0.7 shard_map.133
Async XLA Ops:
  34.8 22.0 %all-to-all-start.1 = ((bf16[16,4,64,128]{3,2,1,0:T(8,128)(2,1)}), bf16[16,4,64,128]{3,2,1,0:T(8,128)(2,1)S(1)}, u32[]{:S(2)}, u32[]{:S(2)}) async-start(bf16[16,4,64,128]{3,2,1,0:T(8,128)(2,1)} %get-tuple-element.20), calls=%async_computation.1 | async-start | bytes 2097152 | tf_op jit(solution)/shard_map/all_to_all | solution.py:51
  41.0 15.8 %copy-start.4 = (bf16[640,256]{1,0:T(8,128)(2,1)S(1)}, bf16[640,256]{1,0:T(8,128)(2,1)}, u32[]{:S(2)}) copy-start(bf16[640,256]{1,0:T(8,128)(2,1)} %key_ref.3) | copy-start | bytes 983044
  41.0 15.8 %copy-start.5 = (bf16[640,256]{1,0:T(8,128)(2,1)S(1)}, bf16[640,256]{1,0:T(8,128)(2,1)}, u32[]{:S(2)}) copy-start(bf16[640,256]{1,0:T(8,128)(2,1)} %value_ref.3) | copy-start | bytes 983044
  41.0 15.8 %copy-start.6 = (s32[4]{0:T(128)S(1)}, s32[4]{0:T(128)}, u32[]{:S(2)}) copy-start(s32[4]{0:T(128)} %length_ref.3) | copy-start | bytes 52
  56.8 1.7 %copy-start.7 = (bf16[4,2,5,256,128]{4,3,2,1,0:T(8,128)(2,1)S(1)}, bf16[4,2,5,256,128]{4,3,2,1,0:T(8,128)(2,1)}, u32[]{:S(2)}) copy-start(bf16[4,2,5,256,128]{4,3,2,1,0:T(8,128)(2,1)} %get-tuple-element.21.stacked_query) | copy-start | bytes 7864324
  58.5 1.7 %copy-start.8 = (bf16[4,2,5,256,128]{4,3,2,1,0:T(8,128)(2,1)S(1)}, bf16[4,2,5,256,128]{4,3,2,1,0:T(8,128)(2,1)}, u32[]{:S(2)}) copy-start(bf16[4,2,5,256,128]{4,3,2,1,0:T(8,128)(2,1)} %get-tuple-element.22.stacked_grad) | copy-start | bytes 7864324
  67.4 3.3 %copy-start = (bf16[4,2,5,416,256]{4,3,2,1,0:T(8,128)(2,1)}, bf16[4,2,5,416,256]{4,3,2,1,0:T(8,128)(2,1)S(1)}, u32[]{:S(2)}) copy-start(bf16[4,2,5,416,256]{4,3,2,1,0:T(8,128)(2,1)S(1)} %get-tuple-element.23.probability_ref) | copy-start | bytes 25559044
  70.7 3.3 %copy-start.2 = (bf16[4,2,5,416,256]{4,3,2,1,0:T(8,128)(2,1)}, bf16[4,2,5,416,256]{4,3,2,1,0:T(8,128)(2,1)S(1)}, u32[]{:S(2)}) copy-start(bf16[4,2,5,416,256]{4,3,2,1,0:T(8,128)(2,1)S(1)} %get-tuple-element.24.score_grad_ref) | copy-start | bytes 25559044
  74.0 27.7 %all-to-all-start.2 = ((bf16[16,4,64,128]{3,2,1,0:T(8,128)(2,1)}), bf16[16,4,64,128]{3,2,1,0:T(8,128)(2,1)S(1)}, u32[]{:S(2)}, u32[]{:S(2)}) async-start(bf16[16,4,64,128]{3,2,1,0:T(8,128)(2,1)} %bitcast.1), calls=%async_computation.2 | async-start | bytes 2097152 | tf_op jit(solution)/shard_map/all_to_all | solution.py:51
  86.0 3.4 %copy-start.1 = (bf16[4,2,5,416,256]{4,3,2,1,0:T(8,128)(2,1)S(1)}, bf16[4,2,5,416,256]{4,3,2,1,0:T(8,128)(2,1)}, u32[]{:S(2)}) copy-start(bf16[4,2,5,416,256]{4,3,2,1,0:T(8,128)(2,1)} %copy-done) | copy-start | bytes 25559044
  89.4 3.4 %copy-start.3 = (bf16[4,2,5,416,256]{4,3,2,1,0:T(8,128)(2,1)S(1)}, bf16[4,2,5,416,256]{4,3,2,1,0:T(8,128)(2,1)}, u32[]{:S(2)}) copy-start(bf16[4,2,5,416,256]{4,3,2,1,0:T(8,128)(2,1)} %copy-done.2) | copy-start | bytes 25559044

commit v5 on v4

--- a/solution.py
+++ b/solution.py
@@ -20,9 +20,10 @@
 CHUNKS = 5
 SENT = TILE + 8
 LOG2E = 1.4426950408889634
-LARGE = pltpu.CompilerParams(vmem_limit_bytes=24 * 1024 * 1024)
+LARGE = pltpu.CompilerParams(vmem_limit_bytes=44 * 1024 * 1024)
 FIRST = pltpu.CompilerParams(vmem_limit_bytes=(64 * 1024 - 64) * 1024)
-STACK = pltpu.CompilerParams(vmem_limit_bytes=55 * 1024 * 1024)
+OUTPUTS = pltpu.CompilerParams(vmem_limit_bytes=58 * 1024 * 1024)
+STACK = pltpu.CompilerParams(vmem_limit_bytes=24 * 1024 * 1024)
 SMALL = pltpu.CompilerParams(vmem_limit_bytes=16 * 1024 * 1024)
 
 STORE_GROUPS = [
@@ -160,6 +161,26 @@
             blank(first, last)
 
 
+def kept_copies(kept, held, sems, response, head, first, out):
+    chunk = first // ROWS
+    rows = pl.ds(0, LP + first + ROWS)
+    for at in range(2):
+        far = kept[at].at[response, head, chunk, rows]
+        near = held[at].at[response, head, chunk, rows]
+        source, target = (near, far) if out else (far, near)
+        yield pltpu.make_async_copy(source, target, sems.at[response, head, chunk, at])
+
+
+def each_live(length_ref, span, act):
+    for response in range(LOCAL):
+        for first in range(0, span, ROWS):
+
+            @pl.when(length_ref[response] > first)
+            def _():
+                for head in range(KV_LANE):
+                    act(response, head, first)
+
+
 def stack_kernel(query_ref, grad_ref, stacked_query, stacked_grad):
     response = pl.program_id(0)
     for chunk in range(CHUNKS):
@@ -180,15 +201,20 @@
     key_grad_ref,
     value_grad_ref,
     prompt_grad_ref,
-    probability_ref,
-    score_grad_ref,
+    probability_hbm,
+    score_grad_hbm,
     keys,
     values,
     scores,
     prob_grads,
+    probability_ref,
+    score_grad_ref,
     key_total,
     value_total,
+    sems,
 ):
+    kept = (probability_hbm, score_grad_hbm)
+    held = (probability_ref, score_grad_ref)
     response = pl.program_id(0)
     length = length_ref[response]
     span = key_ref.shape[0]
@@ -270,6 +296,8 @@
             if slot + 1 < len(streams):
                 largest[slot + 1] = score(slot + 1, *streams[slot + 1])
             soften(slot, *stream, largest[slot])
+            for copy in kept_copies(kept, held, sems, response, *stream, True):
+                copy.start()
             gather(slot, *stream)
 
     def blank(first, last):
@@ -288,24 +316,46 @@
         key_grad_ref[:, lanes] = key_terms[LP:]
         value_grad_ref[:, lanes] = value_terms[LP:]
 
+    def finish(*chunk):
+        for copy in kept_copies(kept, held, sems, *chunk, True):
+            copy.wait()
+
+    @pl.when(response == LOCAL - 1)
+    def _():
+        each_live(length_ref, span, finish)
+
 
 def outputs_kernel(
     length_ref,
     key_ref,
     value_ref,
     prompt_ref,
-    probability_ref,
-    score_grad_ref,
+    probability_hbm,
+    score_grad_hbm,
     out_ref,
     query_grad_ref,
     token_ref,
     keys_t,
     values_t,
+    probability_ref,
+    score_grad_ref,
+    sems,
 ):
+    kept = (probability_hbm, score_grad_hbm)
+    held = (probability_ref, score_grad_ref)
     response = pl.program_id(0)
     length = length_ref[response]
     span = out_ref.shape[0]
     scale = HD**-0.5
+
+    def fetch(*chunk):
+        for copy in kept_copies(kept, held, sems, *chunk, False):
+            copy.start()
+
+    @pl.when(response == 0)
+    def _():
+        each_live(length_ref, span, fetch)
+
     for head in range(KV_LANE):
         lanes = slice(head * HD, (head + 1) * HD)
         for whole_t, own_ref, which in ((keys_t, key_ref, 0), (values_t, value_ref, 1)):
@@ -318,6 +368,9 @@
             count = LP + first + ROWS
             chunk = first // ROWS
             rows = slice(first, first + ROWS)
+            for head in range(KV_LANE):
+                for copy in kept_copies(kept, held, sems, response, head, first, False):
+                    copy.wait()
             for head in range(KV_LANE):
                 output = jnp.dot(
                     values_t[head, :, :count],
@@ -351,7 +404,8 @@
         prompt=pl.BlockSpec(
             (2, KV_LANE, GROUPS, 1, SLICE, HD), lambda i, length: (0, 0, 0, i, 0, 0)
         ),
-        kept=pl.BlockSpec(memory_space=pltpu.VMEM),
+        held=pl.BlockSpec(memory_space=pltpu.VMEM),
+        kept=pl.BlockSpec(memory_space=pl.ANY),
     )
 
 
@@ -395,15 +449,18 @@
         grid_spec=pltpu.PrefetchScalarGridSpec(
             num_scalar_prefetch=1,
             grid=(count,),
-            in_specs=[spec[name] for name in ("kept", "kept", "narrow", "narrow", "prompt")],
+            in_specs=[spec[name] for name in ("held", "held", "narrow", "narrow", "prompt")],
             out_specs=[spec[name] for name in ("narrow", "narrow", "prompt", "kept", "kept")],
             scratch_shapes=[
                 pltpu.VMEM((KV_LANE, both, HD), jnp.bfloat16),
                 pltpu.VMEM((KV_LANE, both, HD), jnp.bfloat16),
                 pltpu.VMEM((streams, both, stacked), jnp.float32),
                 pltpu.VMEM((streams, both, stacked), jnp.float32),
+                pltpu.VMEM(kept.shape, jnp.bfloat16),
+                pltpu.VMEM(kept.shape, jnp.bfloat16),
                 pltpu.VMEM((KV_LANE, both, HD), jnp.float32),
                 pltpu.VMEM((KV_LANE, both, HD), jnp.float32),
+                pltpu.SemaphoreType.DMA((LOCAL, KV_LANE, CHUNKS, 2)),
             ],
         ),
         compiler_params=LARGE,
@@ -437,9 +494,12 @@
             scratch_shapes=[
                 pltpu.VMEM((KV_LANE, HD, both), jnp.bfloat16),
                 pltpu.VMEM((KV_LANE, HD, both), jnp.bfloat16),
+                pltpu.VMEM(probability.shape, jnp.bfloat16),
+                pltpu.VMEM(score_grad.shape, jnp.bfloat16),
+                pltpu.SemaphoreType.DMA((LOCAL, KV_LANE, CHUNKS, 2)),
             ],
         ),
-        compiler_params=LARGE,
+        compiler_params=OUTPUTS,
         cost_estimate=pl.CostEstimate(
             flops=8 * rows * wide * both,
             bytes_accessed=4 * rows * wide + 4 * probability.size,

time: 125 us -> 122 us (0.976)
  Pallas kernels: 23.4 us -> 34.8 us
  starting transfers between devices: 18.2 us -> 11.1 us
  local copies, waits for them, and re-layouts: 16.9 us -> 11 us
  waiting for transfers between devices: 13.5 us -> 11 us
  blocking collectives: 52 us -> 53.6 us
    pallas_call x1, Pallas kernels: 7.11 us -> 15.6 us  [attend(): pl.pallas_call(attend_kernel, out_shape=(jax.ShapeDtypeStruct(resp_keys.s...]
    pallas_call x1, Pallas kernels: 5.23 us -> 13.1 us  [outputs(): pl.pallas_call(outputs_kernel, out_shape=(shape, shape, jax.ShapeDtypeStr...]
    all_to_all x2, starting transfers between devices: 18.2 us -> 11.1 us  [over_pick(): lax.all_to_all(array, 'resp', split_axis=0, concat_axis=0, tiled=True, ax...]
    unnamed x18 -> x22, local copies, waits for them, and re-layouts: 16.9 us -> 11 us
    pallas_call x1, Pallas kernels: 5.94 us -> 0.95 us  [stack(): pl.pallas_call(stack_kernel, out_shape=(shape, shape), grid=(count,), in_...]
    all_to_all x2, waiting for transfers between devices: 13.5 us -> 11 us  [over_pick(): lax.all_to_all(array, 'resp', split_axis=0, concat_axis=0, tiled=True, ax...]
    all_to_all x2, blocking collectives: 52 us -> 53.6 us  [over_store(): lax.all_to_all(array, ('resp', 'tp'), split_axis=0, concat_axis=0, tiled=...]
  transfers between devices with their start and end apart: 2 -> 2, of which waited for: 2 -> 2; matrix products, arithmetic and copies ran while one was open for 0% -> 0% of each run, Pallas kernels for 9% -> 12%
where the time goes in v5:
time: 122 us
  blocking collectives  53.6 us (44%)
  Pallas kernels  34.8 us (29%)
  starting transfers between devices  11.1 us (9%)
  local copies, waits for them, and re-layouts  11 us (9%)
  waiting for transfers between devices  11 us (9%)
    all_to_all x2, blocking collectives, over_store(): lax.all_to_all(array, ('resp', 'tp'), split_axis=0, concat_axis=0, tiled=...  53.6 us
    pallas_call x1, Pallas kernels, attend(): pl.pallas_call(attend_kernel, out_shape=(jax.ShapeDtypeStruct(resp_keys.s...  15.6 us
    pallas_call x1, Pallas kernels, outputs(): pl.pallas_call(outputs_kernel, out_shape=(shape, shape, jax.ShapeDtypeStr...  13.1 us
    all_to_all x2, starting transfers between devices, over_pick(): lax.all_to_all(array, 'resp', split_axis=0, concat_axis=0, tiled=True, ax...  11.1 us
    unnamed x22, local copies, waits for them, and re-layouts  11 us
    all_to_all x2, waiting for transfers between devices, over_pick(): lax.all_to_all(array, 'resp', split_axis=0, concat_axis=0, tiled=True, ax...  11 us
    pallas_call x4, Pallas kernels, whole(): pl.pallas_call(kernel, out_shape=out_shape, in_specs=[pl.BlockSpec(memory...  5.13 us
  transfers between devices with their start and end apart: 2, of which 2 were waited for; matrix products, arithmetic and copies ran while one was open for 0% of the time, Pallas kernels for 12%

profile of v5, /device:TPU:1, one launch (start us, length us, event | category | flops | bytes accessed | tf_op | source)
XLA Modules:
  0.0 122.1 jit_solution(7787315666894984171)
XLA Ops:
  0.6 1.6 %shard_map.127 = bf16[64,24,128]{2,1,0:T(8,128)(2,1)} custom-call(s32[4]{0:T(128)} %owner_hbm.1, bf16[16,1024]{1,0:T(8,128)(2,1)} %key_hbm.1, bf16[16,1024]{1,0:T(8,128)(2,1)} %value_hbm.1), custom_call_target="tpu_custom_call" | custom-call | tf_op jit(solution)/shard_map/pallas_call | solution.py:512
  2.2 30.8 %all_to_all.20.pieces_ref = bf16[64,24,128]{2,1,0:T(8,128)(2,1)S(1)} all-to-all(bf16[64,24,128]{2,1,0:T(8,128)(2,1)} %shard_map.127), channel_id=1, replica_groups={{0,5,10,15,16,21,26,31,32,37,42,47,48,53,58,63,64,69,74,79,80,85,90,95,..., dimensions={0} | all-to-all | bytes 786432 | tf_op jit(solution)/shard_map/all_to_all | solution.py:41
  33.0 1.7 %shard_map.128 = (bf16[16,4,64,128]{3,2,1,0:T(8,128)(2,1)}, s32[16,128]{1,0:T(8,128)S(1)}) custom-call(bf16[64,24,128]{2,1,0:T(8,128)(2,1)S(1)} %all_to_all.20.pieces_ref), custom_call_target="tpu_custom_call" | custom-call | tf_op jit(solution)/shard_map/pallas_call | solution.py:512
  34.8 6.2 %all-to-all-start.1 = ((bf16[16,4,64,128]{3,2,1,0:T(8,128)(2,1)}), bf16[16,4,64,128]{3,2,1,0:T(8,128)(2,1)S(1)}, u32[]{:S(2)}, u32[]{:S(2)}) async-start(bf16[16,4,64,128]{3,2,1,0:T(8,128)(2,1)} %get-tuple-element.20), calls=%async_computation.1 | async-start | bytes 2097152 | tf_op jit(solution)/shard_map/all_to_all | solution.py:52
  41.0 0.0 copy-start.1
  41.0 1.7 %copy-done.1 = bf16[640,2048]{1,0:T(8,128)(2,1)S(1)} copy-done((bf16[640,2048]{1,0:T(8,128)(2,1)S(1)}, bf16[640,2048]{1,0:T(8,128)(2,1)}, u32[]{:S(2)}) %copy-start.1) | copy-done | bytes 2621464
  42.7 0.0 copy-start.2
  42.7 1.7 %copy-done.2 = bf16[640,2048]{1,0:T(8,128)(2,1)S(1)} copy-done((bf16[640,2048]{1,0:T(8,128)(2,1)S(1)}, bf16[640,2048]{1,0:T(8,128)(2,1)}, u32[]{:S(2)}) %copy-start.2) | copy-done | bytes 2621464
  44.5 0.0 copy-start.3
  44.5 0.0 copy-start.4
  44.5 0.0 copy-start.6
  44.5 1.0 shard_map.129
  45.4 0.0 copy-start.7
  45.4 1.5 %copy-done.7 = bf16[4,2,5,256,128]{4,3,2,1,0:T(8,128)(2,1)} copy-done((bf16[4,2,5,256,128]{4,3,2,1,0:T(8,128)(2,1)}, bf16[4,2,5,256,128]{4,3,2,1,0:T(8,128)(2,1)S(1)}, u32[]{:S(2)}) %copy-start.7) | copy-done | bytes 2621464
  46.9 1.5 %copy-done.9 = bf16[4,2,5,256,128]{4,3,2,1,0:T(8,128)(2,1)} copy-done((bf16[4,2,5,256,128]{4,3,2,1,0:T(8,128)(2,1)}, bf16[4,2,5,256,128]{4,3,2,1,0:T(8,128)(2,1)S(1)}, u32[]{:S(2)}) %copy-start.9) | copy-done | bytes 2621464
  48.4 8.4 %all-to-all-done.1 = bf16[16,4,64,128]{3,2,1,0:T(8,128)(2,1)S(1)} async-done(((bf16[16,4,64,128]{3,2,1,0:T(8,128)(2,1)}), bf16[16,4,64,128]{3,2,1,0:T(8,128)(2,1)S(1)}, u32[]{:S(2)}, u32[]{:S(2)}) %all-to-all-start.1) | async-done | bytes 1048608 | tf_op jit(solution)/shard_map/all_to_all | solution.py:52
  56.8 0.0 copy-start
  56.8 0.0 copy-done.3
  56.8 0.0 copy-done.4
  56.8 0.0 copy-done.6
  56.8 0.0 copy-start.8
  56.8 2.1 %copy-done.8 = bf16[4,2,5,256,128]{4,3,2,1,0:T(8,128)(2,1)S(1)} copy-done((bf16[4,2,5,256,128]{4,3,2,1,0:T(8,128)(2,1)S(1)}, bf16[4,2,5,256,128]{4,3,2,1,0:T(8,128)(2,1)}, u32[]{:S(2)}) %copy-start.8) | copy-done | bytes 2621464
  58.9 1.7 %copy-done.10 = bf16[4,2,5,256,128]{4,3,2,1,0:T(8,128)(2,1)S(1)} copy-done((bf16[4,2,5,256,128]{4,3,2,1,0:T(8,128)(2,1)S(1)}, bf16[4,2,5,256,128]{4,3,2,1,0:T(8,128)(2,1)}, u32[]{:S(2)}) %copy-start.10) | copy-done | bytes 2621464
  60.6 15.6 %shard_map.130 = (bf16[640,256]{1,0:T(8,128)(2,1)}, bf16[640,256]{1,0:T(8,128)(2,1)}, bf16[2,2,4,4,64,128]{5,4,3,2,1,0:T(8,128)(2,1)}, bf16[4,2,5,416,256]{4,3,2,1,0:T(8,128)(2,1)}, bf16[4,2,5,416,256]{4,3,2,1,0:T(8,128)(2,1)}) custom-call(s32[4]{0:T(128)S(1)} %copy-done.6, bf16[4,2,5,256,128]{4,3,2,1,0:T(8,128)(2,1)S(1)} %copy-done.8, ...), custom_call_target="tpu_custom_call" | custom-call | flops 8724152320 | bytes 5242880 | tf_op jit(solution)/shard_map/pallas_call | solution.py:440
  76.2 0.0 copy-done
  76.3 4.8 %all-to-all-start.2 = ((bf16[16,4,64,128]{3,2,1,0:T(8,128)(2,1)}), bf16[16,4,64,128]{3,2,1,0:T(8,128)(2,1)S(1)}, u32[]{:S(2)}, u32[]{:S(2)}) async-start(bf16[16,4,64,128]{3,2,1,0:T(8,128)(2,1)} %bitcast.1), calls=%async_computation.2 | async-start | bytes 2097152 | tf_op jit(solution)/shard_map/all_to_all | solution.py:52
  81.1 13.1 %shard_map.131 = (bf16[640,2048]{1,0:T(8,128)(2,1)}, bf16[640,2048]{1,0:T(8,128)(2,1)}, s32[8,128]{1,0:T(8,128)}) custom-call(s32[4]{0:T(128)} %length_ref.3, bf16[640,256]{1,0:T(8,128)(2,1)} %key_ref.3, bf16[640,256]{1,0:T(8,128)(2,1)} %value_ref.3, bf16[2,2,4,4,64,128]{5,4,3,2,1,0:T(8,128)(2,1)} %bitcast.3, ...), custom_call_target="tpu_custom_call" | custom-call | flops 4362076160 | bytes 22282240 | tf_op jit(solution)/shard_map/pallas_call | solution.py:482
  94.2 2.6 %all-to-all-done.2.terms_ref = bf16[16,4,64,128]{3,2,1,0:T(8,128)(2,1)S(1)} async-done(((bf16[16,4,64,128]{3,2,1,0:T(8,128)(2,1)}), bf16[16,4,64,128]{3,2,1,0:T(8,128)(2,1)S(1)}, u32[]{:S(2)}, u32[]{:S(2)}) %all-to-all-start.2) | async-done | bytes 1048608 | tf_op jit(solution)/shard_map/all_to_all | solution.py:52
  96.8 0.7 copy-done.5
  97.5 1.1 shard_map.132
  98.6 22.8 %all_to_all.21.sums_ref = bf16[64,16,128]{2,1,0:T(8,128)(2,1)S(1)} all-to-all(bf16[64,16,128]{2,1,0:T(8,128)(2,1)S(1)} %shard_map.132), channel_id=1, replica_groups={{0,5,10,15,16,21,26,31,32,37,42,47,48,53,58,63,64,69,74,79,80,85,90,95,..., dimensions={0} | all-to-all | bytes 524288 | tf_op jit(solution)/shard_map/all_to_all | solution.py:41
  121.5 0.7 shard_map.133
  (3 shorter events, 0.0 us)
Async XLA Ops:
  34.8 22.0 %all-to-all-start.1 = ((bf16[16,4,64,128]{3,2,1,0:T(8,128)(2,1)}), bf16[16,4,64,128]{3,2,1,0:T(8,128)(2,1)S(1)}, u32[]{:S(2)}, u32[]{:S(2)}) async-start(bf16[16,4,64,128]{3,2,1,0:T(8,128)(2,1)} %get-tuple-element.20), calls=%async_computation.1 | async-start | bytes 2097152 | tf_op jit(solution)/shard_map/all_to_all | solution.py:52
  41.0 1.7 %copy-start.1 = (bf16[640,2048]{1,0:T(8,128)(2,1)S(1)}, bf16[640,2048]{1,0:T(8,128)(2,1)}, u32[]{:S(2)}) copy-start(bf16[640,2048]{1,0:T(8,128)(2,1)} %query_ref.1) | copy-start | bytes 7864324
  42.7 1.7 %copy-start.2 = (bf16[640,2048]{1,0:T(8,128)(2,1)S(1)}, bf16[640,2048]{1,0:T(8,128)(2,1)}, u32[]{:S(2)}) copy-start(bf16[640,2048]{1,0:T(8,128)(2,1)} %grad_ref.1) | copy-start | bytes 7864324
  44.5 12.3 %copy-start.3 = (bf16[640,256]{1,0:T(8,128)(2,1)S(1)}, bf16[640,256]{1,0:T(8,128)(2,1)}, u32[]{:S(2)}) copy-start(bf16[640,256]{1,0:T(8,128)(2,1)} %key_ref.3) | copy-start | bytes 983044
  44.5 12.3 %copy-start.4 = (bf16[640,256]{1,0:T(8,128)(2,1)S(1)}, bf16[640,256]{1,0:T(8,128)(2,1)}, u32[]{:S(2)}) copy-start(bf16[640,256]{1,0:T(8,128)(2,1)} %value_ref.3) | copy-start | bytes 983044
  44.5 12.3 %copy-start.6 = (s32[4]{0:T(128)S(1)}, s32[4]{0:T(128)}, u32[]{:S(2)}) copy-start(s32[4]{0:T(128)} %length_ref.3) | copy-start | bytes 52
  45.4 1.5 %copy-start.7 = (bf16[4,2,5,256,128]{4,3,2,1,0:T(8,128)(2,1)}, bf16[4,2,5,256,128]{4,3,2,1,0:T(8,128)(2,1)S(1)}, u32[]{:S(2)}) copy-start(bf16[4,2,5,256,128]{4,3,2,1,0:T(8,128)(2,1)S(1)} %get-tuple-element.21.stacked_query) | copy-start | bytes 7864324
  46.9 1.5 %copy-start.9 = (bf16[4,2,5,256,128]{4,3,2,1,0:T(8,128)(2,1)}, bf16[4,2,5,256,128]{4,3,2,1,0:T(8,128)(2,1)S(1)}, u32[]{:S(2)}) copy-start(bf16[4,2,5,256,128]{4,3,2,1,0:T(8,128)(2,1)S(1)} %get-tuple-element.22.stacked_grad) | copy-start | bytes 7864324
  56.8 19.5 %copy-start = (bf16[16,4,64,128]{3,2,1,0:T(8,128)(2,1)}, bf16[16,4,64,128]{3,2,1,0:T(8,128)(2,1)S(1)}, u32[]{:S(2)}) copy-start(bf16[16,4,64,128]{3,2,1,0:T(8,128)(2,1)S(1)} %all-to-all-done.1) | copy-start | bytes 3145732
  56.8 2.1 %copy-start.8 = (bf16[4,2,5,256,128]{4,3,2,1,0:T(8,128)(2,1)S(1)}, bf16[4,2,5,256,128]{4,3,2,1,0:T(8,128)(2,1)}, u32[]{:S(2)}) copy-start(bf16[4,2,5,256,128]{4,3,2,1,0:T(8,128)(2,1)} %copy-done.7) | copy-start | bytes 7864324
  58.9 1.7 %copy-start.10 = (bf16[4,2,5,256,128]{4,3,2,1,0:T(8,128)(2,1)S(1)}, bf16[4,2,5,256,128]{4,3,2,1,0:T(8,128)(2,1)}, u32[]{:S(2)}) copy-start(bf16[4,2,5,256,128]{4,3,2,1,0:T(8,128)(2,1)} %copy-done.9) | copy-start | bytes 7864324
  76.3 20.5 %all-to-all-start.2 = ((bf16[16,4,64,128]{3,2,1,0:T(8,128)(2,1)}), bf16[16,4,64,128]{3,2,1,0:T(8,128)(2,1)S(1)}, u32[]{:S(2)}, u32[]{:S(2)}) async-start(bf16[16,4,64,128]{3,2,1,0:T(8,128)(2,1)} %bitcast.1), calls=%async_computation.2 | async-start | bytes 2097152 | tf_op jit(solution)/shard_map/all_to_all | solution.py:52
  96.8 0.7 copy-start.5

commit v6 on v2

--- a/solution.py
+++ b/solution.py
@@ -1,3 +1,5 @@
+import functools
+
 import jax
 import jax.numpy as jnp
 from jax import lax
@@ -18,9 +20,11 @@
 LOCAL = 4
 SLICE = LP // GROUPS
 CHUNKS = 5
+HALF = LOCAL // 2
 SENT = TILE + 8
 LOG2E = 1.4426950408889634
 LARGE = pltpu.CompilerParams(vmem_limit_bytes=48 * 1024 * 1024)
+FIRST = pltpu.CompilerParams(vmem_limit_bytes=(64 * 1024 - 64) * 1024)
 SMALL = pltpu.CompilerParams(vmem_limit_bytes=16 * 1024 * 1024)
 
 STORE_GROUPS = [
@@ -117,7 +121,7 @@
             ].astype(out_ref.dtype)
 
 
-def summed_kernel(sums_ref, key_ref, value_ref):
+def summed_kernel(sums_ref, token_ref, key_ref, value_ref):
     for x in range(4):
         which, head = column_of(x)
         target = value_ref if which else key_ref
@@ -158,6 +162,26 @@
             blank(first, last)
 
 
+def kept_copies(kept, held, sems, response, slot, head, first, out):
+    chunk = first // ROWS
+    rows = pl.ds(0, LP + first + ROWS)
+    for at in range(2):
+        far = kept.at[response, at, head, chunk, rows]
+        near = held[at].at[slot, head, chunk, rows]
+        source, target = (near, far) if out else (far, near)
+        yield pltpu.make_async_copy(source, target, sems.at[slot, head, chunk, at])
+
+
+def each_live(length_ref, start, count, span, act):
+    for slot in range(count):
+        for first in range(0, span, ROWS):
+
+            @pl.when(length_ref[start + slot] > first)
+            def _():
+                for head in range(KV_LANE):
+                    act(start + slot, slot, head, first)
+
+
 def attend_kernel(
     length_ref,
     query_ref,
@@ -168,19 +192,23 @@
     key_grad_ref,
     value_grad_ref,
     prompt_grad_ref,
-    probability_ref,
-    score_grad_ref,
+    kept,
     keys,
     values,
     stacked_query,
     stacked_grad,
     scores,
     prob_grads,
+    probability_ref,
+    score_grad_ref,
     key_total,
     value_total,
+    sems,
 ):
-    length = length_ref[pl.program_id(0)]
-    span = query_ref.shape[0]
+    held = (probability_ref, score_grad_ref)
+    response = pl.program_id(0)
+    length = length_ref[response]
+    span = key_ref.shape[0]
     scale = HD**-0.5
     wide = PER_GROUP * ROWS
     for head in range(KV_LANE):
@@ -221,21 +249,19 @@
         live = first + lane < length
         blocks = [slice(at, at + ROWS) for at in range(0, count, ROWS)]
         total = jnp.zeros((8, wide), jnp.float32)
+        moved = jnp.zeros((8, wide), jnp.float32)
         for block in blocks:
             weights = jnp.exp2(scores[slot, block] * (scale * LOG2E) - largest)
             scores[slot, block] = weights
             total = total + jnp.sum(weights.reshape(-1, 8, wide), axis=0)
+            terms = weights * prob_grads[slot, block]
+            moved = moved + jnp.sum(terms.reshape(-1, 8, wide), axis=0)
         inverse = jnp.where(live, 1.0 / jnp.sum(total, axis=0, keepdims=True), 0.0)
-        total = jnp.zeros((8, wide), jnp.float32)
+        delta = jnp.sum(moved, axis=0, keepdims=True) * inverse
         for block in blocks:
             probability = scores[slot, block] * inverse
-            probability_ref[0, head, chunk, block] = probability.astype(jnp.bfloat16)
-            terms = probability * prob_grads[slot, block]
-            total = total + jnp.sum(terms.reshape(-1, 8, wide), axis=0)
-        delta = jnp.sum(total, axis=0, keepdims=True)
-        for block in blocks:
-            probability = scores[slot, block] * inverse
-            score_grad_ref[0, head, chunk, block] = (
+            probability_ref[response, head, chunk, block] = probability.astype(jnp.bfloat16)
+            score_grad_ref[response, head, chunk, block] = (
                 probability * (prob_grads[slot, block] - delta)
             ).astype(jnp.bfloat16)
 
@@ -247,7 +273,7 @@
             (key_total, score_grad_ref, stacked_query),
         ):
             terms = jnp.dot(
-                left_ref[0, head, chunk, :count],
+                left_ref[response, head, chunk, :count],
                 stacked[slot],
                 preferred_element_type=jnp.float32,
             )
@@ -264,6 +290,8 @@
             if slot + 1 < len(streams):
                 largest[slot + 1] = score(slot + 1, *streams[slot + 1])
             soften(slot, *stream, largest[slot])
+            for copy in kept_copies(kept, held, sems, response, response, *stream, True):
+                copy.start()
             gather(slot, *stream)
 
     def blank(first, last):
@@ -282,23 +310,33 @@
         key_grad_ref[:, lanes] = key_terms[LP:]
         value_grad_ref[:, lanes] = value_terms[LP:]
 
-
-def outputs_kernel(
-    length_ref,
-    key_ref,
-    value_ref,
-    prompt_ref,
-    probability_ref,
-    score_grad_ref,
-    out_ref,
-    query_grad_ref,
-    token_ref,
-    keys_t,
-    values_t,
-):
-    length = length_ref[pl.program_id(0)]
+    def finish(*chunk):
+        for copy in kept_copies(kept, held, sems, *chunk, True):
+            copy.wait()
+
+    @pl.when(response == LOCAL - 1)
+    def _():
+        each_live(length_ref, 0, LOCAL, span, finish)
+
+
+def outputs_kernel(start, length_ref, key_ref, value_ref, prompt_ref, kept, *rest):
+    out_ref, query_grad_ref, token_ref, *rest = rest[-8:]
+    keys_t, values_t, probability_ref, score_grad_ref, sems = rest
+    held = (probability_ref, score_grad_ref)
+    slot = pl.program_id(0)
+    response = start + slot
+    length = length_ref[response]
     span = out_ref.shape[0]
     scale = HD**-0.5
+
+    def fetch(*chunk):
+        for copy in kept_copies(kept, held, sems, *chunk, False):
+            copy.start()
+
+    @pl.when(slot == 0)
+    def _():
+        each_live(length_ref, start, HALF, span, fetch)
+
     for head in range(KV_LANE):
         lanes = slice(head * HD, (head + 1) * HD)
         for whole_t, own_ref, which in ((keys_t, key_ref, 0), (values_t, value_ref, 1)):
@@ -312,14 +350,17 @@
             chunk = first // ROWS
             rows = slice(first, first + ROWS)
             for head in range(KV_LANE):
+                for copy in kept_copies(kept, held, sems, response, slot, head, first, False):
+                    copy.wait()
+            for head in range(KV_LANE):
                 output = jnp.dot(
                     values_t[head, :, :count],
-                    probability_ref[0, head, chunk, :count],
+                    probability_ref[slot, head, chunk, :count],
                     preferred_element_type=jnp.float32,
                 )
                 query_grad = jnp.dot(
                     keys_t[head, :, :count],
-                    score_grad_ref[0, head, chunk, :count],
+                    score_grad_ref[slot, head, chunk, :count],
                     preferred_element_type=jnp.float32,
                 )
                 output = output.astype(jnp.bfloat16).T
@@ -337,18 +378,14 @@
     token_ref[...] = jnp.zeros_like(token_ref)
 
 
-def specs(span, wide, narrow):
-    both = LP + span
-    stacked = PER_GROUP * ROWS
+def specs(span, wide, narrow, start=0):
     return dict(
-        wide=pl.BlockSpec((span, wide), lambda i, length: (i, 0)),
-        narrow=pl.BlockSpec((span, narrow), lambda i, length: (i, 0)),
+        wide=pl.BlockSpec((span, wide), lambda i, length: (start + i, 0)),
+        narrow=pl.BlockSpec((span, narrow), lambda i, length: (start + i, 0)),
         prompt=pl.BlockSpec(
-            (2, KV_LANE, GROUPS, 1, SLICE, HD), lambda i, length: (0, 0, 0, i, 0, 0)
+            (2, KV_LANE, GROUPS, 1, SLICE, HD), lambda i, length: (0, 0, 0, start + i, 0, 0)
         ),
-        kept=pl.BlockSpec(
-            (1, KV_LANE, CHUNKS, both, stacked), lambda i, length: (i, 0, 0, 0, 0)
-        ),
+        kept=pl.BlockSpec(memory_space=pl.ANY),
     )
 
 
@@ -359,21 +396,20 @@
     streams = 2 * KV_LANE
     stacked = PER_GROUP * ROWS
     spec = specs(span, queries.shape[1], resp_keys.shape[1])
-    kept = jax.ShapeDtypeStruct((count, KV_LANE, CHUNKS, both, stacked), jnp.bfloat16)
+    held = (count, KV_LANE, CHUNKS, both, stacked)
     return pl.pallas_call(
         attend_kernel,
         out_shape=(
             jax.ShapeDtypeStruct(resp_keys.shape, jnp.bfloat16),
             jax.ShapeDtypeStruct(resp_keys.shape, jnp.bfloat16),
             jax.ShapeDtypeStruct(prompt_rows.shape, jnp.bfloat16),
-            kept,
-            kept,
+            jax.ShapeDtypeStruct((count, 2, KV_LANE, CHUNKS, both, stacked), jnp.bfloat16),
         ),
         grid_spec=pltpu.PrefetchScalarGridSpec(
             num_scalar_prefetch=1,
             grid=(count,),
             in_specs=[spec[name] for name in ("wide", "wide", "narrow", "narrow", "prompt")],
-            out_specs=[spec[name] for name in ("narrow", "narrow", "prompt", "kept", "kept")],
+            out_specs=[spec[name] for name in ("narrow", "narrow", "prompt", "kept")],
             scratch_shapes=[
                 pltpu.VMEM((KV_LANE, both, HD), jnp.bfloat16),
                 pltpu.VMEM((KV_LANE, both, HD), jnp.bfloat16),
@@ -381,8 +417,11 @@
                 pltpu.VMEM((streams, stacked, HD), jnp.bfloat16),
                 pltpu.VMEM((streams, both, stacked), jnp.float32),
                 pltpu.VMEM((streams, both, stacked), jnp.float32),
+                pltpu.VMEM(held, jnp.bfloat16),
+                pltpu.VMEM(held, jnp.bfloat16),
                 pltpu.VMEM((KV_LANE, both, HD), jnp.float32),
                 pltpu.VMEM((KV_LANE, both, HD), jnp.float32),
+                pltpu.SemaphoreType.DMA((count, KV_LANE, CHUNKS, 2)),
             ],
         ),
         compiler_params=LARGE,
@@ -394,20 +433,21 @@
     )(lengths, queries, out_grad, resp_keys, resp_values, prompt_rows)
 
 
-def outputs(lengths, resp_keys, resp_values, prompt_rows, probability, score_grad, wide):
-    count = lengths.shape[0]
+def outputs(lengths, resp_keys, resp_values, prompt_rows, kept, wide, start=0, earlier=()):
     rows = resp_keys.shape[0]
-    span = rows // count
+    span = rows // lengths.shape[0]
     both = LP + span
-    spec = specs(span, wide, resp_keys.shape[1])
+    spec = specs(span, wide, resp_keys.shape[1], start)
+    held = (HALF, KV_LANE, CHUNKS, both, PER_GROUP * ROWS)
     shape = jax.ShapeDtypeStruct((rows, wide), jnp.bfloat16)
     return pl.pallas_call(
-        outputs_kernel,
+        functools.partial(outputs_kernel, start),
         out_shape=(shape, shape, jax.ShapeDtypeStruct((8, HD), jnp.int32)),
         grid_spec=pltpu.PrefetchScalarGridSpec(
             num_scalar_prefetch=1,
-            grid=(count,),
-            in_specs=[spec[name] for name in ("narrow", "narrow", "prompt", "kept", "kept")],
+            grid=(HALF,),
+            in_specs=[spec[name] for name in ("narrow", "narrow", "prompt", "kept")]
+            + [spec["kept"]] * len(earlier),
             out_specs=[
                 spec["wide"],
                 spec["wide"],
@@ -416,23 +456,27 @@
             scratch_shapes=[
                 pltpu.VMEM((KV_LANE, HD, both), jnp.bfloat16),
                 pltpu.VMEM((KV_LANE, HD, both), jnp.bfloat16),
+                pltpu.VMEM(held, jnp.bfloat16),
+                pltpu.VMEM(held, jnp.bfloat16),
+                pltpu.SemaphoreType.DMA((HALF, KV_LANE, CHUNKS, 2)),
             ],
         ),
+        input_output_aliases={5 + at: at for at in range(len(earlier[:2]))},
         compiler_params=LARGE,
         cost_estimate=pl.CostEstimate(
-            flops=8 * rows * wide * both,
-            bytes_accessed=4 * rows * wide + 4 * probability.size,
+            flops=4 * rows * wide * both,
+            bytes_accessed=2 * rows * wide + kept.size,
             transcendentals=0,
         ),
-    )(lengths, resp_keys, resp_values, prompt_rows, probability, score_grad)
-
-
-def whole(kernel, out_shape, spaces, *operands, **more):
+    )(lengths, resp_keys, resp_values, prompt_rows, kept, *earlier)
+
+
+def whole(kernel, out_shape, spaces, *operands, params=SMALL, **more):
     return pl.pallas_call(
         kernel,
         out_shape=out_shape,
         in_specs=[pl.BlockSpec(memory_space=space) for space in spaces],
-        compiler_params=SMALL,
+        compiler_params=params,
         **more,
     )(*operands)
 
@@ -452,6 +496,7 @@
             prompt_of,
             prompt_keys,
             prompt_values,
+            params=FIRST,
             scratch_shapes=[
                 pltpu.SMEM(prompt_of.shape, jnp.int32),
                 pltpu.VMEM(prompt_keys.shape, jnp.bfloat16),
@@ -468,13 +513,12 @@
         scratch_shapes=[pltpu.SMEM((MEMBERS, HD), jnp.int32), pltpu.SemaphoreType.DMA],
     )
     prompt_rows = over_pick(picked).reshape(2, KV_LANE, GROUPS, LOCAL, SLICE, HD)
-    resp_key_grad, resp_value_grad, terms, probability, score_grad = attend(
+    resp_key_grad, resp_value_grad, terms, kept = attend(
         lengths, queries, out_grad, resp_keys, resp_values, prompt_rows
     )
     terms = over_pick(terms.reshape(MEMBERS, LOCAL, SLICE, HD))
-    attn_out, query_grad, token = outputs(
-        lengths, resp_keys, resp_values, prompt_rows, probability, score_grad, queries.shape[1]
-    )
+    shared = (lengths, resp_keys, resp_values, prompt_rows, kept, queries.shape[1])
+    attn_out, query_grad, token = outputs(*shared)
     sums = whole(
         fold_kernel,
         low(PROMPTS * LANES, TILE, HD),
@@ -484,11 +528,13 @@
         token,
         scratch_shapes=[pltpu.VMEM((PROMPTS, SLICE, HD), jnp.float32)],
     )
+    attn_out, query_grad, token = outputs(*shared, HALF, (attn_out, query_grad, sums))
     prompt_key_grad, prompt_value_grad = whole(
         summed_kernel,
         (low(*prompt_keys.shape), low(*prompt_values.shape)),
-        [pltpu.VMEM],
+        [pltpu.VMEM, pl.ANY],
         over_store(sums),
+        token,
     )
     return (
         attn_out,

time: 116 us -> 117 us (level)
  blocking collectives: 71.1 us -> 52.2 us
  waiting for transfers between devices: 4.38 us -> 17.5 us
  starting transfers between devices: 4.6 us -> 12.3 us
  Pallas kernels: 31.1 us -> 32.4 us
  local copies, waits for them, and re-layouts: 2.24 us -> 1.01 us
    all_to_all x2 -> x1, blocking collectives: 50 us -> 31 us  [over_store(): lax.all_to_all(array, ('resp', 'tp'), split_axis=0, concat_axis=0, tiled=...]
    all_to_all x0 -> x1, waiting for transfers between devices: none -> 8.22 us  [over_store(): lax.all_to_all(array, ('resp', 'tp'), split_axis=0, concat_axis=0, tiled=...]
    all_to_all x0 -> x1, starting transfers between devices: none -> 5.05 us  [over_store(): lax.all_to_all(array, ('resp', 'tp'), split_axis=0, concat_axis=0, tiled=...]
    all_to_all x1, waiting for transfers between devices: 4.38 us -> 9.29 us  [over_pick(): lax.all_to_all(array, 'resp', split_axis=0, concat_axis=0, tiled=True, ax...]
    all_to_all x1, starting transfers between devices: 4.6 us -> 7.24 us  [over_pick(): lax.all_to_all(array, 'resp', split_axis=0, concat_axis=0, tiled=True, ax...]
    pallas_call x4, Pallas kernels: 3.18 us -> 4.85 us  [whole(): pl.pallas_call(kernel, out_shape=out_shape, in_specs=[pl.BlockSpec(memory...]
    pallas_call x1, Pallas kernels: 16.6 us -> 15.3 us  [attend(): pl.pallas_call(attend_kernel, out_shape=(jax.ShapeDtypeStruct(resp_keys.s...]
    unnamed x14 -> x10, local copies, waits for them, and re-layouts: 2.24 us -> 1.01 us
  transfers between devices with their start and end apart: 1 -> 2, of which waited for: 1 -> 2; matrix products, arithmetic and copies ran while one was open for 0% -> 0% of each run, Pallas kernels for 10% -> 11%
where the time goes in v6:
time: 117 us; the launch traced here: 116 us
  blocking collectives  52.2 us (45%)
  Pallas kernels  32.4 us (28%)
  waiting for transfers between devices  17.5 us (15%)
  starting transfers between devices  12.3 us (11%)
    all_to_all x1, blocking collectives, over_store(): lax.all_to_all(array, ('resp', 'tp'), split_axis=0, concat_axis=0, tiled=...  31 us
    all_to_all x1, blocking collectives, over_pick(): lax.all_to_all(array, 'resp', split_axis=0, concat_axis=0, tiled=True, ax...  21.1 us
    pallas_call x1, Pallas kernels, attend(): pl.pallas_call(attend_kernel, out_shape=(jax.ShapeDtypeStruct(resp_keys.s...  15.3 us
    pallas_call x2, Pallas kernels, outputs(): pl.pallas_call(functools.partial(outputs_kernel, start), out_shape=(shape...  12.3 us
    all_to_all x1, waiting for transfers between devices, over_pick(): lax.all_to_all(array, 'resp', split_axis=0, concat_axis=0, tiled=True, ax...  9.29 us
    all_to_all x1, waiting for transfers between devices, over_store(): lax.all_to_all(array, ('resp', 'tp'), split_axis=0, concat_axis=0, tiled=...  8.22 us
    all_to_all x1, starting transfers between devices, over_pick(): lax.all_to_all(array, 'resp', split_axis=0, concat_axis=0, tiled=True, ax...  7.24 us
    all_to_all x1, starting transfers between devices, over_store(): lax.all_to_all(array, ('resp', 'tp'), split_axis=0, concat_axis=0, tiled=...  5.05 us
  transfers between devices with their start and end apart: 2, of which 2 were waited for; matrix products, arithmetic and copies ran while one was open for 0% of the time, Pallas kernels for 11%

profile of v6, /device:TPU:1, one launch (start us, length us, event | category | flops | bytes accessed | tf_op | source)
XLA Modules:
  0.0 116.2 jit_solution(11051297833292679672)
XLA Ops:
  0.6 1.6 %shard_map.127 = bf16[64,24,128]{2,1,0:T(8,128)(2,1)} custom-call(s32[4]{0:T(128)} %owner_hbm.1, bf16[16,1024]{1,0:T(8,128)(2,1)} %key_hbm.1, bf16[16,1024]{1,0:T(8,128)(2,1)} %value_hbm.1), custom_call_target="tpu_custom_call" | custom-call | tf_op jit(solution)/shard_map/pallas_call | solution.py:475
  2.2 0.0 copy-start
  2.2 0.0 copy-start.1
  2.3 0.0 copy-start.3
  2.3 0.0 copy-start.4
  2.3 31.0 %all_to_all.20.pieces_ref = bf16[64,24,128]{2,1,0:T(8,128)(2,1)S(1)} all-to-all(bf16[64,24,128]{2,1,0:T(8,128)(2,1)} %shard_map.127), channel_id=1, replica_groups={{0,5,10,15,16,21,26,31,32,37,42,47,48,53,58,63,64,69,74,79,80,85,90,95,..., dimensions={0} | all-to-all | bytes 786432 | tf_op jit(solution)/shard_map/all_to_all | solution.py:42
  33.3 0.8 shard_map.128
  34.1 21.1 %all_to_all.21 = bf16[16,4,64,128]{3,2,1,0:T(8,128)(2,1)S(1)} all-to-all(bf16[16,4,64,128]{3,2,1,0:T(8,128)(2,1)S(1)} %get-tuple-element.20), channel_id=1, replica_groups={{0,4,8,12,32,36,40,44,64,68,72,76,96,100,104,108},{16,20,24,28,48,52,56..., dimensions={0} | all-to-all | bytes 2097152 | tf_op jit(solution)/shard_map/all_to_all | solution.py:53
  55.2 0.0 copy-done
  55.2 0.0 copy-done.1
  55.2 0.0 copy-done.3
  55.2 0.0 copy-done.4
  55.2 15.3 %shard_map.129 = (bf16[640,256]{1,0:T(8,128)(2,1)}, bf16[640,256]{1,0:T(8,128)(2,1)}, bf16[2,2,4,4,64,128]{5,4,3,2,1,0:T(8,128)(2,1)S(1)}, bf16[4,2,2,5,416,256]{5,4,3,2,1,0:T(8,128)(2,1)}) custom-call(s32[4]{0:T(128)S(1)} %copy-done.3, bf16[640,2048]{1,0:T(8,128)(2,1)S(1)} %copy-done.4, bf16[640,2048]{1,0:T(8,128)(2,1)} %grad_ref.1, ...), custom_call_target="tpu_custom_call" | custom-call | flops 8724152320 | bytes 5242880 | tf_op jit(solution)/shard_map/pallas_call | solution.py:400
  70.6 0.0 copy-start.2
  70.6 1.0 copy-done.2
  71.6 7.2 %all-to-all-start.2 = ((bf16[16,4,64,128]{3,2,1,0:T(8,128)(2,1)}), bf16[16,4,64,128]{3,2,1,0:T(8,128)(2,1)S(1)}, u32[]{:S(2)}, u32[]{:S(2)}) async-start(bf16[16,4,64,128]{3,2,1,0:T(8,128)(2,1)} %bitcast.5), calls=%async_computation.2 | async-start | bytes 2097152 | tf_op jit(solution)/shard_map/all_to_all | solution.py:53
  78.8 6.5 %shard_map.130 = (bf16[640,2048]{1,0:T(8,128)(2,1)}, bf16[640,2048]{1,0:T(8,128)(2,1)}, s32[8,128]{1,0:T(8,128)S(1)}) custom-call(s32[4]{0:T(128)S(1)} %copy-done.3, bf16[640,256]{1,0:T(8,128)(2,1)S(1)} %copy-done, bf16[640,256]{1,0:T(8,128)(2,1)S(1)} %copy-done.1, bf16[2,2,4,4,64,128]{5,4,3,2,1,0:T(8,128)(2,1)S(1)} %bitcast.3, ...), custom_call_target="tpu_custom_call" | custom-call | flops 2181038080 | bytes 11141120 | tf_op jit(solution)/shard_map/pallas_call | solution.py:443
  85.3 9.3 %all-to-all-done.2.terms_ref = bf16[16,4,64,128]{3,2,1,0:T(8,128)(2,1)S(1)} async-done(((bf16[16,4,64,128]{3,2,1,0:T(8,128)(2,1)}), bf16[16,4,64,128]{3,2,1,0:T(8,128)(2,1)S(1)}, u32[]{:S(2)}, u32[]{:S(2)}) %all-to-all-start.2) | async-done | bytes 1048608 | tf_op jit(solution)/shard_map/all_to_all | solution.py:53
  94.6 1.8 %shard_map.131.rest_2_ = bf16[64,16,128]{2,1,0:T(8,128)(2,1)} custom-call(s32[16,128]{1,0:T(8,128)S(1)} %get-tuple-element.24.owner_ref, bf16[16,4,64,128]{3,2,1,0:T(8,128)(2,1)S(1)} %all-to-all-done.2.terms_ref, s32[8,128]{1,0:T(8,128)S(1)} %get-tuple-element.26.token_ref), custom_call_target="tpu_custom_call" | custom-call | tf_op jit(solution)/shard_map/pallas_call | solution.py:475
  96.4 5.0 %all-to-all-start.3 = ((bf16[64,16,128]{2,1,0:T(8,128)(2,1)}), bf16[64,16,128]{2,1,0:T(8,128)(2,1)S(1)}, u32[]{:S(2)}, u32[]{:S(2)}) async-start(bf16[64,16,128]{2,1,0:T(8,128)(2,1)} %shard_map.131.rest_2_), calls=%async_computation.3 | async-start | bytes 524288 | tf_op jit(solution)/shard_map/all_to_all | solution.py:42
  101.5 5.8 %shard_map.132 = (bf16[640,2048]{1,0:T(8,128)(2,1)}, bf16[640,2048]{1,0:T(8,128)(2,1)}, s32[8,128]{1,0:T(8,128)S(1)}) custom-call(s32[4]{0:T(128)S(1)} %copy-done.3, bf16[640,256]{1,0:T(8,128)(2,1)S(1)} %copy-done, bf16[640,256]{1,0:T(8,128)(2,1)S(1)} %copy-done.1, ...), custom_call_target="tpu_custom_call", output_to_operand_aliasing={{0}: (5, {}), {1}: (6, {})} | custom-call | flops 2181038080 | bytes 11141120 | tf_op jit(solution)/shard_map/pallas_call | solution.py:443
  107.3 8.2 %all-to-all-done.3.sums_ref = bf16[64,16,128]{2,1,0:T(8,128)(2,1)S(1)} async-done(((bf16[64,16,128]{2,1,0:T(8,128)(2,1)}), bf16[64,16,128]{2,1,0:T(8,128)(2,1)S(1)}, u32[]{:S(2)}, u32[]{:S(2)}) %all-to-all-start.3) | async-done | bytes 262176 | tf_op jit(solution)/shard_map/all_to_all | solution.py:42
  115.5 0.7 shard_map.133
Async XLA Ops:
  2.2 53.0 %copy-start = (bf16[640,256]{1,0:T(8,128)(2,1)S(1)}, bf16[640,256]{1,0:T(8,128)(2,1)}, u32[]{:S(2)}) copy-start(bf16[640,256]{1,0:T(8,128)(2,1)} %key_ref.5) | copy-start | bytes 983044
  2.2 53.0 %copy-start.1 = (bf16[640,256]{1,0:T(8,128)(2,1)S(1)}, bf16[640,256]{1,0:T(8,128)(2,1)}, u32[]{:S(2)}) copy-start(bf16[640,256]{1,0:T(8,128)(2,1)} %value_ref.5) | copy-start | bytes 983044
  2.3 53.0 %copy-start.3 = (s32[4]{0:T(128)S(1)}, s32[4]{0:T(128)}, u32[]{:S(2)}) copy-start(s32[4]{0:T(128)} %length_ref.5) | copy-start | bytes 52
  2.3 53.0 %copy-start.4 = (bf16[640,2048]{1,0:T(8,128)(2,1)S(1)}, bf16[640,2048]{1,0:T(8,128)(2,1)}, u32[]{:S(2)}) copy-start(bf16[640,2048]{1,0:T(8,128)(2,1)} %query_ref.1) | copy-start | bytes 7864324
  70.6 1.0 copy-start.2
  71.6 23.0 %all-to-all-start.2 = ((bf16[16,4,64,128]{3,2,1,0:T(8,128)(2,1)}), bf16[16,4,64,128]{3,2,1,0:T(8,128)(2,1)S(1)}, u32[]{:S(2)}, u32[]{:S(2)}) async-start(bf16[16,4,64,128]{3,2,1,0:T(8,128)(2,1)} %bitcast.5), calls=%async_computation.2 | async-start | bytes 2097152 | tf_op jit(solution)/shard_map/all_to_all | solution.py:53
  96.4 19.1 %all-to-all-start.3 = ((bf16[64,16,128]{2,1,0:T(8,128)(2,1)}), bf16[64,16,128]{2,1,0:T(8,128)(2,1)S(1)}, u32[]{:S(2)}, u32[]{:S(2)}) async-start(bf16[64,16,128]{2,1,0:T(8,128)(2,1)} %shard_map.131.rest_2_), calls=%async_computation.3 | async-start | bytes 524288 | tf_op jit(solution)/shard_map/all_to_all | solution.py:42

commit v7 on v6

--- a/solution.py
+++ b/solution.py
@@ -135,6 +135,11 @@
             target[:, first : first + HD] = tile.astype(target.dtype)
 
 
+def stacked(ref, head, first):
+    parts = [ref[first : first + ROWS, column] for _, column in heads(head)]
+    return jnp.concatenate(parts, 0)
+
+
 def heads(head):
     for at in range(PER_GROUP):
         column = (head * PER_GROUP + at) * HD
@@ -189,14 +194,10 @@
     key_ref,
     value_ref,
     prompt_ref,
-    key_grad_ref,
-    value_grad_ref,
     prompt_grad_ref,
     kept,
     keys,
     values,
-    stacked_query,
-    stacked_grad,
     scores,
     prob_grads,
     probability_ref,
@@ -220,12 +221,9 @@
         count = LP + first + ROWS
         lane = lax.broadcasted_iota(jnp.int32, (1, wide), 1) % ROWS
         causal = lax.broadcasted_iota(jnp.int32, (ROWS, 1), 0) <= lane
-        for part, column in heads(head):
-            stacked_query[slot, part] = query_ref[first : first + ROWS, column]
-            stacked_grad[slot, part] = grad_ref[first : first + ROWS, column]
         raw = lax.dot_general(
             keys[head, :count],
-            stacked_query[slot],
+            stacked(query_ref, head, first),
             (((1,), (1,)), ((), ())),
             preferred_element_type=jnp.float32,
         )
@@ -236,7 +234,7 @@
         top = jnp.maximum(top, jnp.max(tail.reshape(-1, 8, wide), axis=0))
         prob_grads[slot, :count] = lax.dot_general(
             values[head, :count],
-            stacked_grad[slot],
+            stacked(grad_ref, head, first),
             (((1,), (1,)), ((), ())),
             preferred_element_type=jnp.float32,
         )
@@ -265,23 +263,20 @@
                 probability * (prob_grads[slot, block] - delta)
             ).astype(jnp.bfloat16)
 
-    def gather(slot, head, first):
-        count = LP + first + ROWS
-        chunk = first // ROWS
-        for total, left_ref, stacked in (
-            (value_total, probability_ref, stacked_grad),
-            (key_total, score_grad_ref, stacked_query),
+    def gather(head, first):
+        for total, left_ref, right_ref in (
+            (value_total, probability_ref, grad_ref),
+            (key_total, score_grad_ref, query_ref),
         ):
             terms = jnp.dot(
-                left_ref[response, head, chunk, :count],
-                stacked[slot],
+                left_ref[response, head, first // ROWS, :LP],
+                stacked(right_ref, head, first),
                 preferred_element_type=jnp.float32,
             )
             if first == 0:
-                total[head, :count] = terms
+                total[head] = terms
             else:
-                total[head, : count - ROWS] += terms[: count - ROWS]
-                total[head, count - ROWS : count] = terms[count - ROWS :]
+                total[head] += terms
 
     def work(firsts):
         streams = [(head, first) for first in firsts for head in range(KV_LANE)]
@@ -292,23 +287,15 @@
             soften(slot, *stream, largest[slot])
             for copy in kept_copies(kept, held, sems, response, response, *stream, True):
                 copy.start()
-            gather(slot, *stream)
-
-    def blank(first, last):
-        zeros = jnp.zeros((KV_LANE, last - first, HD), jnp.float32)
-        key_total[:, LP + first : LP + last] = zeros
-        value_total[:, LP + first : LP + last] = zeros
-
-    by_length(length, span, work, blank)
+            gather(*stream)
+
+    by_length(length, span, work, lambda first, last: None)
 
     for head in range(KV_LANE):
-        lanes = slice(head * HD, (head + 1) * HD)
         key_terms = (key_total[head] * scale).astype(jnp.bfloat16)
         value_terms = value_total[head].astype(jnp.bfloat16)
-        prompt_grad_ref[0, head, :, 0] = key_terms[:LP].reshape(GROUPS, SLICE, HD)
-        prompt_grad_ref[1, head, :, 0] = value_terms[:LP].reshape(GROUPS, SLICE, HD)
-        key_grad_ref[:, lanes] = key_terms[LP:]
-        value_grad_ref[:, lanes] = value_terms[LP:]
+        prompt_grad_ref[0, head, :, 0] = key_terms.reshape(GROUPS, SLICE, HD)
+        prompt_grad_ref[1, head, :, 0] = value_terms.reshape(GROUPS, SLICE, HD)
 
     def finish(*chunk):
         for copy in kept_copies(kept, held, sems, *chunk, True):
@@ -319,9 +306,11 @@
         each_live(length_ref, 0, LOCAL, span, finish)
 
 
-def outputs_kernel(start, length_ref, key_ref, value_ref, prompt_ref, kept, *rest):
-    out_ref, query_grad_ref, token_ref, *rest = rest[-8:]
-    keys_t, values_t, probability_ref, score_grad_ref, sems = rest
+def outputs_kernel(
+    start, length_ref, query_ref, grad_ref, key_ref, value_ref, prompt_ref, kept, *rest
+):
+    out_ref, query_grad_ref, key_grad_ref, value_grad_ref, token_ref, *rest = rest[-12:]
+    keys_t, values_t, probability_ref, score_grad_ref, key_total, value_total, sems = rest
     held = (probability_ref, score_grad_ref)
     slot = pl.program_id(0)
     response = start + slot
@@ -368,13 +357,32 @@
                 for part, column in heads(head):
                     out_ref[rows, column] = output[part]
                     query_grad_ref[rows, column] = query_grad[part]
+                for total, left_ref, right_ref in (
+                    (value_total, probability_ref, grad_ref),
+                    (key_total, score_grad_ref, query_ref),
+                ):
+                    terms = jnp.dot(
+                        left_ref[slot, head, chunk, LP:count],
+                        stacked(right_ref, head, first),
+                        preferred_element_type=jnp.float32,
+                    )
+                    if first > 0:
+                        total[head, :first] += terms[:first]
+                    total[head, rows] = terms[first:]
 
     def blank(first, last):
         zeros = jnp.zeros((last - first, out_ref.shape[1]), jnp.bfloat16)
         out_ref[first:last, :] = zeros
         query_grad_ref[first:last, :] = zeros
+        zeros = jnp.zeros((KV_LANE, last - first, HD), jnp.float32)
+        key_total[:, first:last] = zeros
+        value_total[:, first:last] = zeros
 
     by_length(length, span, work, blank)
+    for head in range(KV_LANE):
+        lanes = slice(head * HD, (head + 1) * HD)
+        key_grad_ref[:, lanes] = (key_total[head] * scale).astype(jnp.bfloat16)
+        value_grad_ref[:, lanes] = value_total[head].astype(jnp.bfloat16)
     token_ref[...] = jnp.zeros_like(token_ref)
 
 
@@ -394,33 +402,29 @@
     span = queries.shape[0] // count
     both = LP + span
     streams = 2 * KV_LANE
-    stacked = PER_GROUP * ROWS
+    wide = PER_GROUP * ROWS
     spec = specs(span, queries.shape[1], resp_keys.shape[1])
-    held = (count, KV_LANE, CHUNKS, both, stacked)
+    held = (count, KV_LANE, CHUNKS, both, wide)
     return pl.pallas_call(
         attend_kernel,
         out_shape=(
-            jax.ShapeDtypeStruct(resp_keys.shape, jnp.bfloat16),
-            jax.ShapeDtypeStruct(resp_keys.shape, jnp.bfloat16),
             jax.ShapeDtypeStruct(prompt_rows.shape, jnp.bfloat16),
-            jax.ShapeDtypeStruct((count, 2, KV_LANE, CHUNKS, both, stacked), jnp.bfloat16),
+            jax.ShapeDtypeStruct((count, 2, KV_LANE, CHUNKS, both, wide), jnp.bfloat16),
         ),
         grid_spec=pltpu.PrefetchScalarGridSpec(
             num_scalar_prefetch=1,
             grid=(count,),
             in_specs=[spec[name] for name in ("wide", "wide", "narrow", "narrow", "prompt")],
-            out_specs=[spec[name] for name in ("narrow", "narrow", "prompt", "kept")],
+            out_specs=[spec[name] for name in ("prompt", "kept")],
             scratch_shapes=[
                 pltpu.VMEM((KV_LANE, both, HD), jnp.bfloat16),
                 pltpu.VMEM((KV_LANE, both, HD), jnp.bfloat16),
-                pltpu.VMEM((streams, stacked, HD), jnp.bfloat16),
-                pltpu.VMEM((streams, stacked, HD), jnp.bfloat16),
-                pltpu.VMEM((streams, both, stacked), jnp.float32),
-                pltpu.VMEM((streams, both, stacked), jnp.float32),
+                pltpu.VMEM((streams, both, wide), jnp.float32),
+                pltpu.VMEM((streams, both, wide), jnp.float32),
                 pltpu.VMEM(held, jnp.bfloat16),
                 pltpu.VMEM(held, jnp.bfloat16),
-                pltpu.VMEM((KV_LANE, both, HD), jnp.float32),
-                pltpu.VMEM((KV_LANE, both, HD), jnp.float32),
+                pltpu.VMEM((KV_LANE, LP, HD), jnp.float32),
+                pltpu.VMEM((KV_LANE, LP, HD), jnp.float32),
                 pltpu.SemaphoreType.DMA((count, KV_LANE, CHUNKS, 2)),
             ],
         ),
@@ -433,24 +437,29 @@
     )(lengths, queries, out_grad, resp_keys, resp_values, prompt_rows)
 
 
-def outputs(lengths, resp_keys, resp_values, prompt_rows, kept, wide, start=0, earlier=()):
-    rows = resp_keys.shape[0]
+def outputs(
+    lengths, queries, out_grad, resp_keys, resp_values, prompt_rows, kept, start=0, earlier=()
+):
+    rows, wide = queries.shape
     span = rows // lengths.shape[0]
     both = LP + span
     spec = specs(span, wide, resp_keys.shape[1], start)
     held = (HALF, KV_LANE, CHUNKS, both, PER_GROUP * ROWS)
-    shape = jax.ShapeDtypeStruct((rows, wide), jnp.bfloat16)
+    shape = jax.ShapeDtypeStruct(queries.shape, jnp.bfloat16)
+    own = jax.ShapeDtypeStruct(resp_keys.shape, jnp.bfloat16)
     return pl.pallas_call(
         functools.partial(outputs_kernel, start),
-        out_shape=(shape, shape, jax.ShapeDtypeStruct((8, HD), jnp.int32)),
+        out_shape=(shape, shape, own, own, jax.ShapeDtypeStruct((8, HD), jnp.int32)),
         grid_spec=pltpu.PrefetchScalarGridSpec(
             num_scalar_prefetch=1,
             grid=(HALF,),
-            in_specs=[spec[name] for name in ("narrow", "narrow", "prompt", "kept")]
+            in_specs=[spec[name] for name in ("wide", "wide", "narrow", "narrow", "prompt", "kept")]
             + [spec["kept"]] * len(earlier),
             out_specs=[
                 spec["wide"],
                 spec["wide"],
+                spec["narrow"],
+                spec["narrow"],
                 pl.BlockSpec((8, HD), lambda i, length: (0, 0)),
             ],
             scratch_shapes=[
@@ -458,17 +467,19 @@
                 pltpu.VMEM((KV_LANE, HD, both), jnp.bfloat16),
                 pltpu.VMEM(held, jnp.bfloat16),
                 pltpu.VMEM(held, jnp.bfloat16),
+                pltpu.VMEM((KV_LANE, span, HD), jnp.float32),
+                pltpu.VMEM((KV_LANE, span, HD), jnp.float32),
                 pltpu.SemaphoreType.DMA((HALF, KV_LANE, CHUNKS, 2)),
             ],
         ),
-        input_output_aliases={5 + at: at for at in range(len(earlier[:2]))},
+        input_output_aliases={7 + at: at for at in range(len(earlier[:4]))},
         compiler_params=LARGE,
         cost_estimate=pl.CostEstimate(
             flops=4 * rows * wide * both,
             bytes_accessed=2 * rows * wide + kept.size,
             transcendentals=0,
         ),
-    )(lengths, resp_keys, resp_values, prompt_rows, kept, *earlier)
+    )(lengths, queries, out_grad, resp_keys, resp_values, prompt_rows, kept, *earlier)
 
 
 def whole(kernel, out_shape, spaces, *operands, params=SMALL, **more):
@@ -513,12 +524,10 @@
         scratch_shapes=[pltpu.SMEM((MEMBERS, HD), jnp.int32), pltpu.SemaphoreType.DMA],
     )
     prompt_rows = over_pick(picked).reshape(2, KV_LANE, GROUPS, LOCAL, SLICE, HD)
-    resp_key_grad, resp_value_grad, terms, kept = attend(
-        lengths, queries, out_grad, resp_keys, resp_values, prompt_rows
-    )
+    shared = (lengths, queries, out_grad, resp_keys, resp_values, prompt_rows)
+    terms, kept = attend(*shared)
     terms = over_pick(terms.reshape(MEMBERS, LOCAL, SLICE, HD))
-    shared = (lengths, resp_keys, resp_values, prompt_rows, kept, queries.shape[1])
-    attn_out, query_grad, token = outputs(*shared)
+    *results, token = outputs(*shared, kept)
     sums = whole(
         fold_kernel,
         low(PROMPTS * LANES, TILE, HD),
@@ -528,7 +537,7 @@
         token,
         scratch_shapes=[pltpu.VMEM((PROMPTS, SLICE, HD), jnp.float32)],
     )
-    attn_out, query_grad, token = outputs(*shared, HALF, (attn_out, query_grad, sums))
+    *results, token = outputs(*shared, kept, HALF, (*results, sums))
     prompt_key_grad, prompt_value_grad = whole(
         summed_kernel,
         (low(*prompt_keys.shape), low(*prompt_values.shape)),
@@ -536,14 +545,7 @@
         over_store(sums),
         token,
     )
-    return (
-        attn_out,
-        query_grad,
-        resp_key_grad,
-        resp_value_grad,
-        prompt_key_grad,
-        prompt_value_grad,
-    )
+    return (*results, prompt_key_grad, prompt_value_grad)
 
 
 def solution(mesh):

time: 117 us -> 117 us (level)
  waiting for transfers between devices: 17.5 us -> 13.8 us
  starting transfers between devices: 12.3 us -> 15.8 us
  local copies, waits for them, and re-layouts: 1.01 us -> 3.46 us
  Pallas kernels: 32.4 us -> 30.9 us
    pallas_call x1, Pallas kernels: 15.3 us -> 11.8 us  [attend(): pl.pallas_call(attend_kernel, out_shape=(jax.ShapeDtypeStruct(prompt_rows...]
    unnamed x10 -> x16, local copies, waits for them, and re-layouts: 1.01 us -> 3.46 us
    all_to_all x1, waiting for transfers between devices: 8.22 us -> 6.32 us  [over_store(): lax.all_to_all(array, ('resp', 'tp'), split_axis=0, concat_axis=0, tiled=...]
    all_to_all x1, waiting for transfers between devices: 9.29 us -> 7.49 us  [over_pick(): lax.all_to_all(array, 'resp', split_axis=0, concat_axis=0, tiled=True, ax...]
    all_to_all x1, starting transfers between devices: 7.24 us -> 9.03 us  [over_pick(): lax.all_to_all(array, 'resp', split_axis=0, concat_axis=0, tiled=True, ax...]
    all_to_all x1, starting transfers between devices: 5.05 us -> 6.78 us  [over_store(): lax.all_to_all(array, ('resp', 'tp'), split_axis=0, concat_axis=0, tiled=...]
    pallas_call x2, Pallas kernels: 12.3 us -> 13.8 us  [outputs(): pl.pallas_call(functools.partial(outputs_kernel, start), out_shape=(shape...]
  transfers between devices with their start and end apart: 2 -> 2, of which waited for: 2 -> 2; matrix products, arithmetic and copies ran while one was open for 0% -> 0% of each run, Pallas kernels for 11% -> 12%
where the time goes in v7:
time: 117 us
  blocking collectives  52.2 us (45%)
  Pallas kernels  30.9 us (26%)
  starting transfers between devices  15.8 us (14%)
  waiting for transfers between devices  13.8 us (12%)
  local copies, waits for them, and re-layouts  3.46 us (3%)
    all_to_all x1, blocking collectives, over_store(): lax.all_to_all(array, ('resp', 'tp'), split_axis=0, concat_axis=0, tiled=...  31 us
    all_to_all x1, blocking collectives, over_pick(): lax.all_to_all(array, 'resp', split_axis=0, concat_axis=0, tiled=True, ax...  21.1 us
    pallas_call x2, Pallas kernels, outputs(): pl.pallas_call(functools.partial(outputs_kernel, start), out_shape=(shape...  13.8 us
    pallas_call x1, Pallas kernels, attend(): pl.pallas_call(attend_kernel, out_shape=(jax.ShapeDtypeStruct(prompt_rows...  11.8 us
    all_to_all x1, starting transfers between devices, over_pick(): lax.all_to_all(array, 'resp', split_axis=0, concat_axis=0, tiled=True, ax...  9.03 us
    all_to_all x1, waiting for transfers between devices, over_pick(): lax.all_to_all(array, 'resp', split_axis=0, concat_axis=0, tiled=True, ax...  7.49 us
    all_to_all x1, starting transfers between devices, over_store(): lax.all_to_all(array, ('resp', 'tp'), split_axis=0, concat_axis=0, tiled=...  6.78 us
    all_to_all x1, waiting for transfers between devices, over_store(): lax.all_to_all(array, ('resp', 'tp'), split_axis=0, concat_axis=0, tiled=...  6.32 us
  transfers between devices with their start and end apart: 2, of which 2 were waited for; matrix products, arithmetic and copies ran while one was open for 0% of the time, Pallas kernels for 12%

profile of v7, /device:TPU:1, one launch (start us, length us, event | category | flops | bytes accessed | tf_op | source)
XLA Modules:
  0.0 116.9 jit_solution(1594036502413740664)
XLA Ops:
  0.6 1.6 %shard_map.127 = bf16[64,24,128]{2,1,0:T(8,128)(2,1)} custom-call(s32[4]{0:T(128)} %owner_hbm.1, bf16[16,1024]{1,0:T(8,128)(2,1)} %key_hbm.1, bf16[16,1024]{1,0:T(8,128)(2,1)} %value_hbm.1), custom_call_target="tpu_custom_call" | custom-call | tf_op jit(solution)/shard_map/pallas_call | solution.py:486
  2.2 0.0 copy-start
  2.2 0.0 copy-start.4
  2.3 0.0 copy-start.5
  2.3 0.0 copy-start.7
  2.3 31.0 %all_to_all.20.pieces_ref = bf16[64,24,128]{2,1,0:T(8,128)(2,1)S(1)} all-to-all(bf16[64,24,128]{2,1,0:T(8,128)(2,1)} %shard_map.127), channel_id=1, replica_groups={{0,5,10,15,16,21,26,31,32,37,42,47,48,53,58,63,64,69,74,79,80,85,90,95,..., dimensions={0} | all-to-all | bytes 786432 | tf_op jit(solution)/shard_map/all_to_all | solution.py:42
  33.3 0.8 shard_map.128
  34.1 21.1 %all_to_all.21 = bf16[16,4,64,128]{3,2,1,0:T(8,128)(2,1)S(1)} all-to-all(bf16[16,4,64,128]{3,2,1,0:T(8,128)(2,1)S(1)} %get-tuple-element.22), channel_id=1, replica_groups={{0,4,8,12,32,36,40,44,64,68,72,76,96,100,104,108},{16,20,24,28,48,52,56..., dimensions={0} | all-to-all | bytes 2097152 | tf_op jit(solution)/shard_map/all_to_all | solution.py:53
  55.2 0.0 copy-start.1
  55.2 0.0 copy-done
  55.2 0.0 copy-done.4
  55.2 0.0 copy-done.5
  55.2 0.0 copy-done.7
  55.2 11.8 %shard_map.129 = (bf16[2,2,4,4,64,128]{5,4,3,2,1,0:T(8,128)(2,1)S(1)}, bf16[4,2,2,5,416,256]{5,4,3,2,1,0:T(8,128)(2,1)}) custom-call(s32[4]{0:T(128)S(1)} %copy-done.7, bf16[640,2048]{1,0:T(8,128)(2,1)S(1)} %copy-done, bf16[640,2048]{1,0:T(8,128)(2,1)} %grad_ref.5, bf16[640,256]{1,0:T(8,128)(2,1)S(1)} %copy-done.4, bf16[640,256]{1,0:T(8,128)(2,1)S(1)} %copy-done.5, ...), custom_call_target="tpu_custom_call" | custom-call | flops 8724152320 | bytes 5242880 | tf_op jit(solution)/shard_map/pallas_call | solution.py:408
  67.1 0.0 copy-done.1
  67.1 0.0 copy-start.6
  67.1 1.0 copy-done.6
  68.1 9.0 %all-to-all-start.2 = ((bf16[16,4,64,128]{3,2,1,0:T(8,128)(2,1)}), bf16[16,4,64,128]{3,2,1,0:T(8,128)(2,1)}, u32[]{:S(2)}, u32[]{:S(2)}) async-start(bf16[16,4,64,128]{3,2,1,0:T(8,128)(2,1)} %bitcast.5), calls=%async_computation.2 | async-start | bytes 2097152 | tf_op jit(solution)/shard_map/all_to_all | solution.py:53
  77.1 0.0 copy-start.2
  77.1 1.2 %copy-done.2 = bf16[16,4,64,128]{3,2,1,0:T(8,128)(2,1)S(1)} copy-done((bf16[16,4,64,128]{3,2,1,0:T(8,128)(2,1)S(1)}, bf16[16,4,64,128]{3,2,1,0:T(8,128)(2,1)}, u32[]{:S(2)}) %copy-start.2) | copy-done | bytes 1048600
  78.3 7.1 %shard_map.130 = (bf16[640,2048]{1,0:T(8,128)(2,1)}, bf16[640,2048]{1,0:T(8,128)(2,1)}, bf16[640,256]{1,0:T(8,128)(2,1)}, bf16[640,256]{1,0:T(8,128)(2,1)}, s32[8,128]{1,0:T(8,128)S(1)}) custom-call(s32[4]{0:T(128)S(1)} %copy-done.7, bf16[640,2048]{1,0:T(8,128)(2,1)S(1)} %copy-done, bf16[640,2048]{1,0:T(8,128)(2,1)} %grad_ref.5, ...), custom_call_target="tpu_custom_call" | custom-call | flops 2181038080 | bytes 11141120 | tf_op jit(solution)/shard_map/pallas_call | solution.py:450
  85.4 7.5 %all-to-all-done.2.terms_ref = bf16[16,4,64,128]{3,2,1,0:T(8,128)(2,1)} async-done(((bf16[16,4,64,128]{3,2,1,0:T(8,128)(2,1)}), bf16[16,4,64,128]{3,2,1,0:T(8,128)(2,1)}, u32[]{:S(2)}, u32[]{:S(2)}) %all-to-all-start.2) | async-done | bytes 1048608 | tf_op jit(solution)/shard_map/all_to_all | solution.py:53
  92.9 2.3 %shard_map.131.rest_4_ = bf16[64,16,128]{2,1,0:T(8,128)(2,1)} custom-call(s32[16,128]{1,0:T(8,128)S(1)} %get-tuple-element.28.owner_ref, bf16[16,4,64,128]{3,2,1,0:T(8,128)(2,1)} %all-to-all-done.2.terms_ref, s32[8,128]{1,0:T(8,128)S(1)} %get-tuple-element.30.token_ref), custom_call_target="tpu_custom_call" | custom-call | tf_op jit(solution)/shard_map/pallas_call | solution.py:486
  95.2 6.8 %all-to-all-start.3 = ((bf16[64,16,128]{2,1,0:T(8,128)(2,1)}), bf16[64,16,128]{2,1,0:T(8,128)(2,1)S(1)}, u32[]{:S(2)}, u32[]{:S(2)}) async-start(bf16[64,16,128]{2,1,0:T(8,128)(2,1)} %shard_map.131.rest_4_), calls=%async_computation.3 | async-start | bytes 524288 | tf_op jit(solution)/shard_map/all_to_all | solution.py:42
  102.0 0.0 copy-start.3
  102.0 1.2 %copy-done.3 = bf16[16,4,64,128]{3,2,1,0:T(8,128)(2,1)S(1)} copy-done((bf16[16,4,64,128]{3,2,1,0:T(8,128)(2,1)S(1)}, bf16[16,4,64,128]{3,2,1,0:T(8,128)(2,1)}, u32[]{:S(2)}) %copy-start.3) | copy-done | bytes 1048600
  103.2 6.7 %shard_map.132 = (bf16[640,2048]{1,0:T(8,128)(2,1)}, bf16[640,2048]{1,0:T(8,128)(2,1)}, bf16[640,256]{1,0:T(8,128)(2,1)}, bf16[640,256]{1,0:T(8,128)(2,1)}, s32[8,128]{1,0:T(8,128)S(1)}) custom-call(s32[4]{0:T(128)S(1)} %copy-done.7, bf16[640,2048]{1,0:T(8,128)(2,1)S(1)} %copy-done, ...), custom_call_target="tpu_custom_call", output_to_operand_aliasing={{0}: (7, {}), {1}: (8, {}), {2}: (9, {}), {3}: (10, {})} | custom-call | flops 2181038080 | bytes 11141120 | tf_op jit(solution)/shard_map/pallas_call | solution.py:450
  109.9 6.3 %all-to-all-done.3.sums_ref = bf16[64,16,128]{2,1,0:T(8,128)(2,1)S(1)} async-done(((bf16[64,16,128]{2,1,0:T(8,128)(2,1)}), bf16[64,16,128]{2,1,0:T(8,128)(2,1)S(1)}, u32[]{:S(2)}, u32[]{:S(2)}) %all-to-all-start.3) | async-done | bytes 262176 | tf_op jit(solution)/shard_map/all_to_all | solution.py:42
  116.2 0.7 shard_map.133
Async XLA Ops:
  2.2 53.0 %copy-start = (bf16[640,2048]{1,0:T(8,128)(2,1)S(1)}, bf16[640,2048]{1,0:T(8,128)(2,1)}, u32[]{:S(2)}) copy-start(bf16[640,2048]{1,0:T(8,128)(2,1)} %query_ref.5) | copy-start | bytes 7864324
  2.2 53.0 %copy-start.4 = (bf16[640,256]{1,0:T(8,128)(2,1)S(1)}, bf16[640,256]{1,0:T(8,128)(2,1)}, u32[]{:S(2)}) copy-start(bf16[640,256]{1,0:T(8,128)(2,1)} %key_ref.5) | copy-start | bytes 983044
  2.3 53.0 %copy-start.5 = (bf16[640,256]{1,0:T(8,128)(2,1)S(1)}, bf16[640,256]{1,0:T(8,128)(2,1)}, u32[]{:S(2)}) copy-start(bf16[640,256]{1,0:T(8,128)(2,1)} %value_ref.5) | copy-start | bytes 983044
  2.3 53.0 %copy-start.7 = (s32[4]{0:T(128)S(1)}, s32[4]{0:T(128)}, u32[]{:S(2)}) copy-start(s32[4]{0:T(128)} %length_ref.5) | copy-start | bytes 52
  55.2 11.8 %copy-start.1 = (bf16[16,4,64,128]{3,2,1,0:T(8,128)(2,1)}, bf16[16,4,64,128]{3,2,1,0:T(8,128)(2,1)S(1)}, u32[]{:S(2)}) copy-start(bf16[16,4,64,128]{3,2,1,0:T(8,128)(2,1)S(1)} %all_to_all.21) | copy-start | bytes 3145732
  67.1 1.0 copy-start.6
  68.1 24.8 %all-to-all-start.2 = ((bf16[16,4,64,128]{3,2,1,0:T(8,128)(2,1)}), bf16[16,4,64,128]{3,2,1,0:T(8,128)(2,1)}, u32[]{:S(2)}, u32[]{:S(2)}) async-start(bf16[16,4,64,128]{3,2,1,0:T(8,128)(2,1)} %bitcast.5), calls=%async_computation.2 | async-start | bytes 2097152 | tf_op jit(solution)/shard_map/all_to_all | solution.py:53
  77.1 1.2 %copy-start.2 = (bf16[16,4,64,128]{3,2,1,0:T(8,128)(2,1)S(1)}, bf16[16,4,64,128]{3,2,1,0:T(8,128)(2,1)}, u32[]{:S(2)}) copy-start(bf16[16,4,64,128]{3,2,1,0:T(8,128)(2,1)} %copy-done.1) | copy-start | bytes 3145732
  95.2 21.0 %all-to-all-start.3 = ((bf16[64,16,128]{2,1,0:T(8,128)(2,1)}), bf16[64,16,128]{2,1,0:T(8,128)(2,1)S(1)}, u32[]{:S(2)}, u32[]{:S(2)}) async-start(bf16[64,16,128]{2,1,0:T(8,128)(2,1)} %shard_map.131.rest_4_), calls=%async_computation.3 | async-start | bytes 524288 | tf_op jit(solution)/shard_map/all_to_all | solution.py:42
  102.0 1.2 %copy-start.3 = (bf16[16,4,64,128]{3,2,1,0:T(8,128)(2,1)S(1)}, bf16[16,4,64,128]{3,2,1,0:T(8,128)(2,1)}, u32[]{:S(2)}) copy-start(bf16[16,4,64,128]{3,2,1,0:T(8,128)(2,1)} %copy-done.1) | copy-start | bytes 3145732

commit v8 on v7

--- a/solution.py
+++ b/solution.py
@@ -25,6 +25,8 @@
 LOG2E = 1.4426950408889634
 LARGE = pltpu.CompilerParams(vmem_limit_bytes=48 * 1024 * 1024)
 FIRST = pltpu.CompilerParams(vmem_limit_bytes=(64 * 1024 - 64) * 1024)
+STACK = pltpu.CompilerParams(vmem_limit_bytes=55 * 1024 * 1024)
+ATTEND = pltpu.CompilerParams(vmem_limit_bytes=62 * 1024 * 1024)
 SMALL = pltpu.CompilerParams(vmem_limit_bytes=16 * 1024 * 1024)
 
 STORE_GROUPS = [
@@ -87,7 +89,7 @@
             )
 
 
-def pick_kernel(pieces_ref, out_ref, owner_ref, owners, sem):
+def pick_kernel(pieces_ref, token_ref, out_ref, owner_ref, owners, sem):
     resp = lax.axis_index("resp")
     prompt = resp // 4
     turn = (resp % 4 + LANES - lax.axis_index("tp")) % 4
@@ -136,14 +138,23 @@
 
 
 def stacked(ref, head, first):
-    parts = [ref[first : first + ROWS, column] for _, column in heads(head)]
-    return jnp.concatenate(parts, 0)
+    return ref[0, head, first // ROWS]
 
 
 def heads(head):
     for at in range(PER_GROUP):
         column = (head * PER_GROUP + at) * HD
         yield slice(at * ROWS, (at + 1) * ROWS), slice(column, column + HD)
+
+
+def stack_kernel(query_ref, grad_ref, stacked_query, stacked_grad, token_ref):
+    for chunk in range(CHUNKS):
+        rows = slice(chunk * ROWS, (chunk + 1) * ROWS)
+        for head in range(KV_LANE):
+            for part, column in heads(head):
+                stacked_query[0, head, chunk, part] = query_ref[rows, column]
+                stacked_grad[0, head, chunk, part] = grad_ref[rows, column]
+    token_ref[...] = jnp.zeros_like(token_ref)
 
 
 def by_length(length, span, work, blank):
@@ -389,6 +400,9 @@
 def specs(span, wide, narrow, start=0):
     return dict(
         wide=pl.BlockSpec((span, wide), lambda i, length: (start + i, 0)),
+        rows=pl.BlockSpec(
+            (1, KV_LANE, CHUNKS, PER_GROUP * ROWS, HD), lambda i, length: (start + i, 0, 0, 0, 0)
+        ),
         narrow=pl.BlockSpec((span, narrow), lambda i, length: (start + i, 0)),
         prompt=pl.BlockSpec(
             (2, KV_LANE, GROUPS, 1, SLICE, HD), lambda i, length: (0, 0, 0, start + i, 0, 0)
@@ -397,13 +411,32 @@
     )
 
 
+def stack(queries, out_grad, count):
+    span = queries.shape[0] // count
+    block = (1, KV_LANE, CHUNKS, PER_GROUP * ROWS, HD)
+    shape = jax.ShapeDtypeStruct((count,) + block[1:], jnp.bfloat16)
+    wide = pl.BlockSpec((span, queries.shape[1]), lambda i: (i, 0))
+    rows = pl.BlockSpec(block, lambda i: (i, 0, 0, 0, 0))
+    return pl.pallas_call(
+        stack_kernel,
+        out_shape=(shape, shape, jax.ShapeDtypeStruct((8, HD), jnp.int32)),
+        grid=(count,),
+        in_specs=[wide, wide],
+        out_specs=[rows, rows, pl.BlockSpec((8, HD), lambda i: (0, 0))],
+        compiler_params=STACK,
+        cost_estimate=pl.CostEstimate(
+            flops=0, bytes_accessed=8 * queries.size, transcendentals=0
+        ),
+    )(queries, out_grad)
+
+
 def attend(lengths, queries, out_grad, resp_keys, resp_values, prompt_rows):
     count = lengths.shape[0]
-    span = queries.shape[0] // count
+    span = resp_keys.shape[0] // count
     both = LP + span
     streams = 2 * KV_LANE
     wide = PER_GROUP * ROWS
-    spec = specs(span, queries.shape[1], resp_keys.shape[1])
+    spec = specs(span, queries.size // resp_keys.shape[0], resp_keys.shape[1])
     held = (count, KV_LANE, CHUNKS, both, wide)
     return pl.pallas_call(
         attend_kernel,
@@ -414,7 +447,7 @@
         grid_spec=pltpu.PrefetchScalarGridSpec(
             num_scalar_prefetch=1,
             grid=(count,),
-            in_specs=[spec[name] for name in ("wide", "wide", "narrow", "narrow", "prompt")],
+            in_specs=[spec[name] for name in ("rows", "rows", "narrow", "narrow", "prompt")],
             out_specs=[spec[name] for name in ("prompt", "kept")],
             scratch_shapes=[
                 pltpu.VMEM((KV_LANE, both, HD), jnp.bfloat16),
@@ -428,7 +461,7 @@
                 pltpu.SemaphoreType.DMA((count, KV_LANE, CHUNKS, 2)),
             ],
         ),
-        compiler_params=LARGE,
+        compiler_params=ATTEND,
         cost_estimate=pl.CostEstimate(
             flops=16 * queries.size * both,
             bytes_accessed=4 * queries.size,
@@ -440,12 +473,13 @@
 def outputs(
     lengths, queries, out_grad, resp_keys, resp_values, prompt_rows, kept, start=0, earlier=()
 ):
-    rows, wide = queries.shape
+    rows = resp_keys.shape[0]
+    wide = queries.size // rows
     span = rows // lengths.shape[0]
     both = LP + span
     spec = specs(span, wide, resp_keys.shape[1], start)
     held = (HALF, KV_LANE, CHUNKS, both, PER_GROUP * ROWS)
-    shape = jax.ShapeDtypeStruct(queries.shape, jnp.bfloat16)
+    shape = jax.ShapeDtypeStruct((rows, wide), jnp.bfloat16)
     own = jax.ShapeDtypeStruct(resp_keys.shape, jnp.bfloat16)
     return pl.pallas_call(
         functools.partial(outputs_kernel, start),
@@ -453,7 +487,7 @@
         grid_spec=pltpu.PrefetchScalarGridSpec(
             num_scalar_prefetch=1,
             grid=(HALF,),
-            in_specs=[spec[name] for name in ("wide", "wide", "narrow", "narrow", "prompt", "kept")]
+            in_specs=[spec[name] for name in ("rows", "rows", "narrow", "narrow", "prompt", "kept")]
             + [spec["kept"]] * len(earlier),
             out_specs=[
                 spec["wide"],
@@ -516,15 +550,17 @@
             ],
         )
     )
+    *rows, token = stack(queries, out_grad, lengths.shape[0])
     picked, owners = whole(
         pick_kernel,
         (low(MEMBERS, LOCAL, SLICE, HD), jax.ShapeDtypeStruct((MEMBERS, HD), jnp.int32)),
-        [pltpu.VMEM],
+        [pltpu.VMEM, pl.ANY],
         pieces,
+        token,
         scratch_shapes=[pltpu.SMEM((MEMBERS, HD), jnp.int32), pltpu.SemaphoreType.DMA],
     )
     prompt_rows = over_pick(picked).reshape(2, KV_LANE, GROUPS, LOCAL, SLICE, HD)
-    shared = (lengths, queries, out_grad, resp_keys, resp_values, prompt_rows)
+    shared = (lengths, *rows, resp_keys, resp_values, prompt_rows)
     terms, kept = attend(*shared)
     terms = over_pick(terms.reshape(MEMBERS, LOCAL, SLICE, HD))
     *results, token = outputs(*shared, kept)

time: 117 us -> 118 us (level)
  blocking collectives: 52.2 us -> 21.2 us
  starting transfers between devices: 15.8 us -> 28.7 us
  Pallas kernels: 30.9 us -> 42.6 us
  waiting for transfers between devices: 13.8 us -> 20.3 us
  local copies, waits for them, and re-layouts: 3.46 us -> 4.88 us
    all_to_all x1 -> x0, blocking collectives: 31 us -> none  [over_store(): lax.all_to_all(array, ('resp', 'tp'), split_axis=0, concat_axis=0, tiled=...]
    all_to_all x1 -> x2, starting transfers between devices: 6.78 us -> 22.5 us  [over_store(): lax.all_to_all(array, ('resp', 'tp'), split_axis=0, concat_axis=0, tiled=...]
    all_to_all x1 -> x2, waiting for transfers between devices: 6.32 us -> 16 us  [over_store(): lax.all_to_all(array, ('resp', 'tp'), split_axis=0, concat_axis=0, tiled=...]
    pallas_call x0 -> x1, Pallas kernels: none -> 5.64 us  [stack(): pl.pallas_call(stack_kernel, out_shape=(shape, shape, jax.ShapeDtypeStruc...]
    pallas_call x1, Pallas kernels: 11.8 us -> 15.9 us  [attend(): pl.pallas_call(attend_kernel, out_shape=(jax.ShapeDtypeStruct(prompt_rows...]
    all_to_all x1, waiting for transfers between devices: 7.49 us -> 4.32 us  [over_pick(): lax.all_to_all(array, 'resp', split_axis=0, concat_axis=0, tiled=True, ax...]
    all_to_all x1, starting transfers between devices: 9.03 us -> 6.24 us  [over_pick(): lax.all_to_all(array, 'resp', split_axis=0, concat_axis=0, tiled=True, ax...]
    pallas_call x2, Pallas kernels: 13.8 us -> 15.7 us  [outputs(): pl.pallas_call(functools.partial(outputs_kernel, start), out_shape=(shape...]
  transfers between devices with their start and end apart: 2 -> 3, of which waited for: 2 -> 3; matrix products, arithmetic and copies ran while one was open for 0% -> 0% of each run, Pallas kernels for 12% -> 18%
where the time goes in v8:
time: 118 us
  Pallas kernels  42.6 us (36%)
  starting transfers between devices  28.7 us (24%)
  blocking collectives  21.2 us (18%)
  waiting for transfers between devices  20.3 us (17%)
  local copies, waits for them, and re-layouts  4.88 us (4%)
    all_to_all x2, starting transfers between devices, over_store(): lax.all_to_all(array, ('resp', 'tp'), split_axis=0, concat_axis=0, tiled=...  22.5 us
    all_to_all x1, blocking collectives, over_pick(): lax.all_to_all(array, 'resp', split_axis=0, concat_axis=0, tiled=True, ax...  21.2 us
    all_to_all x2, waiting for transfers between devices, over_store(): lax.all_to_all(array, ('resp', 'tp'), split_axis=0, concat_axis=0, tiled=...  16 us
    pallas_call x1, Pallas kernels, attend(): pl.pallas_call(attend_kernel, out_shape=(jax.ShapeDtypeStruct(prompt_rows...  15.9 us
    pallas_call x2, Pallas kernels, outputs(): pl.pallas_call(functools.partial(outputs_kernel, start), out_shape=(shape...  15.7 us
    all_to_all x1, starting transfers between devices, over_pick(): lax.all_to_all(array, 'resp', split_axis=0, concat_axis=0, tiled=True, ax...  6.24 us
    pallas_call x1, Pallas kernels, stack(): pl.pallas_call(stack_kernel, out_shape=(shape, shape, jax.ShapeDtypeStruc...  5.64 us
    pallas_call x4, Pallas kernels, whole(): pl.pallas_call(kernel, out_shape=out_shape, in_specs=[pl.BlockSpec(memory...  5.28 us
  transfers between devices with their start and end apart: 3, of which 3 were waited for; matrix products, arithmetic and copies ran while one was open for 0% of the time, Pallas kernels for 18%

profile of v8, /device:TPU:1, one launch (start us, length us, event | category | flops | bytes accessed | tf_op | source)
XLA Modules:
  0.0 118.4 jit_solution(11484814062268395474)
XLA Ops:
  0.6 1.6 %shard_map.128 = bf16[64,24,128]{2,1,0:T(8,128)(2,1)} custom-call(s32[4]{0:T(128)} %owner_hbm.1, bf16[16,1024]{1,0:T(8,128)(2,1)} %key_hbm.1, bf16[16,1024]{1,0:T(8,128)(2,1)} %value_hbm.1), custom_call_target="tpu_custom_call" | custom-call | tf_op jit(solution)/shard_map/pallas_call | solution.py:520
  2.2 15.1 %all-to-all-start = ((bf16[64,24,128]{2,1,0:T(8,128)(2,1)}), bf16[64,24,128]{2,1,0:T(8,128)(2,1)S(1)}, u32[]{:S(2)}, u32[]{:S(2)}) async-start(bf16[64,24,128]{2,1,0:T(8,128)(2,1)} %shard_map.128), calls=%async_computation | async-start | bytes 786432 | tf_op jit(solution)/shard_map/all_to_all | solution.py:44
  17.4 5.6 %shard_map.127 = (bf16[4,2,5,256,128]{4,3,2,1,0:T(8,128)(2,1)}, bf16[4,2,5,256,128]{4,3,2,1,0:T(8,128)(2,1)}, s32[8,128]{1,0:T(8,128)}) custom-call(bf16[640,2048]{1,0:T(8,128)(2,1)} %query_ref.1, bf16[640,2048]{1,0:T(8,128)(2,1)} %grad_ref.1), custom_call_target="tpu_custom_call" | custom-call | bytes 10485760 | tf_op jit(solution)/shard_map/pallas_call | solution.py:420
  23.0 10.0 %all-to-all-done.pieces_ref = bf16[64,24,128]{2,1,0:T(8,128)(2,1)S(1)} async-done(((bf16[64,24,128]{2,1,0:T(8,128)(2,1)}), bf16[64,24,128]{2,1,0:T(8,128)(2,1)S(1)}, u32[]{:S(2)}, u32[]{:S(2)}) %all-to-all-start) | async-done | bytes 393248 | tf_op jit(solution)/shard_map/all_to_all | solution.py:44
  33.0 0.0 copy-start.6
  33.0 0.7 copy-done.6
  33.7 0.8 shard_map.129
  34.5 21.2 %all_to_all.20 = bf16[16,4,64,128]{3,2,1,0:T(8,128)(2,1)} all-to-all(bf16[16,4,64,128]{3,2,1,0:T(8,128)(2,1)S(1)} %get-tuple-element.28), channel_id=1, replica_groups={{0,4,8,12,32,36,40,44,64,68,72,76,96,100,104,108},{16,20,24,28,48,52,56..., dimensions={0} | all-to-all | bytes 2097152 | tf_op jit(solution)/shard_map/all_to_all | solution.py:55
  55.7 0.0 copy-start.4
  55.7 0.0 copy-start.5
  55.7 0.0 copy-start.7
  55.7 15.9 %shard_map.130 = (bf16[2,2,4,4,64,128]{5,4,3,2,1,0:T(8,128)(2,1)}, bf16[4,2,2,5,416,256]{5,4,3,2,1,0:T(8,128)(2,1)}) custom-call(s32[4]{0:T(128)} %length_ref.5, bf16[4,2,5,256,128]{4,3,2,1,0:T(8,128)(2,1)} %get-tuple-element.25.query_ref, bf16[4,2,5,256,128]{4,3,2,1,0:T(8,128)(2,1)} %get-tuple-element.26.grad_ref, bf16[640,256]{1,0:T(8,128)(2,1)} %key_ref.5, ...), custom_call_target="tpu_custom_call" | custom-call | flops 8724152320 | bytes 5242880 | tf_op jit(solution)/shard_map/pallas_call | solution.py:441
  71.6 6.2 %all-to-all-start.2 = ((bf16[16,4,64,128]{3,2,1,0:T(8,128)(2,1)}), bf16[16,4,64,128]{3,2,1,0:T(8,128)(2,1)}, u32[]{:S(2)}, u32[]{:S(2)}) async-start(bf16[16,4,64,128]{3,2,1,0:T(8,128)(2,1)} %bitcast.5), calls=%async_computation.2 | async-start | bytes 2097152 | tf_op jit(solution)/shard_map/all_to_all | solution.py:55
  77.9 0.0 copy-done.4
  77.9 0.0 copy-done.5
  77.9 0.0 copy-done.7
  77.9 0.0 copy-start
  77.9 1.7 %copy-done = bf16[4,2,5,256,128]{4,3,2,1,0:T(8,128)(2,1)S(1)} copy-done((bf16[4,2,5,256,128]{4,3,2,1,0:T(8,128)(2,1)S(1)}, bf16[4,2,5,256,128]{4,3,2,1,0:T(8,128)(2,1)}, u32[]{:S(2)}) %copy-start) | copy-done | bytes 2621464
  79.6 0.0 copy-start.2
  79.6 1.2 %copy-done.2 = bf16[16,4,64,128]{3,2,1,0:T(8,128)(2,1)S(1)} copy-done((bf16[16,4,64,128]{3,2,1,0:T(8,128)(2,1)S(1)}, bf16[16,4,64,128]{3,2,1,0:T(8,128)(2,1)}, u32[]{:S(2)}) %copy-start.2) | copy-done | bytes 1048600
  80.9 0.0 copy-start.1
  80.9 8.6 %shard_map.131 = (bf16[640,2048]{1,0:T(8,128)(2,1)}, bf16[640,2048]{1,0:T(8,128)(2,1)}, bf16[640,256]{1,0:T(8,128)(2,1)}, bf16[640,256]{1,0:T(8,128)(2,1)}, s32[8,128]{1,0:T(8,128)S(1)}) custom-call(s32[4]{0:T(128)S(1)} %copy-done.7, bf16[4,2,5,256,128]{4,3,2,1,0:T(8,128)(2,1)S(1)} %copy-done, bf16[4,2,5,256,128]{4,3,2,1,0:T(8,128)(2,1)} %get-tuple-element.26.grad_ref, ...), custom_call_target="tpu_custom_call" | custom-call | flops 2181038080 | bytes 11141120 | tf_op jit(solution)/shard_map/pallas_call | solution.py:484
  89.5 4.3 %all-to-all-done.2.terms_ref = bf16[16,4,64,128]{3,2,1,0:T(8,128)(2,1)} async-done(((bf16[16,4,64,128]{3,2,1,0:T(8,128)(2,1)}), bf16[16,4,64,128]{3,2,1,0:T(8,128)(2,1)}, u32[]{:S(2)}, u32[]{:S(2)}) %all-to-all-start.2) | async-done | bytes 1048608 | tf_op jit(solution)/shard_map/all_to_all | solution.py:55
  93.8 2.3 %shard_map.132.rest_4_ = bf16[64,16,128]{2,1,0:T(8,128)(2,1)} custom-call(s32[16,128]{1,0:T(8,128)S(1)} %get-tuple-element.34.owner_ref, bf16[16,4,64,128]{3,2,1,0:T(8,128)(2,1)} %all-to-all-done.2.terms_ref, s32[8,128]{1,0:T(8,128)S(1)} %get-tuple-element.36.token_ref), custom_call_target="tpu_custom_call" | custom-call | tf_op jit(solution)/shard_map/pallas_call | solution.py:520
  96.0 7.3 %all-to-all-start.3 = ((bf16[64,16,128]{2,1,0:T(8,128)(2,1)}), bf16[64,16,128]{2,1,0:T(8,128)(2,1)S(1)}, u32[]{:S(2)}, u32[]{:S(2)}) async-start(bf16[64,16,128]{2,1,0:T(8,128)(2,1)} %shard_map.132.rest_4_), calls=%async_computation.3 | async-start | bytes 524288 | tf_op jit(solution)/shard_map/all_to_all | solution.py:44
  103.4 0.0 copy-done.1
  103.4 0.0 copy-start.3
  103.4 1.2 %copy-done.3 = bf16[16,4,64,128]{3,2,1,0:T(8,128)(2,1)S(1)} copy-done((bf16[16,4,64,128]{3,2,1,0:T(8,128)(2,1)S(1)}, bf16[16,4,64,128]{3,2,1,0:T(8,128)(2,1)}, u32[]{:S(2)}) %copy-start.3) | copy-done | bytes 1048600
  104.6 7.1 %shard_map.133 = (bf16[640,2048]{1,0:T(8,128)(2,1)}, bf16[640,2048]{1,0:T(8,128)(2,1)}, bf16[640,256]{1,0:T(8,128)(2,1)}, bf16[640,256]{1,0:T(8,128)(2,1)}, s32[8,128]{1,0:T(8,128)S(1)}) custom-call(s32[4]{0:T(128)S(1)} %copy-done.7, ...), custom_call_target="tpu_custom_call", output_to_operand_aliasing={{0}: (7, {}), {1}: (8, {}), {2}: (9, {}), {3}: (10, {})} | custom-call | flops 2181038080 | bytes 11141120 | tf_op jit(solution)/shard_map/pallas_call | solution.py:484
  111.8 6.0 %all-to-all-done.3.sums_ref = bf16[64,16,128]{2,1,0:T(8,128)(2,1)S(1)} async-done(((bf16[64,16,128]{2,1,0:T(8,128)(2,1)}), bf16[64,16,128]{2,1,0:T(8,128)(2,1)S(1)}, u32[]{:S(2)}, u32[]{:S(2)}) %all-to-all-start.3) | async-done | bytes 262176 | tf_op jit(solution)/shard_map/all_to_all | solution.py:44
  117.8 0.7 shard_map.134
Async XLA Ops:
  2.2 30.8 %all-to-all-start = ((bf16[64,24,128]{2,1,0:T(8,128)(2,1)}), bf16[64,24,128]{2,1,0:T(8,128)(2,1)S(1)}, u32[]{:S(2)}, u32[]{:S(2)}) async-start(bf16[64,24,128]{2,1,0:T(8,128)(2,1)} %shard_map.128), calls=%async_computation | async-start | bytes 786432 | tf_op jit(solution)/shard_map/all_to_all | solution.py:44
  33.0 0.7 copy-start.6
  55.7 22.2 %copy-start.4 = (bf16[640,256]{1,0:T(8,128)(2,1)S(1)}, bf16[640,256]{1,0:T(8,128)(2,1)}, u32[]{:S(2)}) copy-start(bf16[640,256]{1,0:T(8,128)(2,1)} %key_ref.5) | copy-start | bytes 983044
  55.7 22.2 %copy-start.5 = (bf16[640,256]{1,0:T(8,128)(2,1)S(1)}, bf16[640,256]{1,0:T(8,128)(2,1)}, u32[]{:S(2)}) copy-start(bf16[640,256]{1,0:T(8,128)(2,1)} %value_ref.5) | copy-start | bytes 983044
  55.7 22.2 %copy-start.7 = (s32[4]{0:T(128)S(1)}, s32[4]{0:T(128)}, u32[]{:S(2)}) copy-start(s32[4]{0:T(128)} %length_ref.5) | copy-start | bytes 52
  71.6 22.1 %all-to-all-start.2 = ((bf16[16,4,64,128]{3,2,1,0:T(8,128)(2,1)}), bf16[16,4,64,128]{3,2,1,0:T(8,128)(2,1)}, u32[]{:S(2)}, u32[]{:S(2)}) async-start(bf16[16,4,64,128]{3,2,1,0:T(8,128)(2,1)} %bitcast.5), calls=%async_computation.2 | async-start | bytes 2097152 | tf_op jit(solution)/shard_map/all_to_all | solution.py:55
  77.9 1.7 %copy-start = (bf16[4,2,5,256,128]{4,3,2,1,0:T(8,128)(2,1)S(1)}, bf16[4,2,5,256,128]{4,3,2,1,0:T(8,128)(2,1)}, u32[]{:S(2)}) copy-start(bf16[4,2,5,256,128]{4,3,2,1,0:T(8,128)(2,1)} %get-tuple-element.25.query_ref) | copy-start | bytes 7864324
  79.6 1.2 %copy-start.2 = (bf16[16,4,64,128]{3,2,1,0:T(8,128)(2,1)S(1)}, bf16[16,4,64,128]{3,2,1,0:T(8,128)(2,1)}, u32[]{:S(2)}) copy-start(bf16[16,4,64,128]{3,2,1,0:T(8,128)(2,1)} %all_to_all.20) | copy-start | bytes 3145732
  80.9 22.5 %copy-start.1 = (bf16[4,2,5,256,128]{4,3,2,1,0:T(8,128)(2,1)S(1)}, bf16[4,2,5,256,128]{4,3,2,1,0:T(8,128)(2,1)}, u32[]{:S(2)}) copy-start(bf16[4,2,5,256,128]{4,3,2,1,0:T(8,128)(2,1)} %get-tuple-element.25.query_ref) | copy-start | bytes 7864324
  96.0 21.7 %all-to-all-start.3 = ((bf16[64,16,128]{2,1,0:T(8,128)(2,1)}), bf16[64,16,128]{2,1,0:T(8,128)(2,1)S(1)}, u32[]{:S(2)}, u32[]{:S(2)}) async-start(bf16[64,16,128]{2,1,0:T(8,128)(2,1)} %shard_map.132.rest_4_), calls=%async_computation.3 | async-start | bytes 524288 | tf_op jit(solution)/shard_map/all_to_all | solution.py:44
  103.4 1.2 %copy-start.3 = (bf16[16,4,64,128]{3,2,1,0:T(8,128)(2,1)S(1)}, bf16[16,4,64,128]{3,2,1,0:T(8,128)(2,1)}, u32[]{:S(2)}) copy-start(bf16[16,4,64,128]{3,2,1,0:T(8,128)(2,1)} %all_to_all.20) | copy-start | bytes 3145732

commit v9 on v7

--- a/solution.py
+++ b/solution.py
@@ -287,7 +287,9 @@
             soften(slot, *stream, largest[slot])
             for copy in kept_copies(kept, held, sems, response, response, *stream, True):
                 copy.start()
-            gather(*stream)
+            if slot > 0:
+                gather(*streams[slot - 1])
+        gather(*streams[-1])
 
     by_length(length, span, work, lambda first, last: None)
 

time: 117 us -> 117 us (level); the launches traced: 117 us -> 115 us
  Pallas kernels: 30.9 us -> 28.6 us
    pallas_call x1, Pallas kernels: 11.8 us -> 10.3 us  [attend(): pl.pallas_call(attend_kernel, out_shape=(jax.ShapeDtypeStruct(prompt_rows...]
  transfers between devices with their start and end apart: 2 -> 2, of which waited for: 2 -> 2; matrix products, arithmetic and copies ran while one was open for 0% -> 0% of each run, Pallas kernels for 12% -> 11%
where the time goes in v9:
time: 117 us; the launch traced here: 115 us
  blocking collectives  52.2 us (45%)
  Pallas kernels  28.6 us (24%)
  starting transfers between devices  16.7 us (14%)
  waiting for transfers between devices  13.7 us (12%)
  local copies, waits for them, and re-layouts  3.46 us (3%)
    all_to_all x1, blocking collectives, over_store(): lax.all_to_all(array, ('resp', 'tp'), split_axis=0, concat_axis=0, tiled=...  31 us
    all_to_all x1, blocking collectives, over_pick(): lax.all_to_all(array, 'resp', split_axis=0, concat_axis=0, tiled=True, ax...  21.1 us
    pallas_call x2, Pallas kernels, outputs(): pl.pallas_call(functools.partial(outputs_kernel, start), out_shape=(shape...  13 us
    pallas_call x1, Pallas kernels, attend(): pl.pallas_call(attend_kernel, out_shape=(jax.ShapeDtypeStruct(prompt_rows...  10.3 us
    all_to_all x1, starting transfers between devices, over_pick(): lax.all_to_all(array, 'resp', split_axis=0, concat_axis=0, tiled=True, ax...  10.1 us
    all_to_all x1, waiting for transfers between devices, over_pick(): lax.all_to_all(array, 'resp', split_axis=0, concat_axis=0, tiled=True, ax...  7.04 us
    all_to_all x1, waiting for transfers between devices, over_store(): lax.all_to_all(array, ('resp', 'tp'), split_axis=0, concat_axis=0, tiled=...  6.7 us
    all_to_all x1, starting transfers between devices, over_store(): lax.all_to_all(array, ('resp', 'tp'), split_axis=0, concat_axis=0, tiled=...  6.58 us
  transfers between devices with their start and end apart: 2, of which 2 were waited for; matrix products, arithmetic and copies ran while one was open for 0% of the time, Pallas kernels for 11%

profile of v9, /device:TPU:1, one launch (start us, length us, event | category | flops | bytes accessed | tf_op | source)
XLA Modules:
  0.0 115.4 jit_solution(16931825825194720169)
XLA Ops:
  0.6 1.6 %shard_map.127 = bf16[64,24,128]{2,1,0:T(8,128)(2,1)} custom-call(s32[4]{0:T(128)} %owner_hbm.1, bf16[16,1024]{1,0:T(8,128)(2,1)} %key_hbm.1, bf16[16,1024]{1,0:T(8,128)(2,1)} %value_hbm.1), custom_call_target="tpu_custom_call" | custom-call | tf_op jit(solution)/shard_map/pallas_call | solution.py:488
  2.2 0.0 copy-start
  2.2 0.0 copy-start.4
  2.3 0.0 copy-start.5
  2.3 0.0 copy-start.7
  2.3 31.0 %all_to_all.20.pieces_ref = bf16[64,24,128]{2,1,0:T(8,128)(2,1)S(1)} all-to-all(bf16[64,24,128]{2,1,0:T(8,128)(2,1)} %shard_map.127), channel_id=1, replica_groups={{0,5,10,15,16,21,26,31,32,37,42,47,48,53,58,63,64,69,74,79,80,85,90,95,..., dimensions={0} | all-to-all | bytes 786432 | tf_op jit(solution)/shard_map/all_to_all | solution.py:42
  33.3 0.8 shard_map.128
  34.1 21.1 %all_to_all.21 = bf16[16,4,64,128]{3,2,1,0:T(8,128)(2,1)S(1)} all-to-all(bf16[16,4,64,128]{3,2,1,0:T(8,128)(2,1)S(1)} %get-tuple-element.22), channel_id=1, replica_groups={{0,4,8,12,32,36,40,44,64,68,72,76,96,100,104,108},{16,20,24,28,48,52,56..., dimensions={0} | all-to-all | bytes 2097152 | tf_op jit(solution)/shard_map/all_to_all | solution.py:53
  55.2 0.0 copy-start.1
  55.2 0.0 copy-done
  55.2 0.0 copy-done.4
  55.2 0.0 copy-done.5
  55.2 0.0 copy-done.7
  55.2 10.3 %shard_map.129 = (bf16[2,2,4,4,64,128]{5,4,3,2,1,0:T(8,128)(2,1)S(1)}, bf16[4,2,2,5,416,256]{5,4,3,2,1,0:T(8,128)(2,1)}) custom-call(s32[4]{0:T(128)S(1)} %copy-done.7, bf16[640,2048]{1,0:T(8,128)(2,1)S(1)} %copy-done, bf16[640,2048]{1,0:T(8,128)(2,1)} %grad_ref.5, bf16[640,256]{1,0:T(8,128)(2,1)S(1)} %copy-done.4, bf16[640,256]{1,0:T(8,128)(2,1)S(1)} %copy-done.5, ...), custom_call_target="tpu_custom_call" | custom-call | flops 8724152320 | bytes 5242880 | tf_op jit(solution)/shard_map/pallas_call | solution.py:410
  65.5 0.0 copy-done.1
  65.5 0.0 copy-start.6
  65.5 1.0 copy-done.6
  66.5 10.1 %all-to-all-start.2 = ((bf16[16,4,64,128]{3,2,1,0:T(8,128)(2,1)}), bf16[16,4,64,128]{3,2,1,0:T(8,128)(2,1)}, u32[]{:S(2)}, u32[]{:S(2)}) async-start(bf16[16,4,64,128]{3,2,1,0:T(8,128)(2,1)} %bitcast.5), calls=%async_computation.2 | async-start | bytes 2097152 | tf_op jit(solution)/shard_map/all_to_all | solution.py:53
  76.7 0.0 copy-start.2
  76.7 1.2 %copy-done.2 = bf16[16,4,64,128]{3,2,1,0:T(8,128)(2,1)S(1)} copy-done((bf16[16,4,64,128]{3,2,1,0:T(8,128)(2,1)S(1)}, bf16[16,4,64,128]{3,2,1,0:T(8,128)(2,1)}, u32[]{:S(2)}) %copy-start.2) | copy-done | bytes 1048600
  77.9 7.5 %shard_map.130 = (bf16[640,2048]{1,0:T(8,128)(2,1)}, bf16[640,2048]{1,0:T(8,128)(2,1)}, bf16[640,256]{1,0:T(8,128)(2,1)}, bf16[640,256]{1,0:T(8,128)(2,1)}, s32[8,128]{1,0:T(8,128)S(1)}) custom-call(s32[4]{0:T(128)S(1)} %copy-done.7, bf16[640,2048]{1,0:T(8,128)(2,1)S(1)} %copy-done, bf16[640,2048]{1,0:T(8,128)(2,1)} %grad_ref.5, ...), custom_call_target="tpu_custom_call" | custom-call | flops 2181038080 | bytes 11141120 | tf_op jit(solution)/shard_map/pallas_call | solution.py:452
  85.4 7.0 %all-to-all-done.2.terms_ref = bf16[16,4,64,128]{3,2,1,0:T(8,128)(2,1)} async-done(((bf16[16,4,64,128]{3,2,1,0:T(8,128)(2,1)}), bf16[16,4,64,128]{3,2,1,0:T(8,128)(2,1)}, u32[]{:S(2)}, u32[]{:S(2)}) %all-to-all-start.2) | async-done | bytes 1048608 | tf_op jit(solution)/shard_map/all_to_all | solution.py:53
  92.5 2.3 %shard_map.131.rest_4_ = bf16[64,16,128]{2,1,0:T(8,128)(2,1)} custom-call(s32[16,128]{1,0:T(8,128)S(1)} %get-tuple-element.28.owner_ref, bf16[16,4,64,128]{3,2,1,0:T(8,128)(2,1)} %all-to-all-done.2.terms_ref, s32[8,128]{1,0:T(8,128)S(1)} %get-tuple-element.30.token_ref), custom_call_target="tpu_custom_call" | custom-call | tf_op jit(solution)/shard_map/pallas_call | solution.py:488
  94.7 6.6 %all-to-all-start.3 = ((bf16[64,16,128]{2,1,0:T(8,128)(2,1)}), bf16[64,16,128]{2,1,0:T(8,128)(2,1)S(1)}, u32[]{:S(2)}, u32[]{:S(2)}) async-start(bf16[64,16,128]{2,1,0:T(8,128)(2,1)} %shard_map.131.rest_4_), calls=%async_computation.3 | async-start | bytes 524288 | tf_op jit(solution)/shard_map/all_to_all | solution.py:42
  101.3 0.0 copy-start.3
  101.3 1.2 %copy-done.3 = bf16[16,4,64,128]{3,2,1,0:T(8,128)(2,1)S(1)} copy-done((bf16[16,4,64,128]{3,2,1,0:T(8,128)(2,1)S(1)}, bf16[16,4,64,128]{3,2,1,0:T(8,128)(2,1)}, u32[]{:S(2)}) %copy-start.3) | copy-done | bytes 1048600
  102.6 5.5 %shard_map.132 = (bf16[640,2048]{1,0:T(8,128)(2,1)}, bf16[640,2048]{1,0:T(8,128)(2,1)}, bf16[640,256]{1,0:T(8,128)(2,1)}, bf16[640,256]{1,0:T(8,128)(2,1)}, s32[8,128]{1,0:T(8,128)S(1)}) custom-call(s32[4]{0:T(128)S(1)} %copy-done.7, bf16[640,2048]{1,0:T(8,128)(2,1)S(1)} %copy-done, ...), custom_call_target="tpu_custom_call", output_to_operand_aliasing={{0}: (7, {}), {1}: (8, {}), {2}: (9, {}), {3}: (10, {})} | custom-call | flops 2181038080 | bytes 11141120 | tf_op jit(solution)/shard_map/pallas_call | solution.py:452
  108.0 6.7 %all-to-all-done.3.sums_ref = bf16[64,16,128]{2,1,0:T(8,128)(2,1)S(1)} async-done(((bf16[64,16,128]{2,1,0:T(8,128)(2,1)}), bf16[64,16,128]{2,1,0:T(8,128)(2,1)S(1)}, u32[]{:S(2)}, u32[]{:S(2)}) %all-to-all-start.3) | async-done | bytes 262176 | tf_op jit(solution)/shard_map/all_to_all | solution.py:42
  114.7 0.7 shard_map.133
Async XLA Ops:
  2.2 53.0 %copy-start = (bf16[640,2048]{1,0:T(8,128)(2,1)S(1)}, bf16[640,2048]{1,0:T(8,128)(2,1)}, u32[]{:S(2)}) copy-start(bf16[640,2048]{1,0:T(8,128)(2,1)} %query_ref.5) | copy-start | bytes 7864324
  2.2 53.0 %copy-start.4 = (bf16[640,256]{1,0:T(8,128)(2,1)S(1)}, bf16[640,256]{1,0:T(8,128)(2,1)}, u32[]{:S(2)}) copy-start(bf16[640,256]{1,0:T(8,128)(2,1)} %key_ref.5) | copy-start | bytes 983044
  2.3 53.0 %copy-start.5 = (bf16[640,256]{1,0:T(8,128)(2,1)S(1)}, bf16[640,256]{1,0:T(8,128)(2,1)}, u32[]{:S(2)}) copy-start(bf16[640,256]{1,0:T(8,128)(2,1)} %value_ref.5) | copy-start | bytes 983044
  2.3 53.0 %copy-start.7 = (s32[4]{0:T(128)S(1)}, s32[4]{0:T(128)}, u32[]{:S(2)}) copy-start(s32[4]{0:T(128)} %length_ref.5) | copy-start | bytes 52
  55.2 10.3 %copy-start.1 = (bf16[16,4,64,128]{3,2,1,0:T(8,128)(2,1)}, bf16[16,4,64,128]{3,2,1,0:T(8,128)(2,1)S(1)}, u32[]{:S(2)}) copy-start(bf16[16,4,64,128]{3,2,1,0:T(8,128)(2,1)S(1)} %all_to_all.21) | copy-start | bytes 3145732
  65.5 1.0 copy-start.6
  66.5 25.9 %all-to-all-start.2 = ((bf16[16,4,64,128]{3,2,1,0:T(8,128)(2,1)}), bf16[16,4,64,128]{3,2,1,0:T(8,128)(2,1)}, u32[]{:S(2)}, u32[]{:S(2)}) async-start(bf16[16,4,64,128]{3,2,1,0:T(8,128)(2,1)} %bitcast.5), calls=%async_computation.2 | async-start | bytes 2097152 | tf_op jit(solution)/shard_map/all_to_all | solution.py:53
  76.7 1.2 %copy-start.2 = (bf16[16,4,64,128]{3,2,1,0:T(8,128)(2,1)S(1)}, bf16[16,4,64,128]{3,2,1,0:T(8,128)(2,1)}, u32[]{:S(2)}) copy-start(bf16[16,4,64,128]{3,2,1,0:T(8,128)(2,1)} %copy-done.1) | copy-start | bytes 3145732
  94.7 20.0 %all-to-all-start.3 = ((bf16[64,16,128]{2,1,0:T(8,128)(2,1)}), bf16[64,16,128]{2,1,0:T(8,128)(2,1)S(1)}, u32[]{:S(2)}, u32[]{:S(2)}) async-start(bf16[64,16,128]{2,1,0:T(8,128)(2,1)} %shard_map.131.rest_4_), calls=%async_computation.3 | async-start | bytes 524288 | tf_op jit(solution)/shard_map/all_to_all | solution.py:42
  101.3 1.2 %copy-start.3 = (bf16[16,4,64,128]{3,2,1,0:T(8,128)(2,1)S(1)}, bf16[16,4,64,128]{3,2,1,0:T(8,128)(2,1)}, u32[]{:S(2)}) copy-start(bf16[16,4,64,128]{3,2,1,0:T(8,128)(2,1)} %copy-done.1) | copy-start | bytes 3145732
